TPU v7x, 512 devices: a whole 4x8x8 slice. The times are simulated.
512 devices in a mesh: seq: 64 (over y, z), head: 8 (over x, core).
Axes of the slice: x: 4, y: 8, z: 8, core: 2. Of those that a mesh axis runs over, the one named last changes fastest.
Arguments:
- queries: bfloat16 [32768, 2048], P('seq', 'head'), may hold values from -100 to 100
- keys: bfloat16 [32768, 2048], P('seq', 'head'), may hold values from -5 to 5
- values: bfloat16 [32768, 2048], P('seq', 'head'), may hold values from -6 to 6
- grad_out: bfloat16 [32768, 2048], P('seq', 'head'), may hold values from -6 to 6
- rand_blocks: int32 [256, 3], replicated, may hold values from 0 to 255, as said below
Outputs:
- context: bfloat16 [32768, 2048], P('seq', 'head')
- grad_q: bfloat16 [32768, 2048], P('seq', 'head')
- grad_k: bfloat16 [32768, 2048], P('seq', 'head')
- grad_v: bfloat16 [32768, 2048], P('seq', 'head')
Inputs may be any that keep to these rules, and one draw needn't show every extreme that they name: `rand_blocks`: entry r of query block i is one of the 4 blocks of seq index (i // 4) XOR (256 // 4 // 2^(r+1)).
All inputs are finite; a program needn't handle non-finite values.
Results may differ from a plain program's by a relative error of at most 0.017.
Values may be sent and summed in bfloat16 or wider, within the bound.
No kernel may reach another device: no remote copies, remote signals or barrier semaphores. Data moves between devices by JAX's collectives and lax.ppermute only.
A program may use at most 64 MiB of HBM per device.

v0:
```python
import jax
import jax.numpy as jnp
from jax import lax
from jax.sharding import PartitionSpec as P

DH = 128
BLK = 128
GLOBAL = 2
RAND = 3


def padded(block, sides, width):
    for axis, dim in sides:
        count = lax.axis_size(axis)
        forward = [(i, i + 1) for i in range(count - 1)]
        backward = [(target, source) for source, target in forward]
        low = lax.ppermute(
            lax.slice_in_dim(block, block.shape[dim] - width, None, axis=dim), axis, forward
        )
        high = lax.ppermute(lax.slice_in_dim(block, 0, width, axis=dim), axis, backward)
        block = jnp.concatenate([low, block, high], axis=dim)
    return block


def from_partner(value, axis, apart):
    mask = 2**apart
    pairs = [(source, source ^ mask) for source in range(lax.axis_size(axis))]
    return lax.ppermute(value, axis, pairs)


def spread(value, axis, source):
    kept = jnp.where(lax.axis_index(axis) == source, value, 0).astype(value.dtype)
    return lax.psum(kept, axis)


def window_rim(edges):
    return padded(edges, (("seq", 0),), BLK)


def partner_blocks(blocks, bit):
    return from_partner(blocks, "seq", bit)


def shards(queries, keys, values, grad_out, rand_blocks):
    n_seq = lax.axis_size("seq")
    myself = lax.axis_index("seq")
    tokens, width = queries.shape
    nblk = tokens // BLK
    heads_here = width // DH
    nkeys = GLOBAL + 3 + RAND
    scale = 1.0 / DH**0.5
    top_bit = n_seq.bit_length() - 1
    kv_local = jnp.concatenate([keys, values], axis=1).reshape(nblk, BLK, 2 * width)
    edges = jnp.concatenate([kv_local[0], kv_local[nblk - 1]], axis=0)
    rims = window_rim(edges)
    left_block = rims[:BLK]
    right_block = rims[3 * BLK :]
    glob = spread(kv_local[:GLOBAL], "seq", 0)
    my_rand = lax.dynamic_slice_in_dim(rand_blocks, myself * nblk, nblk, 0)
    fetched = []
    for step in range(RAND):
        bit = top_bit - 1 - step
        fetched.append(partner_blocks(kv_local, bit))
    pool = jnp.concatenate([kv_local, left_block[None], right_block[None], glob] + fetched, axis=0)
    pool_size = pool.shape[0]
    base = nblk + 2 + GLOBAL
    ids = jnp.arange(nblk, dtype=jnp.int32)
    qblock = myself * nblk + ids
    glob_idx = jnp.broadcast_to(
        nblk + 2 + jnp.arange(GLOBAL, dtype=jnp.int32)[None, :], (nblk, GLOBAL)
    )
    win_idx = jnp.stack(
        [jnp.where(ids > 0, ids - 1, nblk), ids, jnp.where(ids < nblk - 1, ids + 1, nblk + 1)],
        axis=1,
    )
    win_kb = qblock[:, None] + jnp.arange(-1, 2, dtype=jnp.int32)[None, :]
    steps_r = jnp.arange(RAND, dtype=jnp.int32)[None, :]
    rand_idx = base + steps_r * nblk + my_rand % nblk
    indices = jnp.concatenate([glob_idx, win_idx, rand_idx], axis=1)
    live = jnp.concatenate(
        [
            jnp.ones((nblk, GLOBAL), bool),
            (win_kb >= GLOBAL) & (win_kb < nblk * n_seq),
            my_rand >= GLOBAL,
        ],
        axis=1,
    )

    def tile_step(grad_pool, inputs):
        q_blk, do_blk, index_row, live_row = inputs
        chosen = jnp.take(pool, index_row, axis=0)
        k_sel = chosen[:, :, :width].reshape(nkeys * BLK, heads_here, DH)
        v_sel = chosen[:, :, width:].reshape(nkeys * BLK, heads_here, DH)
        query = q_blk.reshape(BLK, heads_here, DH)
        dout = do_blk.reshape(BLK, heads_here, DH)
        mask = jnp.repeat(live_row, BLK)
        scores = (
            jnp.einsum("thd,uhd->htu", query, k_sel, preferred_element_type=jnp.float32) * scale
        )
        scores = jnp.where(mask[None, None, :], scores, -1e30)
        top = jnp.max(scores, axis=-1, keepdims=True)
        expo = jnp.exp(scores - top)
        probs = expo / jnp.sum(expo, axis=-1, keepdims=True)
        probs_b = probs.astype(jnp.bfloat16)
        context = jnp.einsum(
            "htu,uhd->thd", probs_b, v_sel, preferred_element_type=jnp.float32
        ).astype(jnp.bfloat16)
        dprobs = jnp.einsum("thd,uhd->htu", dout, v_sel, preferred_element_type=jnp.float32)
        delta = jnp.sum(probs * dprobs, axis=-1, keepdims=True)
        dscores = (probs * (dprobs - delta) * scale).astype(jnp.bfloat16)
        grad_q = jnp.einsum(
            "htu,uhd->thd", dscores, k_sel, preferred_element_type=jnp.float32
        ).astype(jnp.bfloat16)
        key_terms = jnp.einsum("htu,thd->uhd", dscores, query, preferred_element_type=jnp.float32)
        value_terms = jnp.einsum("htu,thd->uhd", probs_b, dout, preferred_element_type=jnp.float32)
        tiles = jnp.concatenate(
            [key_terms.reshape(nkeys, BLK, width), value_terms.reshape(nkeys, BLK, width)], axis=2
        )
        grad_pool = grad_pool.at[index_row].add(tiles)
        return (grad_pool, (context.reshape(BLK, width), grad_q.reshape(BLK, width)))

    empty = jnp.zeros((pool_size, BLK, 2 * width), jnp.float32)
    inputs = (queries.reshape(nblk, BLK, width), grad_out.reshape(nblk, BLK, width), indices, live)
    grad_pool, (context, grad_q) = lax.scan(tile_step, empty, inputs)
    own = grad_pool[:nblk]
    back_edges = jnp.concatenate([grad_pool[nblk], grad_pool[nblk + 1]], axis=0).astype(
        jnp.bfloat16
    )
    returned = window_rim(back_edges).astype(jnp.float32)
    own = own.at[0].add(returned[:BLK])
    own = own.at[nblk - 1].add(returned[3 * BLK :])
    glob_terms = grad_pool[nblk + 2 : nblk + 2 + GLOBAL]
    glob_sum = lax.psum(glob_terms, "seq")
    own = own.at[:GLOBAL].add(jnp.where(myself == 0, glob_sum, 0.0))
    for step in range(RAND):
        bit = top_bit - 1 - step
        part_terms = grad_pool[base + step * nblk : base + (step + 1) * nblk]
        own = own + partner_blocks(part_terms.astype(jnp.bfloat16), bit).astype(jnp.float32)
    grads = own.astype(jnp.bfloat16)
    grad_k = grads[:, :, :width].reshape(tokens, width)
    grad_v = grads[:, :, width:].reshape(tokens, width)
    return (context.reshape(tokens, width), grad_q.reshape(tokens, width), grad_k, grad_v)


def solution(mesh):
    in_specs = (P("seq", "head"), P("seq", "head"), P("seq", "head"), P("seq", "head"), P())
    out_specs = (P("seq", "head"), P("seq", "head"), P("seq", "head"), P("seq", "head"))
    return jax.shard_map(shards, mesh=mesh, in_specs=in_specs, out_specs=out_specs, check_vma=False)
```

profile of v0, /device:TPU:6, one launch (start us, length us, event | category | flops | bytes accessed | tf_op | source)
XLA Modules:
  0.0 472.6 jit_solution(9159380737852866151)
XLA Ops:
  7.2 1.0 constant_dynamic-update-slice_fusion.3
  8.2 1.0 constant_dynamic-update-slice_fusion.2
  9.2 3.5 collective-permute-start.4
  12.7 4.5 collective-permute-start.3
  17.2 5.0 %collective-permute-start.2 = (bf16[4,128,512]{2,1,0:T(8,128)(2,1)S(1)}, bf16[4,128,512]{2,1,0:T(8,128)(2,1)S(1)}, u32[]{:S(2)}, u32[]{:S(2)}) collective-permute-start(bf16[4,128,512]{2,1,0:T(8,128)(2,1)S(1)} %bitcast.124), channel_id=1, source_target_pairs={{0,256},{8,264},{16,272},{24,280},{32,288},{40,296},{48,304},{56,3... | collective-permute-start | bytes 1572872 | tf_op jit(solution)/shard_map/ppermute | solution.py:28
  23.0 1.3 collective-permute-start.1
  24.3 4.9 %collective-permute-start = (bf16[128,512]{1,0:T(8,128)(2,1)S(1)}, bf16[128,512]{1,0:T(8,128)(2,1)S(1)}, u32[]{:S(2)}, u32[]{:S(2)}) collective-permute-start(bf16[128,512]{1,0:T(8,128)(2,1)S(1)} %get-tuple-element.133), channel_id=1, source_target_pairs={{0,8},{8,16},{16,24},{24,32},{32,40},{40,48},{48,56},{56,64},{64,7... | collective-permute-start | bytes 393224 | tf_op jit(solution)/shard_map/ppermute | solution.py:17
  29.8 0.9 constant_dynamic-update-slice_fusion.8
  30.7 1.1 collective-permute-done
  33.1 165.0 %all-reduce.3.cloned.1.call-done = bf16[2,128,512]{2,1,0:T(8,128)(2,1)} async-done(((bf16[2,128,512]{2,1,0:T(8,128)(2,1)}), bf16[2,128,512]{2,1,0:T(8,128)(2,1)}) %all-reduce.3.cloned.1.call-update) | async-done | bytes 262160 | tf_op jit(solution)/shard_map/psum | solution.py:33
  198.1 1.7 constant_dynamic-update-slice_fusion.7
  199.8 0.8 constant_dynamic-update-slice_fusion.6
  200.6 0.8 constant_dynamic-update-slice_fusion.5
  202.3 3.0 broadcast_in_dim.71
  205.2 89.1 %while.17 = (s32[]{:T(128)}, f32[20,128,512]{2,1,0:T(8,128)}, bf16[4,128,256]{2,1,0:T(8,128)(2,1)}, bf16[4,128,256]{2,1,0:T(8,128)(2,1)}, s32[4,8]{1,0:T(4,128)S...) while((s32[]{:T(128)}, f32[20,128,512]{2,1,0:T(8,128)}, ...), condition=%wide.region_6.7_spmd, body=%wide.region_1.6_spmd.sunk | while | flops 545856576 | bytes 48772516 | solution.py:124
  205.4 0.9 constant_dynamic-slice_fusion.6
  206.3 0.9 constant_dynamic-slice_fusion.7
  207.3 2.4 gather_fusion
  213.1 1.0 convolution_convert_fusion.4
  214.0 2.7 fusion.97
  217.5 1.8 fusion.95
  219.5 1.5 copy.75
  221.0 1.5 pad_maximum_fusion.5
  223.2 4.4 scatter_fusion
  227.7 0.9 constant_dynamic-slice_fusion.6
  228.6 0.9 constant_dynamic-slice_fusion.7
  229.6 2.4 gather_fusion
  235.4 1.0 convolution_convert_fusion.4
  236.4 2.7 fusion.97
  239.8 1.8 fusion.95
  241.8 1.5 copy.75
  243.3 1.5 pad_maximum_fusion.5
  245.5 4.3 scatter_fusion
  249.9 0.9 constant_dynamic-slice_fusion.6
  250.9 0.9 constant_dynamic-slice_fusion.7
  251.9 2.4 gather_fusion
  257.6 1.0 convolution_convert_fusion.4
  258.6 2.7 fusion.97
  262.1 1.8 fusion.95
  264.1 1.5 copy.75
  265.5 1.5 pad_maximum_fusion.5
  267.7 4.3 scatter_fusion
  272.2 0.9 constant_dynamic-slice_fusion.6
  273.2 0.9 constant_dynamic-slice_fusion.7
  274.1 2.4 gather_fusion
  279.9 1.0 convolution_convert_fusion.4
  280.9 2.7 fusion.97
  284.3 1.8 fusion.95
  286.3 1.5 copy.75
  287.8 1.5 pad_maximum_fusion.5
  290.0 4.4 scatter_fusion
  294.4 1.9 slice.138
  296.2 2.9 convert.11
  299.2 2.9 collective-permute-start.5
  302.1 1.3 collective-permute-start.6
  303.4 1.2 fusion.38
  304.5 1.3 slice.130
  305.8 10.8 %collective-permute-start.7 = (bf16[4,128,512]{2,1,0:T(8,128)(2,1)}, bf16[4,128,512]{2,1,0:T(8,128)(2,1)S(1)}, u32[]{:S(2)}, u32[]{:S(2)}) collective-permute-start(bf16[4,128,512]{2,1,0:T(8,128)(2,1)} %get-tuple-element.125), channel_id=1, source_target_pairs={{0,256},{8,264},{16,272},{24,280},{32,288},{40,296},{48,304},{56,3... | collective-permute-start | bytes 1572872 | tf_op jit(solution)/shard_map/ppermute | solution.py:28
  316.6 1.9 collective-permute-start.9
  318.5 2.4 collective-permute-start.8
  321.0 1.0 fusion.30
  322.0 141.4 %all-reduce.5.cloned.1.call-done = f32[2,128,512]{2,1,0:T(8,128)} async-done(((f32[2,128,512]{2,1,0:T(8,128)}), f32[2,128,512]{2,1,0:T(8,128)}) %all-reduce.5.cloned.1.call-update) | async-done | bytes 524304 | tf_op jit(solution)/shard_map/psum | solution.py:133
  463.4 1.2 fusion.27
  464.9 0.8 fusion.39
  (144 shorter events, 24.8 us)
Async XLA Ops:
  7.2 22.2 %copy-start = (s32[256,3]{0,1:T(4,128)S(1)}, s32[256,3]{0,1:T(4,128)}, u32[]{:S(2)}) copy-start(s32[256,3]{0,1:T(4,128)} %param.17) | copy-start | bytes 9220
  7.2 190.9 %all-reduce.3.cloned.1.call-start = ((), (), s32[]{:S(2)}) async-start(), calls=%async_computation | async-start | bytes 524288 | tf_op jit(solution)/shard_map/psum | solution.py:33
  9.2 192.3 %collective-permute-start.4 = (bf16[4,128,512]{2,1,0:T(8,128)(2,1)S(1)}, bf16[4,128,512]{2,1,0:T(8,128)(2,1)S(1)}, u32[]{:S(2)}, u32[]{:S(2)}) collective-permute-start(bf16[4,128,512]{2,1,0:T(8,128)(2,1)S(1)} %bitcast.122), channel_id=1, source_target_pairs={{0,64},{8,72},{16,80},{24,88},{32,96},{40,104},{48,112},{56,120},{... | collective-permute-start | bytes 1572872 | tf_op jit(solution)/shard_map/ppermute | solution.py:28
  12.7 187.9 %collective-permute-start.3 = (bf16[4,128,512]{2,1,0:T(8,128)(2,1)S(1)}, bf16[4,128,512]{2,1,0:T(8,128)(2,1)S(1)}, u32[]{:S(2)}, u32[]{:S(2)}) collective-permute-start(bf16[4,128,512]{2,1,0:T(8,128)(2,1)S(1)} %bitcast.123), channel_id=1, source_target_pairs={{0,128},{8,136},{16,144},{24,152},{32,160},{40,168},{48,176},{56,1... | collective-permute-start | bytes 1572872 | tf_op jit(solution)/shard_map/ppermute | solution.py:28
  17.2 182.6 %collective-permute-start.2 = (bf16[4,128,512]{2,1,0:T(8,128)(2,1)S(1)}, bf16[4,128,512]{2,1,0:T(8,128)(2,1)S(1)}, u32[]{:S(2)}, u32[]{:S(2)}) collective-permute-start(bf16[4,128,512]{2,1,0:T(8,128)(2,1)S(1)} %bitcast.124), channel_id=1, source_target_pairs={{0,256},{8,264},{16,272},{24,280},{32,288},{40,296},{48,304},{56,3... | collective-permute-start | bytes 1572872 | tf_op jit(solution)/shard_map/ppermute | solution.py:28
  23.0 440.4 %all-reduce.5.cloned.1.call-start = ((), (), s32[]{:S(2)}) async-start(), calls=%async_computation.1 | async-start | bytes 1048576 | tf_op jit(solution)/shard_map/psum | solution.py:133
  23.0 9.4 %collective-permute-start.1 = (bf16[128,512]{1,0:T(8,128)(2,1)S(1)}, bf16[128,512]{1,0:T(8,128)(2,1)S(1)}, u32[]{:S(2)}, u32[]{:S(2)}) collective-permute-start(bf16[128,512]{1,0:T(8,128)(2,1)S(1)} %get-tuple-element.132), channel_id=1, source_target_pairs={{8,0},{16,8},{24,16},{32,24},{40,32},{48,40},{56,48},{64,56},{72,6... | collective-permute-start | bytes 393224 | tf_op jit(solution)/shard_map/ppermute | solution.py:20
  24.3 7.4 %collective-permute-start = (bf16[128,512]{1,0:T(8,128)(2,1)S(1)}, bf16[128,512]{1,0:T(8,128)(2,1)S(1)}, u32[]{:S(2)}, u32[]{:S(2)}) collective-permute-start(bf16[128,512]{1,0:T(8,128)(2,1)S(1)} %get-tuple-element.133), channel_id=1, source_target_pairs={{0,8},{8,16},{16,24},{24,32},{32,40},{40,48},{48,56},{56,64},{64,7... | collective-permute-start | bytes 393224 | tf_op jit(solution)/shard_map/ppermute | solution.py:17
  210.5 2.4 copy-start.1
  212.0 1.1 copy-start.2
  232.8 2.4 copy-start.1
  234.3 1.1 copy-start.2
  255.1 2.3 copy-start.1
  256.6 1.1 copy-start.2
  277.3 2.3 copy-start.1
  278.8 1.1 copy-start.2
  299.2 21.8 %collective-permute-start.5 = (bf16[128,512]{1,0:T(8,128)(2,1)S(1)}, bf16[128,512]{1,0:T(8,128)(2,1)S(1)}, u32[]{:S(2)}, u32[]{:S(2)}) collective-permute-start(bf16[128,512]{1,0:T(8,128)(2,1)S(1)} %get-tuple-element.128), channel_id=1, source_target_pairs={{0,8},{8,16},{16,24},{24,32},{32,40},{40,48},{48,56},{56,64},{64,7... | collective-permute-start | bytes 393224 | tf_op jit(solution)/shard_map/ppermute | solution.py:17
  302.1 18.9 %collective-permute-start.6 = (bf16[128,512]{1,0:T(8,128)(2,1)S(1)}, bf16[128,512]{1,0:T(8,128)(2,1)S(1)}, u32[]{:S(2)}, u32[]{:S(2)}) collective-permute-start(bf16[128,512]{1,0:T(8,128)(2,1)S(1)} %get-tuple-element.129), channel_id=1, source_target_pairs={{8,0},{16,8},{24,16},{32,24},{40,32},{48,40},{56,48},{64,56},{72,6... | collective-permute-start | bytes 393224 | tf_op jit(solution)/shard_map/ppermute | solution.py:20
  305.8 158.8 %collective-permute-start.7 = (bf16[4,128,512]{2,1,0:T(8,128)(2,1)}, bf16[4,128,512]{2,1,0:T(8,128)(2,1)S(1)}, u32[]{:S(2)}, u32[]{:S(2)}) collective-permute-start(bf16[4,128,512]{2,1,0:T(8,128)(2,1)} %get-tuple-element.125), channel_id=1, source_target_pairs={{0,256},{8,264},{16,272},{24,280},{32,288},{40,296},{48,304},{56,3... | collective-permute-start | bytes 1572872 | tf_op jit(solution)/shard_map/ppermute | solution.py:28
  316.6 148.0 %collective-permute-start.9 = (bf16[4,128,512]{2,1,0:T(8,128)(2,1)}, bf16[4,128,512]{2,1,0:T(8,128)(2,1)S(1)}, u32[]{:S(2)}, u32[]{:S(2)}) collective-permute-start(bf16[4,128,512]{2,1,0:T(8,128)(2,1)} %get-tuple-element.126), channel_id=1, source_target_pairs={{0,64},{8,72},{16,80},{24,88},{32,96},{40,104},{48,112},{56,120},{... | collective-permute-start | bytes 1572872 | tf_op jit(solution)/shard_map/ppermute | solution.py:28
  318.5 146.1 %collective-permute-start.8 = (bf16[4,128,512]{2,1,0:T(8,128)(2,1)S(1)}, bf16[4,128,512]{2,1,0:T(8,128)(2,1)S(1)}, u32[]{:S(2)}, u32[]{:S(2)}) collective-permute-start(bf16[4,128,512]{2,1,0:T(8,128)(2,1)S(1)} %get-tuple-element.127), channel_id=1, source_target_pairs={{0,128},{8,136},{16,144},{24,152},{32,160},{40,168},{48,176},{56,1... | collective-permute-start | bytes 1572872 | tf_op jit(solution)/shard_map/ppermute | solution.py:28
Sparse Core Ops, SparseCore 0:
  23.1 174.9 all-reduce.2
  299.3 164.0 all-reduce.4
where the time goes:
time: 474 us; the launch traced here: 473 us
  waiting for transfers between devices  308 us (65%)
  local copies, waits for them, and re-layouts  52.5 us (11%)
  starting transfers between devices  38.6 us (8%)
  other arithmetic  30.6 us (6%)
  matrix products  28.4 us (6%)
  between operations  14.3 us (3%)
    psum x1, waiting for transfers between devices, spread(): return lax.psum(kept, axis)  165 us
    psum x1, waiting for transfers between devices, shards(): glob_sum = lax.psum(glob_terms, 'seq')  141 us
    ppermute x6, starting transfers between devices, from_partner(): return lax.ppermute(value, axis, pairs)  28.1 us
    scatter-add x4, other arithmetic, tile_step(): grad_pool = grad_pool.at[index_row].add(tiles)  17.4 us
    dot_general x4, matrix products, tile_step(): jnp.einsum('htu,thd->uhd', dscores, query, preferred_element_type=jnp.flo...  11 us
  transfers between devices with their start and end apart: 12, of which 3 were waited for; matrix products, arithmetic and copies ran while one was open for 2% of the time, Pallas kernels for 0%

commit v1 on v0

v1 whole, which is shorter than its diff:
```python
import jax
import jax.numpy as jnp
from jax import lax
from jax.experimental import pallas as pl
from jax.experimental.pallas import tpu as pltpu
from jax.sharding import PartitionSpec as P

DH = 128
BLK = 128
GLOBAL = 2
RAND = 3
NEG = -1e30
F32 = jnp.float32
BF16 = jnp.bfloat16


def dot(a, b, ca, cb):
    return lax.dot_general(a, b, (((ca,), (cb,)), ((), ())), preferred_element_type=F32)


def attention_kernel(nblk, heads, idx_ref, bias_ref, q_ref, do_ref, k_ref, v_ref, left_ref, right_ref,
                     glob_ref, *rest):
    part_refs = rest[:RAND]
    ctx_ref, dq_ref, own_ref, gleft_ref, gright_ref, gglob_ref = rest[RAND:RAND + 6]
    gpart_refs = rest[RAND + 6:2 * RAND + 6]
    kwin, vwin, ksel, vsel, acc_win, acc_glob, acc_part = rest[2 * RAND + 6:]
    width = heads * DH
    tokens = nblk * BLK
    nwin = GLOBAL + 3
    scale = 1.0 / DH**0.5

    kwin[:BLK] = left_ref[:, :width]
    vwin[:BLK] = left_ref[:, width:]
    kwin[BLK:BLK + tokens] = k_ref[...]
    vwin[BLK:BLK + tokens] = v_ref[...]
    kwin[BLK + tokens:] = right_ref[:, :width]
    vwin[BLK + tokens:] = right_ref[:, width:]
    for h in range(heads):
        hs = slice(h * DH, (h + 1) * DH)
        ksel[:GLOBAL * BLK, hs] = glob_ref[h]
        vsel[:GLOBAL * BLK, hs] = glob_ref[heads + h]
    acc_win[...] = jnp.zeros_like(acc_win)
    acc_glob[...] = jnp.zeros_like(acc_glob)
    acc_part[...] = jnp.zeros_like(acc_part)

    def step(b, carry):
        start = pl.multiple_of(b * BLK, BLK)
        rows = pl.ds(start, BLK)
        ksel[GLOBAL * BLK:nwin * BLK] = kwin[pl.ds(start, 3 * BLK)]
        vsel[GLOBAL * BLK:nwin * BLK] = vwin[pl.ds(start, 3 * BLK)]
        picks = []
        for r in range(RAND):
            pick = idx_ref[b * RAND + r]
            picks.append(pick)
            src = pl.ds(pl.multiple_of(pick * BLK, BLK), BLK)
            dst = slice((nwin + r) * BLK, (nwin + r + 1) * BLK)
            ksel[dst] = part_refs[r][src, :width]
            vsel[dst] = part_refs[r][src, width:]
        bias = bias_ref[b]
        for h in range(heads):
            hs = slice(h * DH, (h + 1) * DH)
            query = q_ref[rows, hs]
            dout = do_ref[rows, hs]
            keys = ksel[:, hs]
            vals = vsel[:, hs]
            scores = dot(query, keys, 1, 1) * scale + bias
            dprobs = dot(dout, vals, 1, 1)
            top = jnp.max(scores, axis=-1, keepdims=True)
            expo = jnp.exp(scores - top)
            probs = expo * (1.0 / jnp.sum(expo, axis=-1, keepdims=True))
            probs_b = probs.astype(BF16)
            delta = jnp.sum(probs * dprobs, axis=-1, keepdims=True)
            dscores = (probs * (dprobs - delta) * scale).astype(BF16)
            ctx_ref[rows, hs] = dot(probs_b, vals, 1, 0).astype(BF16)
            dq_ref[rows, hs] = dot(dscores, keys, 1, 0).astype(BF16)
            kterm = dot(query.T, dscores, 1, 0)
            vterm = dot(dout.T, probs_b, 1, 0)
            for base, term in ((h * DH, kterm), (width + h * DH, vterm)):
                at = slice(base, base + DH)
                for g in range(GLOBAL):
                    acc_glob[g, at] += term[:, g * BLK:(g + 1) * BLK]
                for w in range(3):
                    o = GLOBAL + w
                    acc_win[b + w, at] += term[:, o * BLK:(o + 1) * BLK]
                for r in range(RAND):
                    o = nwin + r
                    acc_part[r, picks[r], at] += term[:, o * BLK:(o + 1) * BLK]
        return carry

    lax.fori_loop(0, nblk, step, 0)
    gleft_ref[...] = acc_win[0].astype(BF16)
    gright_ref[...] = acc_win[nblk + 1].astype(BF16)
    own_ref[...] = acc_win[1:nblk + 1]
    gglob_ref[...] = acc_glob[...].astype(BF16)
    for r in range(RAND):
        gpart_refs[r][...] = acc_part[r].astype(BF16)


def finish_kernel(nblk, heads, first_ref, own_ref, low_ref, high_ref, glob_ref, *rest):
    part_refs = rest[:RAND]
    gk_ref, gv_ref = rest[RAND:]
    first = first_ref[0].astype(F32)
    width = heads * DH
    for b in range(nblk):
        rows = slice(b * BLK, (b + 1) * BLK)
        for c in range(2 * heads):
            at = slice(c * DH, (c + 1) * DH)
            total = own_ref[b, at]
            for r in range(RAND):
                total = total + part_refs[r][b, at].astype(F32)
            if b == 0:
                total = total + low_ref[at].astype(F32)
            if b == nblk - 1:
                total = total + high_ref[at].astype(F32)
            if b < GLOBAL:
                total = jnp.where(first > 0, glob_ref[b, at].astype(F32), total)
            out = gk_ref if c < heads else gv_ref
            h = c % heads
            out[rows, h * DH:(h + 1) * DH] = total.T.astype(BF16)


def shards(queries, keys, values, grad_out, rand_blocks):
    n_seq = lax.axis_size("seq")
    myself = lax.axis_index("seq")
    tokens, width = queries.shape
    nblk = tokens // BLK
    heads = width // DH
    nwin = GLOBAL + 3
    up = [(i, i + 1) for i in range(n_seq - 1)]
    down = [(j, i) for i, j in up]
    masks = [n_seq >> (r + 1) for r in range(RAND)]

    def partner(x, r):
        return lax.ppermute(x, "seq", [(i, i ^ masks[r]) for i in range(n_seq)])

    kv = jnp.concatenate([keys, values], axis=1)
    fetched = [partner(kv, r) for r in range(RAND)]
    left = lax.ppermute(kv[tokens - BLK:], "seq", up)
    right = lax.ppermute(kv[:BLK], "seq", down)

    cols = 2 * heads
    grows = GLOBAL * BLK
    unit = cols * grows // n_seq
    glob = kv[:grows].reshape(grows, cols, DH).transpose(1, 0, 2).reshape(n_seq, unit, DH)
    piece = lax.all_to_all(glob, "seq", 0, 0, tiled=True)[0]
    glob = lax.all_to_all(jnp.broadcast_to(piece[None], (n_seq, unit, DH)), "seq", 0, 0, tiled=True)
    glob = glob.reshape(cols, grows, DH)

    mine = lax.dynamic_slice_in_dim(rand_blocks, myself * nblk, nblk, 0)
    picks = (mine % nblk).reshape(-1)
    qblock = myself * nblk + jnp.arange(nblk, dtype=jnp.int32)
    window = qblock[:, None] + jnp.arange(-1, 2, dtype=jnp.int32)[None, :]
    live = jnp.concatenate(
        [jnp.ones((nblk, GLOBAL), bool), (window >= GLOBAL) & (window < nblk * n_seq), mine >= GLOBAL], axis=1)
    bias = jnp.repeat(jnp.where(live, 0.0, NEG).astype(F32), BLK, axis=1)[:, None, :]

    smem = pl.BlockSpec(memory_space=pltpu.SMEM)
    vmem = pl.BlockSpec(memory_space=pltpu.VMEM)
    sds = jax.ShapeDtypeStruct
    nkeys = (nwin + RAND) * BLK
    outs = pl.pallas_call(
        lambda *refs: attention_kernel(nblk, heads, *refs),
        out_shape=[
            sds((tokens, width), BF16), sds((tokens, width), BF16),
            sds((nblk, 2 * width, BLK), F32), sds((2 * width, BLK), BF16), sds((2 * width, BLK), BF16),
            sds((GLOBAL, 2 * width, BLK), BF16),
        ] + [sds((nblk, 2 * width, BLK), BF16)] * RAND,
        in_specs=[smem] + [vmem] * (8 + RAND),
        out_specs=[vmem] * (6 + RAND),
        scratch_shapes=[
            pltpu.VMEM((tokens + 2 * BLK, width), BF16), pltpu.VMEM((tokens + 2 * BLK, width), BF16),
            pltpu.VMEM((nkeys, width), BF16), pltpu.VMEM((nkeys, width), BF16),
            pltpu.VMEM((nblk + 2, 2 * width, BLK), F32), pltpu.VMEM((GLOBAL, 2 * width, BLK), F32),
            pltpu.VMEM((RAND, nblk, 2 * width, BLK), F32),
        ],
        compiler_params=pltpu.CompilerParams(vmem_limit_bytes=48 * 1024 * 1024),
        name="attention",
    )(picks, bias, queries, grad_out, keys, values, left, right, glob, *fetched)
    context, grad_q, own, gleft, gright, gglob = outs[:6]
    gparts = outs[6:]

    back = [partner(gparts[r], r) for r in range(RAND)]
    high = lax.ppermute(gleft, "seq", down)
    low = lax.ppermute(gright, "seq", up)
    terms = lax.all_to_all(gglob.reshape(n_seq, unit, DH), "seq", 0, 0, tiled=True)
    summed = jnp.sum(terms.astype(F32), axis=0).astype(BF16)
    gsum = lax.all_to_all(jnp.broadcast_to(summed[None], (n_seq, unit, DH)), "seq", 0, 0, tiled=True)
    gsum = gsum.reshape(GLOBAL, 2 * width, BLK)
    first = (myself == 0).astype(jnp.int32).reshape(1)

    grad_k, grad_v = pl.pallas_call(
        lambda *refs: finish_kernel(nblk, heads, *refs),
        out_shape=[sds((tokens, width), BF16), sds((tokens, width), BF16)],
        in_specs=[smem] + [vmem] * (4 + RAND),
        out_specs=[vmem] * 2,
        compiler_params=pltpu.CompilerParams(vmem_limit_bytes=48 * 1024 * 1024),
        name="finish",
    )(first, own, low, high, gsum, *back)
    return context, grad_q, grad_k, grad_v


def solution(mesh):
    specs = (P("seq", "head"),) * 4
    return jax.shard_map(shards, mesh=mesh, in_specs=specs + (P(),), out_specs=specs, check_vma=False)
```

time: 474 us -> 174 us (0.37)
  waiting for transfers between devices: 308 us -> 53.9 us
  starting transfers between devices: 38.6 us -> 97.9 us
  local copies, waits for them, and re-layouts: 52.5 us -> 10.1 us
  other arithmetic: 30.6 us -> 0.32 us
  matrix products: 28.4 us -> 0 us
  between operations: 14.3 us -> 0.85 us
  Pallas kernels: 0 us -> 9.86 us
    psum x2 -> x0, waiting for transfers between devices: 306 us -> none  [the longest x1 165 us: spread(): return lax.psum(kept, axis)]
    all_to_all x0 -> x4, starting transfers between devices: none -> 62.1 us  [the longest x1 32.8 us: shards(): lax.all_to_all(jnp.broadcast_to(piece[None], (n_seq, unit, DH)), 'seq', 0...]
    all_to_all x0 -> x4, waiting for transfers between devices: none -> 42.3 us  [the longest x1 22.4 us: shards(): lax.all_to_all(gglob.reshape(n_seq, unit, DH), 'seq', 0, 0, tiled=True)]
    dot_general x20 -> x0, matrix products: 26.1 us -> none  [the longest x4 11 us: tile_step(): jnp.einsum('htu,thd->uhd', dscores, query, preferred_element_type=jnp.flo...]
    scatter-add x7 -> x0, other arithmetic: 19.7 us -> none  [the longest x4 17.4 us: tile_step(): grad_pool = grad_pool.at[index_row].add(tiles)]
    ppermute x10, waiting for transfers between devices: 1.13 us -> 11.5 us  [the longest x6 5.83 us: partner(): return lax.ppermute(x, 'seq', [(i, i ^ masks[r]) for i in range(n_seq)])]
    reshape x24 -> x2, local copies, waits for them, and re-layouts: 11.8 us -> 1.78 us  [the longest x1 1.7 us: shards(): kv[:grows].reshape(grows, cols, DH).transpose(1, 0, 2)]
    pallas_call x0 -> x2, Pallas kernels: none -> 9.86 us  [the longest x1 8.68 us: shards(): pl.pallas_call(lambda *refs: attention_kernel(nblk, heads, *refs), out_sh...]
  transfers between devices with their start and end apart: 12 -> 14, of which waited for: 3 -> 7; matrix products, arithmetic and copies ran while one was open for 2% -> 2% of each run, Pallas kernels for 0% -> 0%
where the time goes in v1:
time: 174 us; the launch traced here: 173 us
  starting transfers between devices  97.9 us (56%)
  waiting for transfers between devices  53.9 us (31%)
  local copies, waits for them, and re-layouts  10.1 us (6%)
  Pallas kernels  9.86 us (6%)
    all_to_all x1, starting transfers between devices, shards(): lax.all_to_all(jnp.broadcast_to(piece[None], (n_seq, unit, DH)), 'seq', 0...  32.8 us
    ppermute x6, starting transfers between devices, partner(): return lax.ppermute(x, 'seq', [(i, i ^ masks[r]) for i in range(n_seq)])  25.2 us
    all_to_all x1, waiting for transfers between devices, shards(): lax.all_to_all(gglob.reshape(n_seq, unit, DH), 'seq', 0, 0, tiled=True)  22.4 us
    all_to_all x1, starting transfers between devices, shards(): piece = lax.all_to_all(glob, 'seq', 0, 0, tiled=True)[0]  16.6 us
    all_to_all x1, waiting for transfers between devices, shards(): lax.all_to_all(jnp.broadcast_to(piece[None], (n_seq, unit, DH)), 'seq', 0...  10.6 us
    all_to_all x1, waiting for transfers between devices, shards(): lax.all_to_all(jnp.broadcast_to(summed[None], (n_seq, unit, DH)), 'seq',...  9.36 us
    pallas_call x1, Pallas kernels, shards(): pl.pallas_call(lambda *refs: attention_kernel(nblk, heads, *refs), out_sh...  8.68 us
    all_to_all x1, starting transfers between devices, shards(): lax.all_to_all(gglob.reshape(n_seq, unit, DH), 'seq', 0, 0, tiled=True)  7.92 us
  transfers between devices with their start and end apart: 14, of which 7 were waited for; matrix products, arithmetic and copies ran while one was open for 2% of the time, Pallas kernels for 0%

profile of v1, /device:TPU:6, one launch (start us, length us, event | category | flops | bytes accessed | tf_op | source)
XLA Modules:
  0.0 172.9 jit_solution(8068502471987202127)
XLA Ops:
  0.6 0.0 copy-start.2
  0.6 1.7 %constant_dynamic-update-slice_fusion.1 = bf16[512,512]{1,0:T(8,128)(2,1)} fusion(bf16[512,256]{1,0:T(8,128)(2,1)} %refs_4_.1), kind=kLoop, calls=%fused_computation.3 | loop fusion | bytes 524288
  2.4 0.0 copy-done.2
  2.4 0.7 constant_dynamic-update-slice_fusion
  3.1 1.7 copy_bitcast_fusion
  4.8 16.6 %all-to-all-start = ((bf16[64,16,128]{2,1,0:T(8,128)(2,1)}), bf16[64,16,128]{2,1,0:T(8,128)(2,1)S(1)}, u32[]{:S(2)}, u32[]{:S(2)}) async-start(bf16[64,16,128]{2,1,0:T(8,128)(2,1)} %bitcast.2), calls=%async_computation | async-start | bytes 524288 | tf_op jit(solution)/shard_map/all_to_all | solution.py:145
  21.4 4.4 %collective-permute-start.3 = (bf16[512,512]{1,0:T(8,128)(2,1)}, bf16[512,512]{1,0:T(8,128)(2,1)S(1)}, u32[]{:S(2)}, u32[]{:S(2)}) collective-permute-start(bf16[512,512]{1,0:T(8,128)(2,1)} %constant_dynamic-update-slice_fusion), channel_id=1, source_target_pairs={{0,128},{8,136},{16,144},{24,152},{32,160},{40,168},{48,176},{56,1... | collective-permute-start | bytes 1572872 | tf_op jit(solution)/shard_map/ppermute | solution.py:134
  25.8 5.7 %collective-permute-start.2 = (bf16[512,512]{1,0:T(8,128)(2,1)}, bf16[512,512]{1,0:T(8,128)(2,1)S(1)}, u32[]{:S(2)}, u32[]{:S(2)}) collective-permute-start(bf16[512,512]{1,0:T(8,128)(2,1)} %constant_dynamic-update-slice_fusion), channel_id=1, source_target_pairs={{0,256},{8,264},{16,272},{24,280},{32,288},{40,296},{48,304},{56,3... | collective-permute-start | bytes 1572872 | tf_op jit(solution)/shard_map/ppermute | solution.py:134
  31.5 2.5 %collective-permute-start.4 = (bf16[512,512]{1,0:T(8,128)(2,1)}, bf16[512,512]{1,0:T(8,128)(2,1)S(1)}, u32[]{:S(2)}, u32[]{:S(2)}) collective-permute-start(bf16[512,512]{1,0:T(8,128)(2,1)} %constant_dynamic-update-slice_fusion), channel_id=1, source_target_pairs={{0,64},{8,72},{16,80},{24,88},{32,96},{40,104},{48,112},{56,120},{... | collective-permute-start | bytes 1572872 | tf_op jit(solution)/shard_map/ppermute | solution.py:134
  34.0 1.0 fusion.2
  35.0 1.3 collective-permute-start.1
  36.3 4.6 %collective-permute-start = (bf16[128,512]{1,0:T(8,128)(2,1)S(1)}, bf16[128,512]{1,0:T(8,128)(2,1)S(1)}, u32[]{:S(2)}, u32[]{:S(2)}) collective-permute-start(bf16[128,512]{1,0:T(8,128)(2,1)S(1)} %get-tuple-element.27), channel_id=1, source_target_pairs={{0,8},{8,16},{16,24},{24,32},{32,40},{40,48},{48,56},{56,64},{64,7... | collective-permute-start | bytes 393224 | tf_op jit(solution)/shard_map/ppermute | solution.py:138
  40.9 0.0 copy-start.8
  40.9 0.7 copy-done.8
  41.6 0.1 add_select_fusion.1
  41.7 0.1 copy.11
  41.8 0.1 reshape.40.refs_0_
  41.9 0.0 all-to-all-done
  41.9 0.0 copy-start.4
  41.9 0.7 broadcast_in_dim.30
  42.6 0.0 copy-start.1
  42.6 0.0 copy-start.3
  42.6 32.8 %all-to-all-start.1 = ((bf16[64,16,128]{2,1,0:T(8,128)(2,1)}), bf16[64,16,128]{2,1,0:T(8,128)(2,1)S(1)}, u32[]{:S(2)}, u32[]{:S(2)}) async-start(bf16[64,16,128]{2,1,0:T(8,128)(2,1)} %broadcast_in_dim.30), calls=%async_computation.1 | async-start | bytes 524288 | tf_op jit(solution)/shard_map/all_to_all | solution.py:146
  75.5 0.1 fusion.1
  75.6 0.1 add_select_fusion
  75.7 0.1 copy.12
  75.8 0.0 collective-permute-done.1.refs_7_
  75.8 0.0 collective-permute-done.refs_6_
  75.8 0.0 collective-permute-done.3.refs_10_
  75.8 0.0 collective-permute-done.2.refs_9_
  75.8 2.6 %collective-permute-done.4.refs_11_ = bf16[512,512]{1,0:T(8,128)(2,1)S(1)} collective-permute-done((bf16[512,512]{1,0:T(8,128)(2,1)}, bf16[512,512]{1,0:T(8,128)(2,1)S(1)}, u32[]{:S(2)}, u32[]{:S(2)}) %collective-permute-start.4) | collective-permute-done | bytes 524320 | tf_op jit(solution)/shard_map/ppermute | solution.py:134
  78.4 10.6 %all-to-all-done.1 = bf16[64,16,128]{2,1,0:T(8,128)(2,1)S(1)} async-done(((bf16[64,16,128]{2,1,0:T(8,128)(2,1)}), bf16[64,16,128]{2,1,0:T(8,128)(2,1)S(1)}, u32[]{:S(2)}, u32[]{:S(2)}) %all-to-all-start.1) | async-done | bytes 262176 | tf_op jit(solution)/shard_map/all_to_all | solution.py:146
  89.0 0.1 broadcast_in_dim.28
  89.0 0.0 copy-done.4
  89.0 0.0 copy-done.1
  89.0 0.0 copy-done.3
  89.0 8.7 %attention.1 = (bf16[512,256]{1,0:T(8,128)(2,1)}, bf16[512,256]{1,0:T(8,128)(2,1)}, f32[4,512,128]{2,1,0:T(8,128)}, bf16[512,128]{1,0:T(8,128)(2,1)S(1)}, bf16[5...) custom-call(s32[12]{0:T(128)S(1)} %reshape.40.refs_0_, ...), custom_call_target="tpu_custom_call" | custom-call | tf_op jit(solution)/shard_map/attention/pallas_call | solution.py:161
  97.7 0.0 copy-start.5
  97.7 0.8 copy-done.5
  98.5 0.0 copy-start.6
  98.5 0.8 copy-done.6
  99.3 0.0 copy-start.7
  99.3 0.8 copy-done.7
  100.1 0.0 copy-start
  100.1 7.9 %all-to-all-start.2 = ((bf16[64,16,128]{2,1,0:T(8,128)(2,1)}), bf16[64,16,128]{2,1,0:T(8,128)(2,1)S(1)}, u32[]{:S(2)}, u32[]{:S(2)}) async-start(bf16[64,16,128]{2,1,0:T(8,128)(2,1)} %bitcast.6), calls=%async_computation.2 | async-start | bytes 524288 | tf_op jit(solution)/shard_map/all_to_all | solution.py:185
  108.0 7.5 %collective-permute-start.7 = (bf16[4,512,128]{2,1,0:T(8,128)(2,1)}, bf16[4,512,128]{2,1,0:T(8,128)(2,1)S(1)}, u32[]{:S(2)}, u32[]{:S(2)}) collective-permute-start(bf16[4,512,128]{2,1,0:T(8,128)(2,1)} %copy-done.7), channel_id=1, source_target_pairs={{0,256},{8,264},{16,272},{24,280},{32,288},{40,296},{48,304},{56,3... | collective-permute-start | bytes 1572872 | tf_op jit(solution)/shard_map/ppermute | solution.py:134
  115.5 2.6 %collective-permute-start.8 = (bf16[4,512,128]{2,1,0:T(8,128)(2,1)}, bf16[4,512,128]{2,1,0:T(8,128)(2,1)S(1)}, u32[]{:S(2)}, u32[]{:S(2)}) collective-permute-start(bf16[4,512,128]{2,1,0:T(8,128)(2,1)} %copy-done.6), channel_id=1, source_target_pairs={{0,128},{8,136},{16,144},{24,152},{32,160},{40,168},{48,176},{56,1... | collective-permute-start | bytes 1572872 | tf_op jit(solution)/shard_map/ppermute | solution.py:134
  118.1 2.5 %collective-permute-start.9 = (bf16[4,512,128]{2,1,0:T(8,128)(2,1)}, bf16[4,512,128]{2,1,0:T(8,128)(2,1)S(1)}, u32[]{:S(2)}, u32[]{:S(2)}) collective-permute-start(bf16[4,512,128]{2,1,0:T(8,128)(2,1)} %copy-done.5), channel_id=1, source_target_pairs={{0,64},{8,72},{16,80},{24,88},{32,96},{40,104},{48,112},{56,120},{... | collective-permute-start | bytes 1572872 | tf_op jit(solution)/shard_map/ppermute | solution.py:134
  120.7 22.4 %all-to-all-done.2 = bf16[64,16,128]{2,1,0:T(8,128)(2,1)S(1)} async-done(((bf16[64,16,128]{2,1,0:T(8,128)(2,1)}), bf16[64,16,128]{2,1,0:T(8,128)(2,1)S(1)}, u32[]{:S(2)}, u32[]{:S(2)}) %all-to-all-start.2) | async-done | bytes 262176 | tf_op jit(solution)/shard_map/all_to_all | solution.py:185
  143.1 0.1 reduce_sum.12
  143.1 0.7 broadcast_in_dim.31
  143.9 4.7 %all-to-all-start.3 = ((bf16[64,16,128]{2,1,0:T(8,128)(2,1)}), bf16[64,16,128]{2,1,0:T(8,128)(2,1)S(1)}, u32[]{:S(2)}, u32[]{:S(2)}) async-start(bf16[64,16,128]{2,1,0:T(8,128)(2,1)} %broadcast_in_dim.31), calls=%async_computation.3 | async-start | bytes 524288 | tf_op jit(solution)/shard_map/all_to_all | solution.py:187
  148.6 3.5 %collective-permute-start.5 = (bf16[512,128]{1,0:T(8,128)(2,1)S(1)}, bf16[512,128]{1,0:T(8,128)(2,1)S(1)}, u32[]{:S(2)}, u32[]{:S(2)}) collective-permute-start(bf16[512,128]{1,0:T(8,128)(2,1)S(1)} %get-tuple-element.18), channel_id=1, source_target_pairs={{0,8},{8,16},{16,24},{24,32},{32,40},{40,48},{48,56},{56,64},{64,7... | collective-permute-start | bytes 393224 | tf_op jit(solution)/shard_map/ppermute | solution.py:184
  152.1 1.3 collective-permute-start.6
  153.4 1.4 collective-permute-done.5.refs_2_
  154.7 4.3 %collective-permute-done.6.refs_3_ = bf16[512,128]{1,0:T(8,128)(2,1)S(1)} collective-permute-done((bf16[512,128]{1,0:T(8,128)(2,1)S(1)}, bf16[512,128]{1,0:T(8,128)(2,1)S(1)}, u32[]{:S(2)}, u32[]{:S(2)}) %collective-permute-start.6) | collective-permute-done | bytes 131104 | tf_op jit(solution)/shard_map/ppermute | solution.py:183
  159.1 0.0 collective-permute-done.7.refs_5_
  159.1 3.2 %collective-permute-done.8.refs_6_ = bf16[4,512,128]{2,1,0:T(8,128)(2,1)S(1)} collective-permute-done((bf16[4,512,128]{2,1,0:T(8,128)(2,1)}, bf16[4,512,128]{2,1,0:T(8,128)(2,1)S(1)}, u32[]{:S(2)}, u32[]{:S(2)}) %collective-permute-start.8) | collective-permute-done | bytes 524320 | tf_op jit(solution)/shard_map/ppermute | solution.py:134
  162.3 0.0 collective-permute-done.9.refs_7_
  162.3 9.4 %all-to-all-done.3 = bf16[64,16,128]{2,1,0:T(8,128)(2,1)S(1)} async-done(((bf16[64,16,128]{2,1,0:T(8,128)(2,1)}), bf16[64,16,128]{2,1,0:T(8,128)(2,1)S(1)}, u32[]{:S(2)}, u32[]{:S(2)}) %all-to-all-start.3) | async-done | bytes 262176 | tf_op jit(solution)/shard_map/all_to_all | solution.py:187
  171.7 0.0 copy-done
  171.7 1.2 finish.1
  (5 shorter events, 0.0 us)
Async XLA Ops:
  0.6 1.8 %copy-start.2 = (bf16[512,256]{1,0:T(8,128)(2,1)S(1)}, bf16[512,256]{1,0:T(8,128)(2,1)}, u32[]{:S(2)}) copy-start(bf16[512,256]{1,0:T(8,128)(2,1)} %refs_5_.1) | copy-start | bytes 786436
  4.8 37.0 %all-to-all-start = ((bf16[64,16,128]{2,1,0:T(8,128)(2,1)}), bf16[64,16,128]{2,1,0:T(8,128)(2,1)S(1)}, u32[]{:S(2)}, u32[]{:S(2)}) async-start(bf16[64,16,128]{2,1,0:T(8,128)(2,1)} %bitcast.2), calls=%async_computation | async-start | bytes 524288 | tf_op jit(solution)/shard_map/all_to_all | solution.py:145
  21.4 54.3 %collective-permute-start.3 = (bf16[512,512]{1,0:T(8,128)(2,1)}, bf16[512,512]{1,0:T(8,128)(2,1)S(1)}, u32[]{:S(2)}, u32[]{:S(2)}) collective-permute-start(bf16[512,512]{1,0:T(8,128)(2,1)} %constant_dynamic-update-slice_fusion), channel_id=1, source_target_pairs={{0,128},{8,136},{16,144},{24,152},{32,160},{40,168},{48,176},{56,1... | collective-permute-start | bytes 1572872 | tf_op jit(solution)/shard_map/ppermute | solution.py:134
  25.8 50.0 %collective-permute-start.2 = (bf16[512,512]{1,0:T(8,128)(2,1)}, bf16[512,512]{1,0:T(8,128)(2,1)S(1)}, u32[]{:S(2)}, u32[]{:S(2)}) collective-permute-start(bf16[512,512]{1,0:T(8,128)(2,1)} %constant_dynamic-update-slice_fusion), channel_id=1, source_target_pairs={{0,256},{8,264},{16,272},{24,280},{32,288},{40,296},{48,304},{56,3... | collective-permute-start | bytes 1572872 | tf_op jit(solution)/shard_map/ppermute | solution.py:134
  31.5 46.9 %collective-permute-start.4 = (bf16[512,512]{1,0:T(8,128)(2,1)}, bf16[512,512]{1,0:T(8,128)(2,1)S(1)}, u32[]{:S(2)}, u32[]{:S(2)}) collective-permute-start(bf16[512,512]{1,0:T(8,128)(2,1)} %constant_dynamic-update-slice_fusion), channel_id=1, source_target_pairs={{0,64},{8,72},{16,80},{24,88},{32,96},{40,104},{48,112},{56,120},{... | collective-permute-start | bytes 1572872 | tf_op jit(solution)/shard_map/ppermute | solution.py:134
  35.0 40.7 %collective-permute-start.1 = (bf16[128,512]{1,0:T(8,128)(2,1)S(1)}, bf16[128,512]{1,0:T(8,128)(2,1)S(1)}, u32[]{:S(2)}, u32[]{:S(2)}) collective-permute-start(bf16[128,512]{1,0:T(8,128)(2,1)S(1)} %get-tuple-element.26), channel_id=1, source_target_pairs={{8,0},{16,8},{24,16},{32,24},{40,32},{48,40},{56,48},{64,56},{72,6... | collective-permute-start | bytes 393224 | tf_op jit(solution)/shard_map/ppermute | solution.py:139
  36.3 39.4 %collective-permute-start = (bf16[128,512]{1,0:T(8,128)(2,1)S(1)}, bf16[128,512]{1,0:T(8,128)(2,1)S(1)}, u32[]{:S(2)}, u32[]{:S(2)}) collective-permute-start(bf16[128,512]{1,0:T(8,128)(2,1)S(1)} %get-tuple-element.27), channel_id=1, source_target_pairs={{0,8},{8,16},{16,24},{24,32},{32,40},{40,48},{48,56},{56,64},{64,7... | collective-permute-start | bytes 393224 | tf_op jit(solution)/shard_map/ppermute | solution.py:138
  40.9 0.7 copy-start.8
  41.9 47.1 %copy-start.4 = (bf16[512,256]{1,0:T(8,128)(2,1)S(1)}, bf16[512,256]{1,0:T(8,128)(2,1)}, u32[]{:S(2)}) copy-start(bf16[512,256]{1,0:T(8,128)(2,1)} %refs_3_.1) | copy-start | bytes 786436
  42.6 46.4 %copy-start.1 = (bf16[512,256]{1,0:T(8,128)(2,1)S(1)}, bf16[512,256]{1,0:T(8,128)(2,1)}, u32[]{:S(2)}) copy-start(bf16[512,256]{1,0:T(8,128)(2,1)} %refs_4_.1) | copy-start | bytes 786436
  42.6 46.4 %copy-start.3 = (bf16[512,256]{1,0:T(8,128)(2,1)S(1)}, bf16[512,256]{1,0:T(8,128)(2,1)}, u32[]{:S(2)}) copy-start(bf16[512,256]{1,0:T(8,128)(2,1)} %refs_2_.1) | copy-start | bytes 786436
  42.6 46.3 %all-to-all-start.1 = ((bf16[64,16,128]{2,1,0:T(8,128)(2,1)}), bf16[64,16,128]{2,1,0:T(8,128)(2,1)S(1)}, u32[]{:S(2)}, u32[]{:S(2)}) async-start(bf16[64,16,128]{2,1,0:T(8,128)(2,1)} %broadcast_in_dim.30), calls=%async_computation.1 | async-start | bytes 524288 | tf_op jit(solution)/shard_map/all_to_all | solution.py:146
  97.7 0.8 copy-start.5
  98.5 0.8 copy-start.6
  99.3 0.8 copy-start.7
  100.1 71.6 %copy-start = (f32[4,512,128]{2,1,0:T(8,128)S(1)}, f32[4,512,128]{2,1,0:T(8,128)}, u32[]{:S(2)}) copy-start(f32[4,512,128]{2,1,0:T(8,128)} %get-tuple-element.17.refs_1_) | copy-start | bytes 3145732
  100.1 42.9 %all-to-all-start.2 = ((bf16[64,16,128]{2,1,0:T(8,128)(2,1)}), bf16[64,16,128]{2,1,0:T(8,128)(2,1)S(1)}, u32[]{:S(2)}, u32[]{:S(2)}) async-start(bf16[64,16,128]{2,1,0:T(8,128)(2,1)} %bitcast.6), calls=%async_computation.2 | async-start | bytes 524288 | tf_op jit(solution)/shard_map/all_to_all | solution.py:185
  108.0 51.0 %collective-permute-start.7 = (bf16[4,512,128]{2,1,0:T(8,128)(2,1)}, bf16[4,512,128]{2,1,0:T(8,128)(2,1)S(1)}, u32[]{:S(2)}, u32[]{:S(2)}) collective-permute-start(bf16[4,512,128]{2,1,0:T(8,128)(2,1)} %copy-done.7), channel_id=1, source_target_pairs={{0,256},{8,264},{16,272},{24,280},{32,288},{40,296},{48,304},{56,3... | collective-permute-start | bytes 1572872 | tf_op jit(solution)/shard_map/ppermute | solution.py:134
  115.5 46.8 %collective-permute-start.8 = (bf16[4,512,128]{2,1,0:T(8,128)(2,1)}, bf16[4,512,128]{2,1,0:T(8,128)(2,1)S(1)}, u32[]{:S(2)}, u32[]{:S(2)}) collective-permute-start(bf16[4,512,128]{2,1,0:T(8,128)(2,1)} %copy-done.6), channel_id=1, source_target_pairs={{0,128},{8,136},{16,144},{24,152},{32,160},{40,168},{48,176},{56,1... | collective-permute-start | bytes 1572872 | tf_op jit(solution)/shard_map/ppermute | solution.py:134
  118.1 44.2 %collective-permute-start.9 = (bf16[4,512,128]{2,1,0:T(8,128)(2,1)}, bf16[4,512,128]{2,1,0:T(8,128)(2,1)S(1)}, u32[]{:S(2)}, u32[]{:S(2)}) collective-permute-start(bf16[4,512,128]{2,1,0:T(8,128)(2,1)} %copy-done.5), channel_id=1, source_target_pairs={{0,64},{8,72},{16,80},{24,88},{32,96},{40,104},{48,112},{56,120},{... | collective-permute-start | bytes 1572872 | tf_op jit(solution)/shard_map/ppermute | solution.py:134
  143.9 27.8 %all-to-all-start.3 = ((bf16[64,16,128]{2,1,0:T(8,128)(2,1)}), bf16[64,16,128]{2,1,0:T(8,128)(2,1)S(1)}, u32[]{:S(2)}, u32[]{:S(2)}) async-start(bf16[64,16,128]{2,1,0:T(8,128)(2,1)} %broadcast_in_dim.31), calls=%async_computation.3 | async-start | bytes 524288 | tf_op jit(solution)/shard_map/all_to_all | solution.py:187
  148.6 6.1 %collective-permute-start.5 = (bf16[512,128]{1,0:T(8,128)(2,1)S(1)}, bf16[512,128]{1,0:T(8,128)(2,1)S(1)}, u32[]{:S(2)}, u32[]{:S(2)}) collective-permute-start(bf16[512,128]{1,0:T(8,128)(2,1)S(1)} %get-tuple-element.18), channel_id=1, source_target_pairs={{0,8},{8,16},{16,24},{24,32},{32,40},{40,48},{48,56},{56,64},{64,7... | collective-permute-start | bytes 393224 | tf_op jit(solution)/shard_map/ppermute | solution.py:184
  152.1 7.0 %collective-permute-start.6 = (bf16[512,128]{1,0:T(8,128)(2,1)S(1)}, bf16[512,128]{1,0:T(8,128)(2,1)S(1)}, u32[]{:S(2)}, u32[]{:S(2)}) collective-permute-start(bf16[512,128]{1,0:T(8,128)(2,1)S(1)} %get-tuple-element.19), channel_id=1, source_target_pairs={{8,0},{16,8},{24,16},{32,24},{40,32},{48,40},{56,48},{64,56},{72,6... | collective-permute-start | bytes 393224 | tf_op jit(solution)/shard_map/ppermute | solution.py:183

commit v2 on v1

v2 whole, which is shorter than its diff:
```python
import jax
import jax.numpy as jnp
from jax import lax
from jax.experimental import pallas as pl
from jax.experimental.pallas import tpu as pltpu
from jax.sharding import Mesh, PartitionSpec as P

DH = 128
BLK = 128
GLOBAL = 2
RAND = 3
NEG = -1e30
F32 = jnp.float32
BF16 = jnp.bfloat16
SEQ_AXES = ("y", "z")
VMEM_LIMIT = 48 * 1024 * 1024


def dot(a, b, ca, cb):
    return lax.dot_general(a, b, (((ca,), (cb,)), ((), ())), preferred_element_type=F32)


def attention_kernel(nblk, heads, slot_ref, idx_ref, bias_ref, q_ref, do_ref, k_ref, v_ref, left_ref,
                     right_ref, glob_ref, *rest):
    part_refs = rest[:RAND]
    ctx_ref, dq_ref, own_ref, gleft_ref, gright_ref, gglob_ref, stat_ref = rest[RAND:RAND + 7]
    kwin, vwin, ksel, vsel, acc_win, acc_glob = rest[RAND + 7:]
    width = heads * DH
    tokens = nblk * BLK
    nwin = GLOBAL + 3
    scale = 1.0 / DH**0.5

    kwin[:BLK] = left_ref[:, :width]
    vwin[:BLK] = left_ref[:, width:]
    kwin[BLK:BLK + tokens] = k_ref[...]
    vwin[BLK:BLK + tokens] = v_ref[...]
    kwin[BLK + tokens:] = right_ref[:, :width]
    vwin[BLK + tokens:] = right_ref[:, width:]
    for h in range(heads):
        hs = slice(h * DH, (h + 1) * DH)
        ksel[:GLOBAL * BLK, hs] = glob_ref[h]
        vsel[:GLOBAL * BLK, hs] = glob_ref[heads + h]
    acc_win[...] = jnp.zeros_like(acc_win)
    acc_glob[...] = jnp.zeros_like(acc_glob)
    lane = lax.broadcasted_iota(jnp.int32, (BLK, BLK), 1)

    def step(b, carry):
        start = pl.multiple_of(b * BLK, BLK)
        rows = pl.ds(start, BLK)
        ksel[GLOBAL * BLK:nwin * BLK] = kwin[pl.ds(start, 3 * BLK)]
        vsel[GLOBAL * BLK:nwin * BLK] = vwin[pl.ds(start, 3 * BLK)]
        for r in range(RAND):
            src = pl.ds(pl.multiple_of(idx_ref[b * RAND + r] * BLK, BLK), BLK)
            dst = slice((nwin + r) * BLK, (nwin + r + 1) * BLK)
            ksel[dst] = part_refs[r][0, src, :width]
            vsel[dst] = part_refs[r][0, src, width:]
        bias = bias_ref[b]
        stats = jnp.zeros((BLK, BLK), F32)
        for h in range(heads):
            hs = slice(h * DH, (h + 1) * DH)
            query = q_ref[rows, hs]
            dout = do_ref[rows, hs]
            keys = ksel[:, hs]
            vals = vsel[:, hs]
            scores = dot(query, keys, 1, 1) * scale + bias
            dprobs = dot(dout, vals, 1, 1)
            top = jnp.max(scores, axis=-1, keepdims=True)
            expo = jnp.exp(scores - top)
            inv = 1.0 / jnp.sum(expo, axis=-1, keepdims=True)
            probs = expo * inv
            probs_b = probs.astype(BF16)
            delta = jnp.sum(probs * dprobs, axis=-1, keepdims=True)
            dscores = (probs * (dprobs - delta) * scale).astype(BF16)
            ctx_ref[rows, hs] = dot(probs_b, vals, 1, 0).astype(BF16)
            dq_ref[rows, hs] = dot(dscores, keys, 1, 0).astype(BF16)
            kterm = dot(query.T, dscores[:, :nwin * BLK], 1, 0)
            vterm = dot(dout.T, probs_b[:, :nwin * BLK], 1, 0)
            for base, term in ((h * DH, kterm), (width + h * DH, vterm)):
                at = slice(base, base + DH)
                for g in range(GLOBAL):
                    acc_glob[g, at] += term[:, g * BLK:(g + 1) * BLK]
                for w in range(3):
                    o = GLOBAL + w
                    acc_win[b + w, at] += term[:, o * BLK:(o + 1) * BLK]
            for n, stat in enumerate((top, inv, delta)):
                stats = jnp.where(lane == 3 * h + n, stat, stats)
        stat_ref[:, rows] = stats.T[:8]
        return carry

    lax.fori_loop(0, nblk, step, 0)
    gleft_ref[...] = acc_win[0].astype(BF16)
    gright_ref[...] = acc_win[nblk + 1].astype(BF16)
    own_ref[...] = acc_win[1:nblk + 1]
    gglob_ref[...] = acc_glob[...].astype(BF16)


def owner_kernel(nblk, heads, slot_ref, idx_ref, live_ref, k_ref, v_ref, *rest):
    stat_refs = rest[:RAND]
    part_refs = rest[RAND:2 * RAND]
    acc_ref, = rest[2 * RAND:]
    width = heads * DH
    scale = 1.0 / DH**0.5
    acc_ref[...] = jnp.zeros_like(acc_ref)

    def step(b, carry):
        rows = pl.ds(pl.multiple_of(b * BLK, BLK), BLK)
        for r in range(RAND):
            home = pl.ds(pl.multiple_of(idx_ref[b * RAND + r] * BLK, BLK), BLK)
            bias = jnp.where(live_ref[b * RAND + r] > 0, 0.0, NEG)
            for h in range(heads):
                hs = slice(h * DH, (h + 1) * DH)
                vs = slice(width + h * DH, width + (h + 1) * DH)
                query = part_refs[r][0, rows, hs]
                dout = part_refs[r][0, rows, vs]
                top, inv, delta = (stat_refs[r][3 * h + n:3 * h + n + 1, rows] for n in range(3))
                scores = dot(k_ref[home, hs], query, 1, 1) * scale + bias
                probs = jnp.exp(scores - top) * inv
                dprobs = dot(v_ref[home, hs], dout, 1, 1)
                dscores = (probs * (dprobs - delta) * scale).astype(BF16)
                acc_ref[home, hs] += dot(dscores, query, 1, 0)
                acc_ref[home, vs] += dot(probs.astype(BF16), dout, 1, 0)
        return carry

    lax.fori_loop(0, nblk, step, 0)


def finish_kernel(nblk, heads, first_ref, own_ref, part_ref, low_ref, high_ref, glob_ref, gk_ref, gv_ref):
    first = first_ref[0].astype(F32)
    for b in range(nblk):
        rows = slice(b * BLK, (b + 1) * BLK)
        for c in range(2 * heads):
            at = slice(c * DH, (c + 1) * DH)
            total = own_ref[b, at]
            if b == 0:
                total = total + low_ref[at].astype(F32)
            if b == nblk - 1:
                total = total + high_ref[at].astype(F32)
            if b < GLOBAL:
                total = jnp.where(first > 0, glob_ref[b, at].astype(F32), total)
            out = gk_ref if c < heads else gv_ref
            h = c % heads
            out[rows, h * DH:(h + 1) * DH] = (total.T + part_ref[rows, at]).astype(BF16)


def whole(shape):
    return pl.BlockSpec(shape, lambda i, *s: (0,) * len(shape))


def slot(shape, r):
    return pl.BlockSpec((1,) + shape, lambda i, s, *t: (s[r], 0, 0))


def exchange(x, axis):
    return lax.all_to_all(x, axis, 0, 0, tiled=True)


def spread(piece, count):
    return jnp.broadcast_to(piece[None], (count,) + piece.shape)


def total(pieces):
    return jnp.sum(pieces.astype(F32), axis=0).astype(BF16)


def shards(queries, keys, values, grad_out, rand_blocks):
    ny, nz = lax.axis_size("y"), lax.axis_size("z")
    n_seq = ny * nz
    at_y, at_z = lax.axis_index("y"), lax.axis_index("z")
    myself = at_y * nz + at_z
    tokens, width = queries.shape
    nblk = tokens // BLK
    heads = width // DH
    nwin = GLOBAL + 3
    nkeys = (nwin + RAND) * BLK
    up = [(i, i + 1) for i in range(n_seq - 1)]
    down = [(j, i) for i, j in up]
    masks = [ny >> (r + 1) for r in range(RAND)]
    sds = jax.ShapeDtypeStruct
    params = pltpu.CompilerParams(vmem_limit_bytes=VMEM_LIMIT)

    kv = jnp.concatenate([keys, values], axis=1)
    qd = jnp.concatenate([queries, grad_out], axis=1)
    all_kv = lax.all_gather(kv, "y")
    left = lax.ppermute(kv[tokens - BLK:], SEQ_AXES, up)
    right = lax.ppermute(kv[:BLK], SEQ_AXES, down)

    cols = 2 * heads
    grows = GLOBAL * BLK
    glob = kv[:grows].reshape(grows, cols, DH).transpose(1, 0, 2).reshape(nz, -1, DH)
    piece = exchange(glob, "z")[0]
    piece = exchange(spread(piece, ny), "y")[0]
    glob = exchange(spread(piece, nz), "z").reshape(cols, grows, DH)

    slots = jnp.stack([at_y ^ m for m in masks]).astype(jnp.int32)
    mine = lax.dynamic_slice_in_dim(rand_blocks, myself * nblk, nblk, 0)
    picks = (mine % nblk).reshape(-1)
    qblock = myself * nblk + jnp.arange(nblk, dtype=jnp.int32)
    window = qblock[:, None] + jnp.arange(-1, 2, dtype=jnp.int32)[None, :]
    live = jnp.concatenate(
        [jnp.ones((nblk, GLOBAL), bool), (window >= GLOBAL) & (window < nblk * n_seq), mine >= GLOBAL], axis=1)
    bias = jnp.repeat(jnp.where(live, 0.0, NEG).astype(F32), BLK, axis=1)[:, None, :]
    theirs = jnp.stack(
        [lax.dynamic_slice(rand_blocks, (((at_y ^ m) * nz + at_z) * nblk, r), (nblk, 1))[:, 0]
         for r, m in enumerate(masks)], axis=1)
    homes = (theirs % nblk).reshape(-1)
    alive = (theirs >= GLOBAL).astype(jnp.int32).reshape(-1)

    tw = (tokens, width)
    pair = (tokens, 2 * width)
    context, grad_q, own, gleft, gright, gglob, stats = pl.pallas_call(
        lambda *refs: attention_kernel(nblk, heads, *refs),
        out_shape=[
            sds(tw, BF16), sds(tw, BF16), sds((nblk, 2 * width, BLK), F32), sds((2 * width, BLK), BF16),
            sds((2 * width, BLK), BF16), sds((GLOBAL, 2 * width, BLK), BF16), sds((8, tokens), F32),
        ],
        grid_spec=pltpu.PrefetchScalarGridSpec(
            num_scalar_prefetch=2,
            grid=(1,),
            in_specs=[whole((nblk, 1, nkeys))] + [whole(tw)] * 4 + [whole((BLK, 2 * width))] * 2
            + [whole((cols, grows, DH))] + [slot(pair, r) for r in range(RAND)],
            out_specs=[whole(tw), whole(tw), whole((nblk, 2 * width, BLK)), whole((2 * width, BLK)),
                       whole((2 * width, BLK)), whole((GLOBAL, 2 * width, BLK)), whole((8, tokens))],
            scratch_shapes=[
                pltpu.VMEM((tokens + 2 * BLK, width), BF16), pltpu.VMEM((tokens + 2 * BLK, width), BF16),
                pltpu.VMEM((nkeys, width), BF16), pltpu.VMEM((nkeys, width), BF16),
                pltpu.VMEM((nblk + 2, 2 * width, BLK), F32), pltpu.VMEM((GLOBAL, 2 * width, BLK), F32),
            ],
        ),
        compiler_params=params,
        name="attention",
    )(slots, picks, bias, queries, grad_out, keys, values, left, right, glob, *([all_kv] * RAND))

    all_qd = lax.all_gather(qd, "y")
    pieces = total(exchange(gglob.reshape(nz, -1, DH), "z"))
    high = lax.ppermute(gleft, SEQ_AXES, down)
    low = lax.ppermute(gright, SEQ_AXES, up)
    their_stats = [lax.ppermute(stats, "y", [(i, i ^ m) for i in range(ny)]) for m in masks]
    pieces = total(exchange(spread(pieces, ny), "y"))
    gsum = exchange(spread(pieces, nz), "z").reshape(GLOBAL, 2 * width, BLK)

    part = pl.pallas_call(
        lambda *refs: owner_kernel(nblk, heads, *refs),
        out_shape=sds(pair, F32),
        grid_spec=pltpu.PrefetchScalarGridSpec(
            num_scalar_prefetch=3,
            grid=(1,),
            in_specs=[whole(tw)] * 2 + [whole((8, tokens))] * RAND + [slot(pair, r) for r in range(RAND)],
            out_specs=whole(pair),
        ),
        compiler_params=params,
        name="owner",
    )(slots, homes, alive, keys, values, *their_stats, *([all_qd] * RAND))

    first = (myself == 0).astype(jnp.int32).reshape(1)
    smem = pl.BlockSpec(memory_space=pltpu.SMEM)
    vmem = pl.BlockSpec(memory_space=pltpu.VMEM)
    grad_k, grad_v = pl.pallas_call(
        lambda *refs: finish_kernel(nblk, heads, *refs),
        out_shape=[sds(tw, BF16), sds(tw, BF16)],
        in_specs=[smem] + [vmem] * 5,
        out_specs=[vmem] * 2,
        compiler_params=params,
        name="finish",
    )(first, own, part, low, high, gsum)
    return context, grad_q, grad_k, grad_v


def solution(mesh):
    grid = Mesh(mesh.devices.reshape(8, 8, 8), ("y", "z", "head"))
    specs = (P(SEQ_AXES, "head"),) * 4
    return jax.shard_map(shards, mesh=grid, in_specs=specs + (P(),), out_specs=specs, check_vma=False)
```

time: 174 us -> 164 us (0.943)
  the two profiles are of different devices: /device:TPU:6 before, /device:TPU:56 now
where the time goes in v2:
time: 164 us; the launch traced here: 163 us
  starting transfers between devices  48.4 us (30%)
  blocking collectives  41.3 us (25%)
  waiting for transfers between devices  30.9 us (19%)
  Pallas kernels  15.4 us (9%)
  between operations  14.3 us (9%)
  local copies, waits for them, and re-layouts  10.5 us (6%)
  other arithmetic  2.36 us (1%)
    all_to_all x2, blocking collectives, exchange(): return lax.all_to_all(x, axis, 0, 0, tiled=True)  41.3 us
    all_to_all x4, waiting for transfers between devices, exchange(): return lax.all_to_all(x, axis, 0, 0, tiled=True)  23.9 us
    all_to_all x4, starting transfers between devices, exchange(): return lax.all_to_all(x, axis, 0, 0, tiled=True)  20 us
    ppermute x3, starting transfers between devices, shards(): lax.ppermute(stats, 'y', [(i, i ^ m) for i in range(ny)])  12.5 us
    pallas_call x1, Pallas kernels, shards(): pl.pallas_call(lambda *refs: attention_kernel(nblk, heads, *refs), out_sh...  8.86 us
    all_gather x1, waiting for transfers between devices, shards(): all_kv = lax.all_gather(kv, 'y')  6.92 us
    ppermute x1, starting transfers between devices, shards(): right = lax.ppermute(kv[:BLK], SEQ_AXES, down)  5.48 us
    pallas_call x1, Pallas kernels, shards(): pl.pallas_call(lambda *refs: owner_kernel(nblk, heads, *refs), out_shape=...  5.4 us
  transfers between devices with their start and end apart: 13, of which 4 were waited for; matrix products, arithmetic and copies ran while one was open for 5% of the time, Pallas kernels for 9%

profile of v2, /device:TPU:56, one launch (start us, length us, event | category | flops | bytes accessed | tf_op | source)
XLA Modules:
  0.0 163.2 jit_solution(3058173668196243208)
XLA Ops:
  7.2 0.0 copy-start.1
  7.2 0.0 copy-start.2
  7.2 0.0 copy-start.3
  7.2 0.0 copy-start.4
  7.2 0.0 copy-start.6
  7.2 0.0 all-gather.5.cloned.1.call-start
  7.3 1.0 constant_dynamic-update-slice_fusion.1
  8.3 1.0 constant_dynamic-update-slice_fusion
  9.3 0.0 copy-start.5
  9.3 0.8 copy-done.5
  10.1 0.0 all-gather.5.cloned.1.call-update
  10.1 0.0 all-gather.7.cloned.1.call-start
  10.2 1.9 %pad_maximum_fusion = bf16[512,512]{1,0:T(8,128)(2,1)} fusion(bf16[512,256]{1,0:T(8,128)(2,1)} %refs_4_.2, bf16[512,256]{1,0:T(8,128)(2,1)} %refs_3_.2), kind=kLoop, calls=%fused_computation | loop fusion | flops 1048576 | bytes 1048576 | tf_op jit(solution)/shard_map/concatenate | solution.py:182
  12.1 0.0 all-gather.7.cloned.1.call-update
  12.1 1.0 copy_bitcast_fusion
  13.1 22.0 %all_to_all.30 = bf16[8,128,128]{2,1,0:T(8,128)(2,1)S(1)} all-to-all(bf16[8,128,128]{2,1,0:T(8,128)(2,1)S(1)} %bitcast.32), channel_id=1, replica_groups=mesh['y'=8,'z'=8,'head'=8] {'z'}, dimensions={0} | all-to-all | bytes 524288 | tf_op jit(solution)/shard_map/all_to_all | solution.py:154
  35.1 0.7 broadcast_in_dim.43
  35.8 6.9 %all-to-all-start.1 = ((bf16[8,128,128]{2,1,0:T(8,128)(2,1)}), bf16[8,128,128]{2,1,0:T(8,128)(2,1)S(1)}, u32[]{:S(2)}, u32[]{:S(2)}) async-start(bf16[8,128,128]{2,1,0:T(8,128)(2,1)} %broadcast_in_dim.43), calls=%async_computation.1 | async-start | bytes 524288 | tf_op jit(solution)/shard_map/all_to_all | solution.py:154
  42.7 1.0 fusion.3
  43.7 2.5 %collective-permute-start = (bf16[128,512]{1,0:T(8,128)(2,1)S(1)}, bf16[128,512]{1,0:T(8,128)(2,1)S(1)}, u32[]{:S(2)}, u32[]{:S(2)}) collective-permute-start(bf16[128,512]{1,0:T(8,128)(2,1)S(1)} %get-tuple-element.23), channel_id=1, source_target_pairs={{0,8},{8,16},{16,24},{24,32},{32,40},{40,48},{48,56},{56,64},{64,7... | collective-permute-start | bytes 393224 | tf_op jit(solution)/shard_map/ppermute | solution.py:184
  46.2 5.5 %collective-permute-start.1 = (bf16[128,512]{1,0:T(8,128)(2,1)S(1)}, bf16[128,512]{1,0:T(8,128)(2,1)S(1)}, u32[]{:S(2)}, u32[]{:S(2)}) collective-permute-start(bf16[128,512]{1,0:T(8,128)(2,1)S(1)} %get-tuple-element.22), channel_id=1, source_target_pairs={{8,0},{16,8},{24,16},{32,24},{40,32},{48,40},{56,48},{64,56},{72,6... | collective-permute-start | bytes 393224 | tf_op jit(solution)/shard_map/ppermute | solution.py:185
  51.7 2.9 %all-to-all-done.1 = bf16[8,128,128]{2,1,0:T(8,128)(2,1)S(1)} async-done(((bf16[8,128,128]{2,1,0:T(8,128)(2,1)}), bf16[8,128,128]{2,1,0:T(8,128)(2,1)S(1)}, u32[]{:S(2)}, u32[]{:S(2)}) %all-to-all-start.1) | async-done | bytes 262176 | tf_op jit(solution)/shard_map/all_to_all | solution.py:154
  54.6 0.7 broadcast_in_dim.45
  55.3 3.4 %all-to-all-start.2 = ((bf16[8,128,128]{2,1,0:T(8,128)(2,1)}), bf16[8,128,128]{2,1,0:T(8,128)(2,1)S(1)}, u32[]{:S(2)}, u32[]{:S(2)}) async-start(bf16[8,128,128]{2,1,0:T(8,128)(2,1)} %broadcast_in_dim.45), calls=%async_computation.2 | async-start | bytes 524288 | tf_op jit(solution)/shard_map/all_to_all | solution.py:154
  58.8 0.0 copy-done.6
  58.8 0.1 fusion.1
  58.9 0.1 add_select_fusion
  58.9 0.1 add_select_fusion.1
  59.0 0.1 copy.17
  59.1 0.1 copy.16
  59.2 0.1 reshape.45.refs_1_
  59.3 0.1 pad_add_fusion.1.refs_0_
  59.4 0.0 collective-permute-done.refs_7_
  59.4 0.0 collective-permute-done.1.refs_8_
  59.4 9.8 %all-to-all-done.2 = bf16[8,128,128]{2,1,0:T(8,128)(2,1)S(1)} async-done(((bf16[8,128,128]{2,1,0:T(8,128)(2,1)}), bf16[8,128,128]{2,1,0:T(8,128)(2,1)S(1)}, u32[]{:S(2)}, u32[]{:S(2)}) %all-to-all-start.2) | async-done | bytes 262176 | tf_op jit(solution)/shard_map/all_to_all | solution.py:154
  69.1 6.9 %all-gather.5.cloned.1.call-done = bf16[4096,512]{1,0:T(8,128)(2,1)} async-done(((bf16[512,512]{1,0:T(8,128)(2,1)}), bf16[4096,512]{1,0:T(8,128)(2,1)}) %all-gather.5.cloned.1.call-update) | async-done | bytes 4194320 | tf_op jit(solution)/shard_map/all_gather | solution.py:183
  76.1 0.1 broadcast_in_dim.41
  76.1 0.0 copy-done.1
  76.1 0.0 copy-done.3
  76.1 8.9 %attention.1 = (bf16[512,256]{1,0:T(8,128)(2,1)}, bf16[512,256]{1,0:T(8,128)(2,1)}, f32[4,512,128]{2,1,0:T(8,128)S(1)}, bf16[512,128]{1,0:T(8,128)(2,1)S(1)}, bf...) custom-call(s32[3]{0:T(128)S(1)} %pad_add_fusion.1.refs_0_, ...), custom_call_target="tpu_custom_call" | custom-call | tf_op jit(solution)/shard_map/attention/pallas_call | solution.py:210
  85.0 19.3 %all_to_all.31 = bf16[8,128,128]{2,1,0:T(8,128)(2,1)S(1)} all-to-all(bf16[8,128,128]{2,1,0:T(8,128)(2,1)S(1)} %bitcast.27), channel_id=1, replica_groups=mesh['y'=8,'z'=8,'head'=8] {'z'}, dimensions={0} | all-to-all | bytes 524288 | tf_op jit(solution)/shard_map/all_to_all | solution.py:154
  104.3 0.7 broadcast_in_dim.46
  105.1 6.3 %all-to-all-start.4 = ((bf16[8,128,128]{2,1,0:T(8,128)(2,1)}), bf16[8,128,128]{2,1,0:T(8,128)(2,1)S(1)}, u32[]{:S(2)}, u32[]{:S(2)}) async-start(bf16[8,128,128]{2,1,0:T(8,128)(2,1)} %broadcast_in_dim.46), calls=%async_computation.4 | async-start | bytes 524288 | tf_op jit(solution)/shard_map/all_to_all | solution.py:154
  111.3 0.1 constant_dynamic-slice_fusion
  111.4 11.3 %all-to-all-done.4 = bf16[8,128,128]{2,1,0:T(8,128)(2,1)S(1)} async-done(((bf16[8,128,128]{2,1,0:T(8,128)(2,1)}), bf16[8,128,128]{2,1,0:T(8,128)(2,1)S(1)}, u32[]{:S(2)}, u32[]{:S(2)}) %all-to-all-start.4) | async-done | bytes 262176 | tf_op jit(solution)/shard_map/all_to_all | solution.py:154
  122.7 0.7 broadcast_in_dim.47
  123.5 3.4 %all-to-all-start.5 = ((bf16[8,128,128]{2,1,0:T(8,128)(2,1)}), bf16[8,128,128]{2,1,0:T(8,128)(2,1)S(1)}, u32[]{:S(2)}, u32[]{:S(2)}) async-start(bf16[8,128,128]{2,1,0:T(8,128)(2,1)} %broadcast_in_dim.47), calls=%async_computation.5 | async-start | bytes 524288 | tf_op jit(solution)/shard_map/all_to_all | solution.py:154
  126.9 0.1 copy.19
  127.0 0.1 stack.22
  127.1 4.8 %collective-permute-start.2 = (f32[8,512]{1,0:T(8,128)S(1)}, f32[8,512]{1,0:T(8,128)S(1)}, u32[]{:S(2)}, u32[]{:S(2)}) collective-permute-start(f32[8,512]{1,0:T(8,128)S(1)} %get-tuple-element.16), channel_id=1, source_target_pairs={{0,256},{64,320},{128,384},{192,448},{256,0},{320,64},{384,128},{4... | collective-permute-start | bytes 49160 | tf_op jit(solution)/shard_map/ppermute | solution.py:237
  131.9 4.6 %collective-permute-start.3 = (f32[8,512]{1,0:T(8,128)S(1)}, f32[8,512]{1,0:T(8,128)S(1)}, u32[]{:S(2)}, u32[]{:S(2)}) collective-permute-start(f32[8,512]{1,0:T(8,128)S(1)} %get-tuple-element.16), channel_id=1, source_target_pairs={{0,128},{64,192},{128,0},{192,64},{256,384},{320,448},{384,256},{4... | collective-permute-start | bytes 49160 | tf_op jit(solution)/shard_map/ppermute | solution.py:237
  136.6 3.1 %collective-permute-start.4 = (f32[8,512]{1,0:T(8,128)S(1)}, f32[8,512]{1,0:T(8,128)S(1)}, u32[]{:S(2)}, u32[]{:S(2)}) collective-permute-start(f32[8,512]{1,0:T(8,128)S(1)} %get-tuple-element.16), channel_id=1, source_target_pairs={{0,64},{64,0},{128,192},{192,128},{256,320},{320,256},{384,448},{4... | collective-permute-start | bytes 49160 | tf_op jit(solution)/shard_map/ppermute | solution.py:237
  139.6 3.8 %collective-permute-start.5 = (bf16[512,128]{1,0:T(8,128)(2,1)S(1)}, bf16[512,128]{1,0:T(8,128)(2,1)S(1)}, u32[]{:S(2)}, u32[]{:S(2)}) collective-permute-start(bf16[512,128]{1,0:T(8,128)(2,1)S(1)} %get-tuple-element.17), channel_id=1, source_target_pairs={{0,8},{8,16},{16,24},{24,32},{32,40},{40,48},{48,56},{56,64},{64,7... | collective-permute-start | bytes 393224 | tf_op jit(solution)/shard_map/ppermute | solution.py:236
  143.4 4.1 %collective-permute-start.6 = (bf16[512,128]{1,0:T(8,128)(2,1)S(1)}, bf16[512,128]{1,0:T(8,128)(2,1)S(1)}, u32[]{:S(2)}, u32[]{:S(2)}) collective-permute-start(bf16[512,128]{1,0:T(8,128)(2,1)S(1)} %get-tuple-element.18), channel_id=1, source_target_pairs={{8,0},{16,8},{24,16},{32,24},{40,32},{48,40},{56,48},{64,56},{72,6... | collective-permute-start | bytes 393224 | tf_op jit(solution)/shard_map/ppermute | solution.py:235
  147.6 0.0 all-gather.7.cloned.1.call-done
  147.6 0.0 collective-permute-done.2.refs_5_
  147.6 0.0 collective-permute-done.3.refs_6_
  147.7 0.0 collective-permute-done.4.refs_7_
  147.7 2.2 %copy-done = bf16[4096,512]{1,0:T(8,128)(2,1)S(1)} copy-done((bf16[4096,512]{1,0:T(8,128)(2,1)S(1)}, bf16[4096,512]{1,0:T(8,128)(2,1)}, u32[]{:S(2)}) %copy-start) | copy-done | bytes 4194328
  149.8 5.4 %owner.1.refs_2_ = f32[512,512]{1,0:T(8,128)S(1)} custom-call(s32[3]{0:T(128)S(1)} %pad_add_fusion.1.refs_0_, s32[12]{0:T(128)S(1)} %and_select_fusion.refs_1_, s32[12]{0:T(128)S(1)} %compare_convert_fusion.refs_2_, bf16[512,256]{1,0:T(8,128)(2,1)S(1)} %copy-done.1, bf16[512,256]{1,0:T(8,128)(2,1)S(1)} %copy-done.2, ...), custom_call_target="tpu_custom_call" | custom-call | tf_op jit(solution)/shard_map/owner/pallas_call | solution.py:241
  155.2 0.0 collective-permute-done.5.refs_3_
  155.3 0.0 collective-permute-done.6.refs_4_
  155.3 0.0 all-to-all-done.5
  155.3 1.1 finish.1
  (14 shorter events, 0.1 us)
Async XLA Ops:
  7.2 69.0 %copy-start.1 = (bf16[512,256]{1,0:T(8,128)(2,1)S(1)}, bf16[512,256]{1,0:T(8,128)(2,1)}, u32[]{:S(2)}) copy-start(bf16[512,256]{1,0:T(8,128)(2,1)} %refs_3_.3) | copy-start | bytes 786436
  7.2 69.0 %copy-start.2 = (bf16[512,256]{1,0:T(8,128)(2,1)S(1)}, bf16[512,256]{1,0:T(8,128)(2,1)}, u32[]{:S(2)}) copy-start(bf16[512,256]{1,0:T(8,128)(2,1)} %refs_4_.3) | copy-start | bytes 786436
  7.2 68.9 %copy-start.3 = (bf16[512,256]{1,0:T(8,128)(2,1)S(1)}, bf16[512,256]{1,0:T(8,128)(2,1)}, u32[]{:S(2)}) copy-start(bf16[512,256]{1,0:T(8,128)(2,1)} %refs_3_.2) | copy-start | bytes 786436
  7.2 68.9 %copy-start.4 = (bf16[512,256]{1,0:T(8,128)(2,1)S(1)}, bf16[512,256]{1,0:T(8,128)(2,1)}, u32[]{:S(2)}) copy-start(bf16[512,256]{1,0:T(8,128)(2,1)} %refs_4_.2) | copy-start | bytes 786436
  7.2 51.5 %copy-start.6 = (s32[256,3]{0,1:T(4,128)S(1)}, s32[256,3]{0,1:T(4,128)}, u32[]{:S(2)}) copy-start(s32[256,3]{0,1:T(4,128)} %param.9) | copy-start | bytes 9220
  7.2 68.8 %all-gather.5.cloned.1.call-start = ((), (), s32[]{:S(2)}) async-start(), calls=%async_computation.6 | async-start | bytes 4718592 | tf_op jit(solution)/shard_map/all_gather | solution.py:183
  9.3 0.8 copy-start.5
  10.1 137.5 %all-gather.7.cloned.1.call-start = ((), (), s32[]{:S(2)}) async-start(), calls=%async_computation.7 | async-start | bytes 4718592 | tf_op jit(solution)/shard_map/all_gather | solution.py:233
  35.8 18.7 %all-to-all-start.1 = ((bf16[8,128,128]{2,1,0:T(8,128)(2,1)}), bf16[8,128,128]{2,1,0:T(8,128)(2,1)S(1)}, u32[]{:S(2)}, u32[]{:S(2)}) async-start(bf16[8,128,128]{2,1,0:T(8,128)(2,1)} %broadcast_in_dim.43), calls=%async_computation.1 | async-start | bytes 524288 | tf_op jit(solution)/shard_map/all_to_all | solution.py:154
  43.7 15.7 %collective-permute-start = (bf16[128,512]{1,0:T(8,128)(2,1)S(1)}, bf16[128,512]{1,0:T(8,128)(2,1)S(1)}, u32[]{:S(2)}, u32[]{:S(2)}) collective-permute-start(bf16[128,512]{1,0:T(8,128)(2,1)S(1)} %get-tuple-element.23), channel_id=1, source_target_pairs={{0,8},{8,16},{16,24},{24,32},{32,40},{40,48},{48,56},{56,64},{64,7... | collective-permute-start | bytes 393224 | tf_op jit(solution)/shard_map/ppermute | solution.py:184
  46.2 13.2 %collective-permute-start.1 = (bf16[128,512]{1,0:T(8,128)(2,1)S(1)}, bf16[128,512]{1,0:T(8,128)(2,1)S(1)}, u32[]{:S(2)}, u32[]{:S(2)}) collective-permute-start(bf16[128,512]{1,0:T(8,128)(2,1)S(1)} %get-tuple-element.22), channel_id=1, source_target_pairs={{8,0},{16,8},{24,16},{32,24},{40,32},{48,40},{56,48},{64,56},{72,6... | collective-permute-start | bytes 393224 | tf_op jit(solution)/shard_map/ppermute | solution.py:185
  55.3 13.8 %all-to-all-start.2 = ((bf16[8,128,128]{2,1,0:T(8,128)(2,1)}), bf16[8,128,128]{2,1,0:T(8,128)(2,1)S(1)}, u32[]{:S(2)}, u32[]{:S(2)}) async-start(bf16[8,128,128]{2,1,0:T(8,128)(2,1)} %broadcast_in_dim.45), calls=%async_computation.2 | async-start | bytes 524288 | tf_op jit(solution)/shard_map/all_to_all | solution.py:154
  105.1 17.6 %all-to-all-start.4 = ((bf16[8,128,128]{2,1,0:T(8,128)(2,1)}), bf16[8,128,128]{2,1,0:T(8,128)(2,1)S(1)}, u32[]{:S(2)}, u32[]{:S(2)}) async-start(bf16[8,128,128]{2,1,0:T(8,128)(2,1)} %broadcast_in_dim.46), calls=%async_computation.4 | async-start | bytes 524288 | tf_op jit(solution)/shard_map/all_to_all | solution.py:154
  123.5 31.8 %all-to-all-start.5 = ((bf16[8,128,128]{2,1,0:T(8,128)(2,1)}), bf16[8,128,128]{2,1,0:T(8,128)(2,1)S(1)}, u32[]{:S(2)}, u32[]{:S(2)}) async-start(bf16[8,128,128]{2,1,0:T(8,128)(2,1)} %broadcast_in_dim.47), calls=%async_computation.5 | async-start | bytes 524288 | tf_op jit(solution)/shard_map/all_to_all | solution.py:154
  127.1 20.5 %collective-permute-start.2 = (f32[8,512]{1,0:T(8,128)S(1)}, f32[8,512]{1,0:T(8,128)S(1)}, u32[]{:S(2)}, u32[]{:S(2)}) collective-permute-start(f32[8,512]{1,0:T(8,128)S(1)} %get-tuple-element.16), channel_id=1, source_target_pairs={{0,256},{64,320},{128,384},{192,448},{256,0},{320,64},{384,128},{4... | collective-permute-start | bytes 49160 | tf_op jit(solution)/shard_map/ppermute | solution.py:237
  131.9 15.7 %collective-permute-start.3 = (f32[8,512]{1,0:T(8,128)S(1)}, f32[8,512]{1,0:T(8,128)S(1)}, u32[]{:S(2)}, u32[]{:S(2)}) collective-permute-start(f32[8,512]{1,0:T(8,128)S(1)} %get-tuple-element.16), channel_id=1, source_target_pairs={{0,128},{64,192},{128,0},{192,64},{256,384},{320,448},{384,256},{4... | collective-permute-start | bytes 49160 | tf_op jit(solution)/shard_map/ppermute | solution.py:237
  136.6 11.1 %collective-permute-start.4 = (f32[8,512]{1,0:T(8,128)S(1)}, f32[8,512]{1,0:T(8,128)S(1)}, u32[]{:S(2)}, u32[]{:S(2)}) collective-permute-start(f32[8,512]{1,0:T(8,128)S(1)} %get-tuple-element.16), channel_id=1, source_target_pairs={{0,64},{64,0},{128,192},{192,128},{256,320},{320,256},{384,448},{4... | collective-permute-start | bytes 49160 | tf_op jit(solution)/shard_map/ppermute | solution.py:237
  139.6 15.6 %collective-permute-start.5 = (bf16[512,128]{1,0:T(8,128)(2,1)S(1)}, bf16[512,128]{1,0:T(8,128)(2,1)S(1)}, u32[]{:S(2)}, u32[]{:S(2)}) collective-permute-start(bf16[512,128]{1,0:T(8,128)(2,1)S(1)} %get-tuple-element.17), channel_id=1, source_target_pairs={{0,8},{8,16},{16,24},{24,32},{32,40},{40,48},{48,56},{56,64},{64,7... | collective-permute-start | bytes 393224 | tf_op jit(solution)/shard_map/ppermute | solution.py:236
  143.4 11.8 %collective-permute-start.6 = (bf16[512,128]{1,0:T(8,128)(2,1)S(1)}, bf16[512,128]{1,0:T(8,128)(2,1)S(1)}, u32[]{:S(2)}, u32[]{:S(2)}) collective-permute-start(bf16[512,128]{1,0:T(8,128)(2,1)S(1)} %get-tuple-element.18), channel_id=1, source_target_pairs={{8,0},{16,8},{24,16},{32,24},{40,32},{48,40},{56,48},{64,56},{72,6... | collective-permute-start | bytes 393224 | tf_op jit(solution)/shard_map/ppermute | solution.py:235
  147.7 2.2 %copy-start = (bf16[4096,512]{1,0:T(8,128)(2,1)S(1)}, bf16[4096,512]{1,0:T(8,128)(2,1)}, u32[]{:S(2)}) copy-start(bf16[4096,512]{1,0:T(8,128)(2,1)} %all-gather.7.cloned.1.call-done) | copy-start | bytes 12582916
Sparse Core Ops, SparseCore 0:
  10.2 65.7 all-gather.4
  78.1 63.2 all-gather.6

commit v3 on v1

--- a/solution.py
+++ b/solution.py
@@ -3,7 +3,7 @@
 from jax import lax
 from jax.experimental import pallas as pl
 from jax.experimental.pallas import tpu as pltpu
-from jax.sharding import PartitionSpec as P
+from jax.sharding import Mesh, PartitionSpec as P
 
 DH = 128
 BLK = 128
@@ -12,6 +12,8 @@
 NEG = -1e30
 F32 = jnp.float32
 BF16 = jnp.bfloat16
+SEQ_AXES = ("y", "z")
+VMEM_LIMIT = 48 * 1024 * 1024
 
 
 def dot(a, b, ca, cb):
@@ -35,10 +37,8 @@
     vwin[BLK:BLK + tokens] = v_ref[...]
     kwin[BLK + tokens:] = right_ref[:, :width]
     vwin[BLK + tokens:] = right_ref[:, width:]
-    for h in range(heads):
-        hs = slice(h * DH, (h + 1) * DH)
-        ksel[:GLOBAL * BLK, hs] = glob_ref[h]
-        vsel[:GLOBAL * BLK, hs] = glob_ref[heads + h]
+    ksel[:GLOBAL * BLK] = glob_ref[:, :width]
+    vsel[:GLOBAL * BLK] = glob_ref[:, width:]
     acc_win[...] = jnp.zeros_like(acc_win)
     acc_glob[...] = jnp.zeros_like(acc_glob)
     acc_part[...] = jnp.zeros_like(acc_part)
@@ -119,32 +119,51 @@
             out[rows, h * DH:(h + 1) * DH] = total.T.astype(BF16)
 
 
+def exchange(x, axis):
+    return lax.all_to_all(x, axis, 0, 0, tiled=True)
+
+
+def spread(piece, count):
+    return jnp.broadcast_to(piece[None], (count,) + piece.shape)
+
+
+def total(pieces):
+    return jnp.sum(pieces.astype(F32), axis=0).astype(BF16)
+
+
+def tie(*values):
+    return lax.optimization_barrier(values)
+
+
 def shards(queries, keys, values, grad_out, rand_blocks):
-    n_seq = lax.axis_size("seq")
-    myself = lax.axis_index("seq")
+    ny, nz = lax.axis_size("y"), lax.axis_size("z")
+    n_seq = ny * nz
+    myself = lax.axis_index("y") * nz + lax.axis_index("z")
     tokens, width = queries.shape
     nblk = tokens // BLK
     heads = width // DH
     nwin = GLOBAL + 3
+    nkeys = (nwin + RAND) * BLK
     up = [(i, i + 1) for i in range(n_seq - 1)]
     down = [(j, i) for i, j in up]
-    masks = [n_seq >> (r + 1) for r in range(RAND)]
+    masks = [ny >> (r + 1) for r in range(RAND)]
+    sds = jax.ShapeDtypeStruct
+    params = pltpu.CompilerParams(vmem_limit_bytes=VMEM_LIMIT)
 
     def partner(x, r):
-        return lax.ppermute(x, "seq", [(i, i ^ masks[r]) for i in range(n_seq)])
-
+        return lax.ppermute(x, "y", [(i, i ^ masks[r]) for i in range(ny)])
+
+    grows = GLOBAL * BLK
+    glob = jnp.concatenate([keys[:grows], values[:grows]], axis=1)
+    piece = exchange(glob.reshape(nz, grows // nz, 2 * width), "z")[0]
     kv = jnp.concatenate([keys, values], axis=1)
-    fetched = [partner(kv, r) for r in range(RAND)]
-    left = lax.ppermute(kv[tokens - BLK:], "seq", up)
-    right = lax.ppermute(kv[:BLK], "seq", down)
-
-    cols = 2 * heads
-    grows = GLOBAL * BLK
-    unit = cols * grows // n_seq
-    glob = kv[:grows].reshape(grows, cols, DH).transpose(1, 0, 2).reshape(n_seq, unit, DH)
-    piece = lax.all_to_all(glob, "seq", 0, 0, tiled=True)[0]
-    glob = lax.all_to_all(jnp.broadcast_to(piece[None], (n_seq, unit, DH)), "seq", 0, 0, tiled=True)
-    glob = glob.reshape(cols, grows, DH)
+    left = lax.ppermute(kv[tokens - BLK:], SEQ_AXES, up)
+    right = lax.ppermute(kv[:BLK], SEQ_AXES, down)
+    far = partner(kv, 0)
+    kv, piece = tie(kv, piece)
+    fetched = [far] + [partner(kv, r) for r in range(1, RAND)]
+    piece = exchange(spread(piece, ny), "y")[0]
+    glob = exchange(spread(piece, nz), "z").reshape(grows, 2 * width)
 
     mine = lax.dynamic_slice_in_dim(rand_blocks, myself * nblk, nblk, 0)
     picks = (mine % nblk).reshape(-1)
@@ -156,8 +175,6 @@
 
     smem = pl.BlockSpec(memory_space=pltpu.SMEM)
     vmem = pl.BlockSpec(memory_space=pltpu.VMEM)
-    sds = jax.ShapeDtypeStruct
-    nkeys = (nwin + RAND) * BLK
     outs = pl.pallas_call(
         lambda *refs: attention_kernel(nblk, heads, *refs),
         out_shape=[
@@ -173,32 +190,34 @@
             pltpu.VMEM((nblk + 2, 2 * width, BLK), F32), pltpu.VMEM((GLOBAL, 2 * width, BLK), F32),
             pltpu.VMEM((RAND, nblk, 2 * width, BLK), F32),
         ],
-        compiler_params=pltpu.CompilerParams(vmem_limit_bytes=48 * 1024 * 1024),
+        compiler_params=params,
         name="attention",
     )(picks, bias, queries, grad_out, keys, values, left, right, glob, *fetched)
     context, grad_q, own, gleft, gright, gglob = outs[:6]
     gparts = outs[6:]
 
-    back = [partner(gparts[r], r) for r in range(RAND)]
-    high = lax.ppermute(gleft, "seq", down)
-    low = lax.ppermute(gright, "seq", up)
-    terms = lax.all_to_all(gglob.reshape(n_seq, unit, DH), "seq", 0, 0, tiled=True)
-    summed = jnp.sum(terms.astype(F32), axis=0).astype(BF16)
-    gsum = lax.all_to_all(jnp.broadcast_to(summed[None], (n_seq, unit, DH)), "seq", 0, 0, tiled=True)
-    gsum = gsum.reshape(GLOBAL, 2 * width, BLK)
+    pieces = total(exchange(gglob.reshape(nz, -1, DH), "z"))
+    far = partner(gparts[0], 0)
+    far, gleft, gright, *gnear = tie(far, gleft, gright, *gparts[1:])
+    back = [far] + [partner(g, r + 1) for r, g in enumerate(gnear)]
+    high = lax.ppermute(gleft, SEQ_AXES, down)
+    low = lax.ppermute(gright, SEQ_AXES, up)
+    pieces = total(exchange(spread(pieces, ny), "y"))
+    gsum = exchange(spread(pieces, nz), "z").reshape(GLOBAL, 2 * width, BLK)
+
     first = (myself == 0).astype(jnp.int32).reshape(1)
-
     grad_k, grad_v = pl.pallas_call(
         lambda *refs: finish_kernel(nblk, heads, *refs),
         out_shape=[sds((tokens, width), BF16), sds((tokens, width), BF16)],
         in_specs=[smem] + [vmem] * (4 + RAND),
         out_specs=[vmem] * 2,
-        compiler_params=pltpu.CompilerParams(vmem_limit_bytes=48 * 1024 * 1024),
+        compiler_params=params,
         name="finish",
     )(first, own, low, high, gsum, *back)
     return context, grad_q, grad_k, grad_v
 
 
 def solution(mesh):
-    specs = (P("seq", "head"),) * 4
-    return jax.shard_map(shards, mesh=mesh, in_specs=specs + (P(),), out_specs=specs, check_vma=False)
+    grid = Mesh(mesh.devices.reshape(8, 8, 8), ("y", "z", "head"))
+    specs = (P(SEQ_AXES, "head"),) * 4
+    return jax.shard_map(shards, mesh=grid, in_specs=specs + (P(),), out_specs=specs, check_vma=False)

time: 174 us -> 157 us (0.902)
  waiting for transfers between devices: 53.9 us -> 41.1 us
  starting transfers between devices: 97.9 us -> 92.7 us
    all_to_all x4 -> x6, waiting for transfers between devices: 42.3 us -> 13.4 us  [exchange(): return lax.all_to_all(x, axis, 0, 0, tiled=True)]
    ppermute x10, waiting for transfers between devices: 11.5 us -> 27.7 us  [the longest x6 22.1 us: partner(): return lax.ppermute(x, 'y', [(i, i ^ masks[r]) for i in range(ny)])]
    all_to_all x4 -> x6, starting transfers between devices: 62.1 us -> 46.7 us  [exchange(): return lax.all_to_all(x, axis, 0, 0, tiled=True)]
    ppermute x10, starting transfers between devices: 35.8 us -> 46 us  [the longest x6 34.9 us: partner(): return lax.ppermute(x, 'y', [(i, i ^ masks[r]) for i in range(ny)])]
    unnamed x19 -> x17, local copies, waits for them, and re-layouts: 4.83 us -> 2.54 us
  transfers between devices with their start and end apart: 14 -> 16, of which waited for: 7 -> 8; matrix products, arithmetic and copies ran while one was open for 2% -> 4% of each run, Pallas kernels for 0% -> 0%
where the time goes in v3:
time: 157 us; the launch traced here: 154 us
  starting transfers between devices  92.7 us (59%)
  waiting for transfers between devices  41.1 us (26%)
  Pallas kernels  10.2 us (6%)
  local copies, waits for them, and re-layouts  8.53 us (5%)
    all_to_all x6, starting transfers between devices, exchange(): return lax.all_to_all(x, axis, 0, 0, tiled=True)  46.7 us
    ppermute x6, starting transfers between devices, partner(): return lax.ppermute(x, 'y', [(i, i ^ masks[r]) for i in range(ny)])  34.9 us
    ppermute x6, waiting for transfers between devices, partner(): return lax.ppermute(x, 'y', [(i, i ^ masks[r]) for i in range(ny)])  22.1 us
    all_to_all x6, waiting for transfers between devices, exchange(): return lax.all_to_all(x, axis, 0, 0, tiled=True)  13.4 us
    pallas_call x1, Pallas kernels, shards(): pl.pallas_call(lambda *refs: attention_kernel(nblk, heads, *refs), out_sh...  8.98 us
    ppermute x1, starting transfers between devices, shards(): left = lax.ppermute(kv[tokens - BLK:], SEQ_AXES, up)  4.55 us
    ppermute x1, starting transfers between devices, shards(): low = lax.ppermute(gright, SEQ_AXES, up)  3.92 us
    ppermute x1, waiting for transfers between devices, shards(): high = lax.ppermute(gleft, SEQ_AXES, down)  3.22 us
  transfers between devices with their start and end apart: 16, of which 8 were waited for; matrix products, arithmetic and copies ran while one was open for 4% of the time, Pallas kernels for 0%

profile of v3, /device:TPU:6, one launch (start us, length us, event | category | flops | bytes accessed | tf_op | source)
XLA Modules:
  0.0 154.3 jit_solution(13635081873438822351)
XLA Ops:
  0.6 0.0 slice-start
  0.6 0.0 slice-start.1
  0.7 0.9 slice-done
  1.5 0.1 slice-done.1
  1.6 0.7 pad_maximum_fusion
  2.3 10.4 %all-to-all-start = ((bf16[8,32,512]{2,1,0:T(8,128)(2,1)}), bf16[8,32,512]{2,1,0:T(8,128)(2,1)S(1)}, u32[]{:S(2)}, u32[]{:S(2)}) async-start(bf16[8,32,512]{2,1,0:T(8,128)(2,1)} %bitcast.1), calls=%async_computation | async-start | bytes 524288 | tf_op jit(solution)/shard_map/all_to_all | solution.py:123
  12.8 0.0 copy-done
  12.8 0.0 copy-start.1
  12.8 0.8 constant_dynamic-update-slice_fusion.1
  13.5 0.3 copy-done.1
  13.8 0.8 constant_dynamic-update-slice_fusion
  14.6 7.7 %collective-permute-start.2 = (bf16[512,512]{1,0:T(8,128)(2,1)}, bf16[512,512]{1,0:T(8,128)(2,1)S(1)}, u32[]{:S(2)}, u32[]{:S(2)}) collective-permute-start(bf16[512,512]{1,0:T(8,128)(2,1)} %constant_dynamic-update-slice_fusion), channel_id=1, source_target_pairs={{0,256},{64,320},{128,384},{192,448},{256,0},{320,64},{384,128},{4... | collective-permute-start | bytes 1572872 | tf_op jit(solution)/shard_map/ppermute | solution.py:154
  22.3 2.3 %all-to-all-done = bf16[8,32,512]{2,1,0:T(8,128)(2,1)S(1)} async-done(((bf16[8,32,512]{2,1,0:T(8,128)(2,1)}), bf16[8,32,512]{2,1,0:T(8,128)(2,1)S(1)}, u32[]{:S(2)}, u32[]{:S(2)}) %all-to-all-start) | async-done | bytes 262176 | tf_op jit(solution)/shard_map/all_to_all | solution.py:123
  24.7 0.7 broadcast_in_dim.41
  25.4 7.1 %all-to-all-start.1 = ((bf16[8,32,512]{2,1,0:T(8,128)(2,1)}), bf16[8,32,512]{2,1,0:T(8,128)(2,1)S(1)}, u32[]{:S(2)}, u32[]{:S(2)}) async-start(bf16[8,32,512]{2,1,0:T(8,128)(2,1)} %broadcast_in_dim.41), calls=%async_computation.1 | async-start | bytes 524288 | tf_op jit(solution)/shard_map/all_to_all | solution.py:123
  32.5 1.0 fusion.2
  33.5 1.3 collective-permute-start.1
  34.8 4.6 %collective-permute-start = (bf16[128,512]{1,0:T(8,128)(2,1)S(1)}, bf16[128,512]{1,0:T(8,128)(2,1)S(1)}, u32[]{:S(2)}, u32[]{:S(2)}) collective-permute-start(bf16[128,512]{1,0:T(8,128)(2,1)S(1)} %get-tuple-element.41), channel_id=1, source_target_pairs={{0,8},{8,16},{16,24},{24,32},{32,40},{40,48},{48,56},{56,64},{64,7... | collective-permute-start | bytes 393224 | tf_op jit(solution)/shard_map/ppermute | solution.py:160
  39.3 0.0 copy-start.7
  39.4 0.7 copy-done.7
  40.0 0.1 add_select_fusion.1
  40.1 3.9 %collective-permute-start.4 = (bf16[512,512]{1,0:T(8,128)(2,1)}, bf16[512,512]{1,0:T(8,128)(2,1)S(1)}, u32[]{:S(2)}, u32[]{:S(2)}) collective-permute-start(bf16[512,512]{1,0:T(8,128)(2,1)} %constant_dynamic-update-slice_fusion), channel_id=1, source_target_pairs={{0,64},{64,0},{128,192},{192,128},{256,320},{320,256},{384,448},{4... | collective-permute-start | bytes 1572872 | tf_op jit(solution)/shard_map/ppermute | solution.py:154
  44.0 4.3 %collective-permute-start.3 = (bf16[512,512]{1,0:T(8,128)(2,1)}, bf16[512,512]{1,0:T(8,128)(2,1)S(1)}, u32[]{:S(2)}, u32[]{:S(2)}) collective-permute-start(bf16[512,512]{1,0:T(8,128)(2,1)} %constant_dynamic-update-slice_fusion), channel_id=1, source_target_pairs={{0,128},{64,192},{128,0},{192,64},{256,384},{320,448},{384,256},{4... | collective-permute-start | bytes 1572872 | tf_op jit(solution)/shard_map/ppermute | solution.py:154
  48.3 3.3 %all-to-all-done.1 = bf16[8,32,512]{2,1,0:T(8,128)(2,1)S(1)} async-done(((bf16[8,32,512]{2,1,0:T(8,128)(2,1)}), bf16[8,32,512]{2,1,0:T(8,128)(2,1)S(1)}, u32[]{:S(2)}, u32[]{:S(2)}) %all-to-all-start.1) | async-done | bytes 262176 | tf_op jit(solution)/shard_map/all_to_all | solution.py:123
  51.6 0.7 broadcast_in_dim.43
  52.3 7.1 %all-to-all-start.2 = ((bf16[8,32,512]{2,1,0:T(8,128)(2,1)}), bf16[8,32,512]{2,1,0:T(8,128)(2,1)S(1)}, u32[]{:S(2)}, u32[]{:S(2)}) async-start(bf16[8,32,512]{2,1,0:T(8,128)(2,1)} %broadcast_in_dim.43), calls=%async_computation.2 | async-start | bytes 524288 | tf_op jit(solution)/shard_map/all_to_all | solution.py:123
  59.5 0.1 copy.11
  59.6 0.1 reshape.39.refs_0_
  59.7 0.1 fusion.1
  59.7 0.1 add_select_fusion
  59.8 0.1 copy.12
  59.9 0.0 collective-permute-done.1.refs_7_
  59.9 0.0 collective-permute-done.refs_6_
  59.9 0.0 collective-permute-done.2.refs_9_
  59.9 16.8 %collective-permute-done.4.refs_11_ = bf16[512,512]{1,0:T(8,128)(2,1)S(1)} collective-permute-done((bf16[512,512]{1,0:T(8,128)(2,1)}, bf16[512,512]{1,0:T(8,128)(2,1)S(1)}, u32[]{:S(2)}, u32[]{:S(2)}) %collective-permute-start.4) | collective-permute-done | bytes 524320 | tf_op jit(solution)/shard_map/ppermute | solution.py:154
  76.7 0.0 collective-permute-done.3.refs_10_
  76.7 0.0 all-to-all-done.2
  76.7 0.1 broadcast_in_dim.40
  76.8 0.0 copy-done.3
  76.8 0.0 copy-done.4
  76.8 9.0 %attention.1 = (bf16[512,256]{1,0:T(8,128)(2,1)}, bf16[512,256]{1,0:T(8,128)(2,1)}, f32[4,512,128]{2,1,0:T(8,128)}, bf16[512,128]{1,0:T(8,128)(2,1)S(1)}, bf16[5...) custom-call(s32[12]{0:T(128)S(1)} %reshape.39.refs_0_, ...), custom_call_target="tpu_custom_call" | custom-call | tf_op jit(solution)/shard_map/attention/pallas_call | solution.py:178
  85.8 0.8 copy-done.5
  86.6 4.2 %all-to-all-start.3 = ((bf16[8,128,128]{2,1,0:T(8,128)(2,1)}), bf16[8,128,128]{2,1,0:T(8,128)(2,1)S(1)}, u32[]{:S(2)}, u32[]{:S(2)}) async-start(bf16[8,128,128]{2,1,0:T(8,128)(2,1)} %bitcast.6), calls=%async_computation.3 | async-start | bytes 524288 | tf_op jit(solution)/shard_map/all_to_all | solution.py:123
  90.8 0.0 copy-done.6
  90.8 2.9 %collective-permute-start.5 = (bf16[4,512,128]{2,1,0:T(8,128)(2,1)S(1)}, bf16[4,512,128]{2,1,0:T(8,128)(2,1)S(1)}, u32[]{:S(2)}, u32[]{:S(2)}) collective-permute-start(bf16[4,512,128]{2,1,0:T(8,128)(2,1)S(1)} %copy-done.6), channel_id=1, source_target_pairs={{0,256},{64,320},{128,384},{192,448},{256,0},{320,64},{384,128},{4... | collective-permute-start | bytes 1572872 | tf_op jit(solution)/shard_map/ppermute | solution.py:154
  93.8 7.8 %all-to-all-done.3 = bf16[8,128,128]{2,1,0:T(8,128)(2,1)S(1)} async-done(((bf16[8,128,128]{2,1,0:T(8,128)(2,1)}), bf16[8,128,128]{2,1,0:T(8,128)(2,1)S(1)}, u32[]{:S(2)}, u32[]{:S(2)}) %all-to-all-start.3) | async-done | bytes 262176 | tf_op jit(solution)/shard_map/all_to_all | solution.py:123
  101.6 0.0 copy-start.2
  101.6 0.7 broadcast_in_dim.44
  102.3 10.4 %all-to-all-start.4 = ((bf16[8,128,128]{2,1,0:T(8,128)(2,1)}), bf16[8,128,128]{2,1,0:T(8,128)(2,1)S(1)}, u32[]{:S(2)}, u32[]{:S(2)}) async-start(bf16[8,128,128]{2,1,0:T(8,128)(2,1)} %broadcast_in_dim.44), calls=%async_computation.4 | async-start | bytes 524288 | tf_op jit(solution)/shard_map/all_to_all | solution.py:123
  112.7 0.0 collective-permute-done.5.refs_5_
  112.7 12.4 %collective-permute-start.8 = (bf16[4,512,128]{2,1,0:T(8,128)(2,1)}, bf16[4,512,128]{2,1,0:T(8,128)(2,1)S(1)}, u32[]{:S(2)}, u32[]{:S(2)}) collective-permute-start(bf16[4,512,128]{2,1,0:T(8,128)(2,1)} %get-tuple-element.36), channel_id=1, source_target_pairs={{0,128},{64,192},{128,0},{192,64},{256,384},{320,448},{384,256},{4... | collective-permute-start | bytes 1572872 | tf_op jit(solution)/shard_map/ppermute | solution.py:154
  125.1 3.8 %collective-permute-start.9 = (bf16[4,512,128]{2,1,0:T(8,128)(2,1)}, bf16[4,512,128]{2,1,0:T(8,128)(2,1)S(1)}, u32[]{:S(2)}, u32[]{:S(2)}) collective-permute-start(bf16[4,512,128]{2,1,0:T(8,128)(2,1)} %get-tuple-element.37), channel_id=1, source_target_pairs={{0,64},{64,0},{128,192},{192,128},{256,320},{320,256},{384,448},{4... | collective-permute-start | bytes 1572872 | tf_op jit(solution)/shard_map/ppermute | solution.py:154
  128.9 0.0 all-to-all-done.4
  128.9 0.7 broadcast_in_dim.45
  129.7 7.4 %all-to-all-start.5 = ((bf16[8,128,128]{2,1,0:T(8,128)(2,1)}), bf16[8,128,128]{2,1,0:T(8,128)(2,1)S(1)}, u32[]{:S(2)}, u32[]{:S(2)}) async-start(bf16[8,128,128]{2,1,0:T(8,128)(2,1)} %broadcast_in_dim.45), calls=%async_computation.5 | async-start | bytes 524288 | tf_op jit(solution)/shard_map/all_to_all | solution.py:123
  137.0 3.9 %collective-permute-start.6 = (bf16[512,128]{1,0:T(8,128)(2,1)S(1)}, bf16[512,128]{1,0:T(8,128)(2,1)S(1)}, u32[]{:S(2)}, u32[]{:S(2)}) collective-permute-start(bf16[512,128]{1,0:T(8,128)(2,1)S(1)} %get-tuple-element.32), channel_id=1, source_target_pairs={{0,8},{8,16},{16,24},{24,32},{32,40},{40,48},{48,56},{56,64},{64,7... | collective-permute-start | bytes 393224 | tf_op jit(solution)/shard_map/ppermute | solution.py:204
  141.0 1.3 collective-permute-start.7
  142.3 2.3 %collective-permute-done.6.refs_2_ = bf16[512,128]{1,0:T(8,128)(2,1)S(1)} collective-permute-done((bf16[512,128]{1,0:T(8,128)(2,1)S(1)}, bf16[512,128]{1,0:T(8,128)(2,1)S(1)}, u32[]{:S(2)}, u32[]{:S(2)}) %collective-permute-start.6) | collective-permute-done | bytes 131104 | tf_op jit(solution)/shard_map/ppermute | solution.py:204
  144.6 3.2 %collective-permute-done.7.refs_3_ = bf16[512,128]{1,0:T(8,128)(2,1)S(1)} collective-permute-done((bf16[512,128]{1,0:T(8,128)(2,1)S(1)}, bf16[512,128]{1,0:T(8,128)(2,1)S(1)}, u32[]{:S(2)}, u32[]{:S(2)}) %collective-permute-start.7) | collective-permute-done | bytes 131104 | tf_op jit(solution)/shard_map/ppermute | solution.py:203
  147.8 1.0 collective-permute-done.8.refs_6_
  148.8 4.4 %collective-permute-done.9.refs_7_ = bf16[4,512,128]{2,1,0:T(8,128)(2,1)S(1)} collective-permute-done((bf16[4,512,128]{2,1,0:T(8,128)(2,1)}, bf16[4,512,128]{2,1,0:T(8,128)(2,1)S(1)}, u32[]{:S(2)}, u32[]{:S(2)}) %collective-permute-start.9) | collective-permute-done | bytes 524320 | tf_op jit(solution)/shard_map/ppermute | solution.py:154
  153.2 0.0 all-to-all-done.5
  153.2 0.0 copy-done.2
  153.2 1.2 finish.1
  (13 shorter events, 0.1 us)
Async XLA Ops:
  0.6 0.9 slice-start
  0.6 1.0 slice-start.1
  2.3 10.5 %copy-start = (bf16[512,256]{1,0:T(8,128)(2,1)S(1)}, bf16[512,256]{1,0:T(8,128)(2,1)}, u32[]{:S(2)}) copy-start(bf16[512,256]{1,0:T(8,128)(2,1)} %refs_4_.1) | copy-start | bytes 786436
  2.3 22.3 %all-to-all-start = ((bf16[8,32,512]{2,1,0:T(8,128)(2,1)}), bf16[8,32,512]{2,1,0:T(8,128)(2,1)S(1)}, u32[]{:S(2)}, u32[]{:S(2)}) async-start(bf16[8,32,512]{2,1,0:T(8,128)(2,1)} %bitcast.1), calls=%async_computation | async-start | bytes 524288 | tf_op jit(solution)/shard_map/all_to_all | solution.py:123
  12.8 1.0 copy-start.1
  14.6 45.3 %collective-permute-start.2 = (bf16[512,512]{1,0:T(8,128)(2,1)}, bf16[512,512]{1,0:T(8,128)(2,1)S(1)}, u32[]{:S(2)}, u32[]{:S(2)}) collective-permute-start(bf16[512,512]{1,0:T(8,128)(2,1)} %constant_dynamic-update-slice_fusion), channel_id=1, source_target_pairs={{0,256},{64,320},{128,384},{192,448},{256,0},{320,64},{384,128},{4... | collective-permute-start | bytes 1572872 | tf_op jit(solution)/shard_map/ppermute | solution.py:154
  25.4 26.2 %all-to-all-start.1 = ((bf16[8,32,512]{2,1,0:T(8,128)(2,1)}), bf16[8,32,512]{2,1,0:T(8,128)(2,1)S(1)}, u32[]{:S(2)}, u32[]{:S(2)}) async-start(bf16[8,32,512]{2,1,0:T(8,128)(2,1)} %broadcast_in_dim.41), calls=%async_computation.1 | async-start | bytes 524288 | tf_op jit(solution)/shard_map/all_to_all | solution.py:123
  33.5 26.4 %collective-permute-start.1 = (bf16[128,512]{1,0:T(8,128)(2,1)S(1)}, bf16[128,512]{1,0:T(8,128)(2,1)S(1)}, u32[]{:S(2)}, u32[]{:S(2)}) collective-permute-start(bf16[128,512]{1,0:T(8,128)(2,1)S(1)} %get-tuple-element.40), channel_id=1, source_target_pairs={{8,0},{16,8},{24,16},{32,24},{40,32},{48,40},{56,48},{64,56},{72,6... | collective-permute-start | bytes 393224 | tf_op jit(solution)/shard_map/ppermute | solution.py:161
  34.8 25.1 %collective-permute-start = (bf16[128,512]{1,0:T(8,128)(2,1)S(1)}, bf16[128,512]{1,0:T(8,128)(2,1)S(1)}, u32[]{:S(2)}, u32[]{:S(2)}) collective-permute-start(bf16[128,512]{1,0:T(8,128)(2,1)S(1)} %get-tuple-element.41), channel_id=1, source_target_pairs={{0,8},{8,16},{16,24},{24,32},{32,40},{40,48},{48,56},{56,64},{64,7... | collective-permute-start | bytes 393224 | tf_op jit(solution)/shard_map/ppermute | solution.py:160
  39.3 0.7 copy-start.7
  40.1 36.6 %collective-permute-start.4 = (bf16[512,512]{1,0:T(8,128)(2,1)}, bf16[512,512]{1,0:T(8,128)(2,1)S(1)}, u32[]{:S(2)}, u32[]{:S(2)}) collective-permute-start(bf16[512,512]{1,0:T(8,128)(2,1)} %constant_dynamic-update-slice_fusion), channel_id=1, source_target_pairs={{0,64},{64,0},{128,192},{192,128},{256,320},{320,256},{384,448},{4... | collective-permute-start | bytes 1572872 | tf_op jit(solution)/shard_map/ppermute | solution.py:154
  44.0 32.7 %collective-permute-start.3 = (bf16[512,512]{1,0:T(8,128)(2,1)}, bf16[512,512]{1,0:T(8,128)(2,1)S(1)}, u32[]{:S(2)}, u32[]{:S(2)}) collective-permute-start(bf16[512,512]{1,0:T(8,128)(2,1)} %constant_dynamic-update-slice_fusion), channel_id=1, source_target_pairs={{0,128},{64,192},{128,0},{192,64},{256,384},{320,448},{384,256},{4... | collective-permute-start | bytes 1572872 | tf_op jit(solution)/shard_map/ppermute | solution.py:154
  52.3 24.5 %copy-start.3 = (bf16[512,256]{1,0:T(8,128)(2,1)S(1)}, bf16[512,256]{1,0:T(8,128)(2,1)}, u32[]{:S(2)}) copy-start(bf16[512,256]{1,0:T(8,128)(2,1)} %refs_2_.1) | copy-start | bytes 786436
  52.3 24.5 %copy-start.4 = (bf16[512,256]{1,0:T(8,128)(2,1)S(1)}, bf16[512,256]{1,0:T(8,128)(2,1)}, u32[]{:S(2)}) copy-start(bf16[512,256]{1,0:T(8,128)(2,1)} %refs_3_.1) | copy-start | bytes 786436
  52.3 24.4 %all-to-all-start.2 = ((bf16[8,32,512]{2,1,0:T(8,128)(2,1)}), bf16[8,32,512]{2,1,0:T(8,128)(2,1)S(1)}, u32[]{:S(2)}, u32[]{:S(2)}) async-start(bf16[8,32,512]{2,1,0:T(8,128)(2,1)} %broadcast_in_dim.43), calls=%async_computation.2 | async-start | bytes 524288 | tf_op jit(solution)/shard_map/all_to_all | solution.py:123
  85.8 0.8 copy-start.5
  86.6 4.2 %copy-start.6 = (bf16[4,512,128]{2,1,0:T(8,128)(2,1)S(1)}, bf16[4,512,128]{2,1,0:T(8,128)(2,1)}, u32[]{:S(2)}) copy-start(bf16[4,512,128]{2,1,0:T(8,128)(2,1)} %copy-done.5) | copy-start | bytes 1572868
  86.6 14.9 %all-to-all-start.3 = ((bf16[8,128,128]{2,1,0:T(8,128)(2,1)}), bf16[8,128,128]{2,1,0:T(8,128)(2,1)S(1)}, u32[]{:S(2)}, u32[]{:S(2)}) async-start(bf16[8,128,128]{2,1,0:T(8,128)(2,1)} %bitcast.6), calls=%async_computation.3 | async-start | bytes 524288 | tf_op jit(solution)/shard_map/all_to_all | solution.py:123
  90.8 21.9 %collective-permute-start.5 = (bf16[4,512,128]{2,1,0:T(8,128)(2,1)S(1)}, bf16[4,512,128]{2,1,0:T(8,128)(2,1)S(1)}, u32[]{:S(2)}, u32[]{:S(2)}) collective-permute-start(bf16[4,512,128]{2,1,0:T(8,128)(2,1)S(1)} %copy-done.6), channel_id=1, source_target_pairs={{0,256},{64,320},{128,384},{192,448},{256,0},{320,64},{384,128},{4... | collective-permute-start | bytes 1572872 | tf_op jit(solution)/shard_map/ppermute | solution.py:154
  101.6 51.6 %copy-start.2 = (f32[4,512,128]{2,1,0:T(8,128)S(1)}, f32[4,512,128]{2,1,0:T(8,128)}, u32[]{:S(2)}) copy-start(f32[4,512,128]{2,1,0:T(8,128)} %get-tuple-element.26.refs_1_) | copy-start | bytes 3145732
  102.3 26.5 %all-to-all-start.4 = ((bf16[8,128,128]{2,1,0:T(8,128)(2,1)}), bf16[8,128,128]{2,1,0:T(8,128)(2,1)S(1)}, u32[]{:S(2)}, u32[]{:S(2)}) async-start(bf16[8,128,128]{2,1,0:T(8,128)(2,1)} %broadcast_in_dim.44), calls=%async_computation.4 | async-start | bytes 524288 | tf_op jit(solution)/shard_map/all_to_all | solution.py:123
  112.7 36.1 %collective-permute-start.8 = (bf16[4,512,128]{2,1,0:T(8,128)(2,1)}, bf16[4,512,128]{2,1,0:T(8,128)(2,1)S(1)}, u32[]{:S(2)}, u32[]{:S(2)}) collective-permute-start(bf16[4,512,128]{2,1,0:T(8,128)(2,1)} %get-tuple-element.36), channel_id=1, source_target_pairs={{0,128},{64,192},{128,0},{192,64},{256,384},{320,448},{384,256},{4... | collective-permute-start | bytes 1572872 | tf_op jit(solution)/shard_map/ppermute | solution.py:154
  125.1 28.1 %collective-permute-start.9 = (bf16[4,512,128]{2,1,0:T(8,128)(2,1)}, bf16[4,512,128]{2,1,0:T(8,128)(2,1)S(1)}, u32[]{:S(2)}, u32[]{:S(2)}) collective-permute-start(bf16[4,512,128]{2,1,0:T(8,128)(2,1)} %get-tuple-element.37), channel_id=1, source_target_pairs={{0,64},{64,0},{128,192},{192,128},{256,320},{320,256},{384,448},{4... | collective-permute-start | bytes 1572872 | tf_op jit(solution)/shard_map/ppermute | solution.py:154
  129.7 23.5 %all-to-all-start.5 = ((bf16[8,128,128]{2,1,0:T(8,128)(2,1)}), bf16[8,128,128]{2,1,0:T(8,128)(2,1)S(1)}, u32[]{:S(2)}, u32[]{:S(2)}) async-start(bf16[8,128,128]{2,1,0:T(8,128)(2,1)} %broadcast_in_dim.45), calls=%async_computation.5 | async-start | bytes 524288 | tf_op jit(solution)/shard_map/all_to_all | solution.py:123
  137.0 7.6 %collective-permute-start.6 = (bf16[512,128]{1,0:T(8,128)(2,1)S(1)}, bf16[512,128]{1,0:T(8,128)(2,1)S(1)}, u32[]{:S(2)}, u32[]{:S(2)}) collective-permute-start(bf16[512,128]{1,0:T(8,128)(2,1)S(1)} %get-tuple-element.32), channel_id=1, source_target_pairs={{0,8},{8,16},{16,24},{24,32},{32,40},{40,48},{48,56},{56,64},{64,7... | collective-permute-start | bytes 393224 | tf_op jit(solution)/shard_map/ppermute | solution.py:204
  141.0 6.9 %collective-permute-start.7 = (bf16[512,128]{1,0:T(8,128)(2,1)S(1)}, bf16[512,128]{1,0:T(8,128)(2,1)S(1)}, u32[]{:S(2)}, u32[]{:S(2)}) collective-permute-start(bf16[512,128]{1,0:T(8,128)(2,1)S(1)} %get-tuple-element.33), channel_id=1, source_target_pairs={{8,0},{16,8},{24,16},{32,24},{40,32},{48,40},{56,48},{64,56},{72,6... | collective-permute-start | bytes 393224 | tf_op jit(solution)/shard_map/ppermute | solution.py:203

commit v4 on v3

--- a/solution.py
+++ b/solution.py
@@ -57,24 +57,23 @@
             ksel[dst] = part_refs[r][src, :width]
             vsel[dst] = part_refs[r][src, width:]
         bias = bias_ref[b]
+        hss = [slice(h * DH, (h + 1) * DH) for h in range(heads)]
+        query = [q_ref[rows, hs] for hs in hss]
+        dout = [do_ref[rows, hs] for hs in hss]
+        scores = [dot(query[h], ksel[:, hss[h]], 1, 1) * scale + bias for h in range(heads)]
+        dprobs = [dot(dout[h], vsel[:, hss[h]], 1, 1) for h in range(heads)]
         for h in range(heads):
-            hs = slice(h * DH, (h + 1) * DH)
-            query = q_ref[rows, hs]
-            dout = do_ref[rows, hs]
-            keys = ksel[:, hs]
-            vals = vsel[:, hs]
-            scores = dot(query, keys, 1, 1) * scale + bias
-            dprobs = dot(dout, vals, 1, 1)
-            top = jnp.max(scores, axis=-1, keepdims=True)
-            expo = jnp.exp(scores - top)
+            hs = hss[h]
+            top = jnp.max(scores[h], axis=-1, keepdims=True)
+            expo = jnp.exp(scores[h] - top)
             probs = expo * (1.0 / jnp.sum(expo, axis=-1, keepdims=True))
             probs_b = probs.astype(BF16)
-            delta = jnp.sum(probs * dprobs, axis=-1, keepdims=True)
-            dscores = (probs * (dprobs - delta) * scale).astype(BF16)
-            ctx_ref[rows, hs] = dot(probs_b, vals, 1, 0).astype(BF16)
-            dq_ref[rows, hs] = dot(dscores, keys, 1, 0).astype(BF16)
-            kterm = dot(query.T, dscores, 1, 0)
-            vterm = dot(dout.T, probs_b, 1, 0)
+            delta = jnp.sum(probs * dprobs[h], axis=-1, keepdims=True)
+            dscores = (probs * (dprobs[h] - delta) * scale).astype(BF16)
+            ctx_ref[rows, hs] = dot(probs_b, vsel[:, hs], 1, 0).astype(BF16)
+            dq_ref[rows, hs] = dot(dscores, ksel[:, hs], 1, 0).astype(BF16)
+            kterm = dot(query[h].T, dscores, 1, 0)
+            vterm = dot(dout[h].T, probs_b, 1, 0)
             for base, term in ((h * DH, kterm), (width + h * DH, vterm)):
                 at = slice(base, base + DH)
                 for g in range(GLOBAL):
@@ -87,7 +86,7 @@
                     acc_part[r, picks[r], at] += term[:, o * BLK:(o + 1) * BLK]
         return carry
 
-    lax.fori_loop(0, nblk, step, 0)
+    lax.fori_loop(0, nblk, step, 0, unroll=4)
     gleft_ref[...] = acc_win[0].astype(BF16)
     gright_ref[...] = acc_win[nblk + 1].astype(BF16)
     own_ref[...] = acc_win[1:nblk + 1]

time: 157 us -> 155 us (0.987)
  Pallas kernels: 10.2 us -> 8.08 us
    pallas_call x1, Pallas kernels: 8.98 us -> 6.89 us  [shards(): pl.pallas_call(lambda *refs: attention_kernel(nblk, heads, *refs), out_sh...]
where the time goes in v4:
time: 155 us; the launch traced here: 152 us
  starting transfers between devices  92.7 us (60%)
  waiting for transfers between devices  41.1 us (27%)
  local copies, waits for them, and re-layouts  8.53 us (6%)
  Pallas kernels  8.08 us (5%)
    all_to_all x6, starting transfers between devices, exchange(): return lax.all_to_all(x, axis, 0, 0, tiled=True)  46.7 us
    ppermute x6, starting transfers between devices, partner(): return lax.ppermute(x, 'y', [(i, i ^ masks[r]) for i in range(ny)])  34.9 us
    ppermute x6, waiting for transfers between devices, partner(): return lax.ppermute(x, 'y', [(i, i ^ masks[r]) for i in range(ny)])  22.1 us
    all_to_all x6, waiting for transfers between devices, exchange(): return lax.all_to_all(x, axis, 0, 0, tiled=True)  13.4 us
    pallas_call x1, Pallas kernels, shards(): pl.pallas_call(lambda *refs: attention_kernel(nblk, heads, *refs), out_sh...  6.89 us
    ppermute x1, starting transfers between devices, shards(): left = lax.ppermute(kv[tokens - BLK:], SEQ_AXES, up)  4.55 us
    ppermute x1, starting transfers between devices, shards(): low = lax.ppermute(gright, SEQ_AXES, up)  3.92 us
    ppermute x1, waiting for transfers between devices, shards(): high = lax.ppermute(gleft, SEQ_AXES, down)  3.22 us
  transfers between devices with their start and end apart: 16, of which 8 were waited for; matrix products, arithmetic and copies ran while one was open for 4% of the time, Pallas kernels for 0%

profile of v4, /device:TPU:6, one launch (start us, length us, event | category | flops | bytes accessed | tf_op | source)
XLA Modules:
  0.0 152.3 jit_solution(1961456808761616460)
XLA Ops:
  0.6 0.0 slice-start
  0.6 0.0 slice-start.1
  0.7 0.9 slice-done
  1.5 0.1 slice-done.1
  1.6 0.7 pad_maximum_fusion
  2.3 10.4 %all-to-all-start = ((bf16[8,32,512]{2,1,0:T(8,128)(2,1)}), bf16[8,32,512]{2,1,0:T(8,128)(2,1)S(1)}, u32[]{:S(2)}, u32[]{:S(2)}) async-start(bf16[8,32,512]{2,1,0:T(8,128)(2,1)} %bitcast.1), calls=%async_computation | async-start | bytes 524288 | tf_op jit(solution)/shard_map/all_to_all | solution.py:122
  12.8 0.0 copy-done
  12.8 0.0 copy-start.1
  12.8 0.8 constant_dynamic-update-slice_fusion.1
  13.5 0.3 copy-done.1
  13.8 0.8 constant_dynamic-update-slice_fusion
  14.6 7.7 %collective-permute-start.2 = (bf16[512,512]{1,0:T(8,128)(2,1)}, bf16[512,512]{1,0:T(8,128)(2,1)S(1)}, u32[]{:S(2)}, u32[]{:S(2)}) collective-permute-start(bf16[512,512]{1,0:T(8,128)(2,1)} %constant_dynamic-update-slice_fusion), channel_id=1, source_target_pairs={{0,256},{64,320},{128,384},{192,448},{256,0},{320,64},{384,128},{4... | collective-permute-start | bytes 1572872 | tf_op jit(solution)/shard_map/ppermute | solution.py:153
  22.3 2.3 %all-to-all-done = bf16[8,32,512]{2,1,0:T(8,128)(2,1)S(1)} async-done(((bf16[8,32,512]{2,1,0:T(8,128)(2,1)}), bf16[8,32,512]{2,1,0:T(8,128)(2,1)S(1)}, u32[]{:S(2)}, u32[]{:S(2)}) %all-to-all-start) | async-done | bytes 262176 | tf_op jit(solution)/shard_map/all_to_all | solution.py:122
  24.7 0.7 broadcast_in_dim.41
  25.4 7.1 %all-to-all-start.1 = ((bf16[8,32,512]{2,1,0:T(8,128)(2,1)}), bf16[8,32,512]{2,1,0:T(8,128)(2,1)S(1)}, u32[]{:S(2)}, u32[]{:S(2)}) async-start(bf16[8,32,512]{2,1,0:T(8,128)(2,1)} %broadcast_in_dim.41), calls=%async_computation.1 | async-start | bytes 524288 | tf_op jit(solution)/shard_map/all_to_all | solution.py:122
  32.5 1.0 fusion.2
  33.5 1.3 collective-permute-start.1
  34.8 4.6 %collective-permute-start = (bf16[128,512]{1,0:T(8,128)(2,1)S(1)}, bf16[128,512]{1,0:T(8,128)(2,1)S(1)}, u32[]{:S(2)}, u32[]{:S(2)}) collective-permute-start(bf16[128,512]{1,0:T(8,128)(2,1)S(1)} %get-tuple-element.41), channel_id=1, source_target_pairs={{0,8},{8,16},{16,24},{24,32},{32,40},{40,48},{48,56},{56,64},{64,7... | collective-permute-start | bytes 393224 | tf_op jit(solution)/shard_map/ppermute | solution.py:159
  39.3 0.0 copy-start.7
  39.4 0.7 copy-done.7
  40.0 0.1 add_select_fusion.1
  40.1 3.9 %collective-permute-start.4 = (bf16[512,512]{1,0:T(8,128)(2,1)}, bf16[512,512]{1,0:T(8,128)(2,1)S(1)}, u32[]{:S(2)}, u32[]{:S(2)}) collective-permute-start(bf16[512,512]{1,0:T(8,128)(2,1)} %constant_dynamic-update-slice_fusion), channel_id=1, source_target_pairs={{0,64},{64,0},{128,192},{192,128},{256,320},{320,256},{384,448},{4... | collective-permute-start | bytes 1572872 | tf_op jit(solution)/shard_map/ppermute | solution.py:153
  44.0 4.3 %collective-permute-start.3 = (bf16[512,512]{1,0:T(8,128)(2,1)}, bf16[512,512]{1,0:T(8,128)(2,1)S(1)}, u32[]{:S(2)}, u32[]{:S(2)}) collective-permute-start(bf16[512,512]{1,0:T(8,128)(2,1)} %constant_dynamic-update-slice_fusion), channel_id=1, source_target_pairs={{0,128},{64,192},{128,0},{192,64},{256,384},{320,448},{384,256},{4... | collective-permute-start | bytes 1572872 | tf_op jit(solution)/shard_map/ppermute | solution.py:153
  48.3 3.3 %all-to-all-done.1 = bf16[8,32,512]{2,1,0:T(8,128)(2,1)S(1)} async-done(((bf16[8,32,512]{2,1,0:T(8,128)(2,1)}), bf16[8,32,512]{2,1,0:T(8,128)(2,1)S(1)}, u32[]{:S(2)}, u32[]{:S(2)}) %all-to-all-start.1) | async-done | bytes 262176 | tf_op jit(solution)/shard_map/all_to_all | solution.py:122
  51.6 0.7 broadcast_in_dim.43
  52.3 7.1 %all-to-all-start.2 = ((bf16[8,32,512]{2,1,0:T(8,128)(2,1)}), bf16[8,32,512]{2,1,0:T(8,128)(2,1)S(1)}, u32[]{:S(2)}, u32[]{:S(2)}) async-start(bf16[8,32,512]{2,1,0:T(8,128)(2,1)} %broadcast_in_dim.43), calls=%async_computation.2 | async-start | bytes 524288 | tf_op jit(solution)/shard_map/all_to_all | solution.py:122
  59.5 0.1 copy.11
  59.6 0.1 reshape.39.refs_0_
  59.7 0.1 fusion.1
  59.7 0.1 add_select_fusion
  59.8 0.1 copy.12
  59.9 0.0 collective-permute-done.1.refs_7_
  59.9 0.0 collective-permute-done.refs_6_
  59.9 0.0 collective-permute-done.2.refs_9_
  59.9 16.8 %collective-permute-done.4.refs_11_ = bf16[512,512]{1,0:T(8,128)(2,1)S(1)} collective-permute-done((bf16[512,512]{1,0:T(8,128)(2,1)}, bf16[512,512]{1,0:T(8,128)(2,1)S(1)}, u32[]{:S(2)}, u32[]{:S(2)}) %collective-permute-start.4) | collective-permute-done | bytes 524320 | tf_op jit(solution)/shard_map/ppermute | solution.py:153
  76.7 0.0 collective-permute-done.3.refs_10_
  76.7 0.0 all-to-all-done.2
  76.7 0.1 broadcast_in_dim.40
  76.8 0.0 copy-done.3
  76.8 0.0 copy-done.4
  76.8 6.9 %attention.1 = (bf16[512,256]{1,0:T(8,128)(2,1)}, bf16[512,256]{1,0:T(8,128)(2,1)}, f32[4,512,128]{2,1,0:T(8,128)}, bf16[512,128]{1,0:T(8,128)(2,1)S(1)}, bf16[5...) custom-call(s32[12]{0:T(128)S(1)} %reshape.39.refs_0_, ...), custom_call_target="tpu_custom_call" | custom-call | tf_op jit(solution)/shard_map/attention/pallas_call | solution.py:177
  83.7 0.8 copy-done.5
  84.5 4.2 %all-to-all-start.3 = ((bf16[8,128,128]{2,1,0:T(8,128)(2,1)}), bf16[8,128,128]{2,1,0:T(8,128)(2,1)S(1)}, u32[]{:S(2)}, u32[]{:S(2)}) async-start(bf16[8,128,128]{2,1,0:T(8,128)(2,1)} %bitcast.6), calls=%async_computation.3 | async-start | bytes 524288 | tf_op jit(solution)/shard_map/all_to_all | solution.py:122
  88.8 0.0 copy-done.6
  88.8 2.9 %collective-permute-start.5 = (bf16[4,512,128]{2,1,0:T(8,128)(2,1)S(1)}, bf16[4,512,128]{2,1,0:T(8,128)(2,1)S(1)}, u32[]{:S(2)}, u32[]{:S(2)}) collective-permute-start(bf16[4,512,128]{2,1,0:T(8,128)(2,1)S(1)} %copy-done.6), channel_id=1, source_target_pairs={{0,256},{64,320},{128,384},{192,448},{256,0},{320,64},{384,128},{4... | collective-permute-start | bytes 1572872 | tf_op jit(solution)/shard_map/ppermute | solution.py:153
  91.7 7.8 %all-to-all-done.3 = bf16[8,128,128]{2,1,0:T(8,128)(2,1)S(1)} async-done(((bf16[8,128,128]{2,1,0:T(8,128)(2,1)}), bf16[8,128,128]{2,1,0:T(8,128)(2,1)S(1)}, u32[]{:S(2)}, u32[]{:S(2)}) %all-to-all-start.3) | async-done | bytes 262176 | tf_op jit(solution)/shard_map/all_to_all | solution.py:122
  99.5 0.0 copy-start.2
  99.5 0.7 broadcast_in_dim.44
  100.3 10.4 %all-to-all-start.4 = ((bf16[8,128,128]{2,1,0:T(8,128)(2,1)}), bf16[8,128,128]{2,1,0:T(8,128)(2,1)S(1)}, u32[]{:S(2)}, u32[]{:S(2)}) async-start(bf16[8,128,128]{2,1,0:T(8,128)(2,1)} %broadcast_in_dim.44), calls=%async_computation.4 | async-start | bytes 524288 | tf_op jit(solution)/shard_map/all_to_all | solution.py:122
  110.7 0.0 collective-permute-done.5.refs_5_
  110.7 12.4 %collective-permute-start.8 = (bf16[4,512,128]{2,1,0:T(8,128)(2,1)}, bf16[4,512,128]{2,1,0:T(8,128)(2,1)S(1)}, u32[]{:S(2)}, u32[]{:S(2)}) collective-permute-start(bf16[4,512,128]{2,1,0:T(8,128)(2,1)} %get-tuple-element.36), channel_id=1, source_target_pairs={{0,128},{64,192},{128,0},{192,64},{256,384},{320,448},{384,256},{4... | collective-permute-start | bytes 1572872 | tf_op jit(solution)/shard_map/ppermute | solution.py:153
  123.0 3.8 %collective-permute-start.9 = (bf16[4,512,128]{2,1,0:T(8,128)(2,1)}, bf16[4,512,128]{2,1,0:T(8,128)(2,1)S(1)}, u32[]{:S(2)}, u32[]{:S(2)}) collective-permute-start(bf16[4,512,128]{2,1,0:T(8,128)(2,1)} %get-tuple-element.37), channel_id=1, source_target_pairs={{0,64},{64,0},{128,192},{192,128},{256,320},{320,256},{384,448},{4... | collective-permute-start | bytes 1572872 | tf_op jit(solution)/shard_map/ppermute | solution.py:153
  126.8 0.0 all-to-all-done.4
  126.9 0.7 broadcast_in_dim.45
  127.6 7.4 %all-to-all-start.5 = ((bf16[8,128,128]{2,1,0:T(8,128)(2,1)}), bf16[8,128,128]{2,1,0:T(8,128)(2,1)S(1)}, u32[]{:S(2)}, u32[]{:S(2)}) async-start(bf16[8,128,128]{2,1,0:T(8,128)(2,1)} %broadcast_in_dim.45), calls=%async_computation.5 | async-start | bytes 524288 | tf_op jit(solution)/shard_map/all_to_all | solution.py:122
  135.0 3.9 %collective-permute-start.6 = (bf16[512,128]{1,0:T(8,128)(2,1)S(1)}, bf16[512,128]{1,0:T(8,128)(2,1)S(1)}, u32[]{:S(2)}, u32[]{:S(2)}) collective-permute-start(bf16[512,128]{1,0:T(8,128)(2,1)S(1)} %get-tuple-element.32), channel_id=1, source_target_pairs={{0,8},{8,16},{16,24},{24,32},{32,40},{40,48},{48,56},{56,64},{64,7... | collective-permute-start | bytes 393224 | tf_op jit(solution)/shard_map/ppermute | solution.py:203
  138.9 1.3 collective-permute-start.7
  140.2 2.3 %collective-permute-done.6.refs_2_ = bf16[512,128]{1,0:T(8,128)(2,1)S(1)} collective-permute-done((bf16[512,128]{1,0:T(8,128)(2,1)S(1)}, bf16[512,128]{1,0:T(8,128)(2,1)S(1)}, u32[]{:S(2)}, u32[]{:S(2)}) %collective-permute-start.6) | collective-permute-done | bytes 131104 | tf_op jit(solution)/shard_map/ppermute | solution.py:203
  142.5 3.2 %collective-permute-done.7.refs_3_ = bf16[512,128]{1,0:T(8,128)(2,1)S(1)} collective-permute-done((bf16[512,128]{1,0:T(8,128)(2,1)S(1)}, bf16[512,128]{1,0:T(8,128)(2,1)S(1)}, u32[]{:S(2)}, u32[]{:S(2)}) %collective-permute-start.7) | collective-permute-done | bytes 131104 | tf_op jit(solution)/shard_map/ppermute | solution.py:202
  145.8 1.0 collective-permute-done.8.refs_6_
  146.7 4.4 %collective-permute-done.9.refs_7_ = bf16[4,512,128]{2,1,0:T(8,128)(2,1)S(1)} collective-permute-done((bf16[4,512,128]{2,1,0:T(8,128)(2,1)}, bf16[4,512,128]{2,1,0:T(8,128)(2,1)S(1)}, u32[]{:S(2)}, u32[]{:S(2)}) %collective-permute-start.9) | collective-permute-done | bytes 524320 | tf_op jit(solution)/shard_map/ppermute | solution.py:153
  151.1 0.0 all-to-all-done.5
  151.1 0.0 copy-done.2
  151.1 1.2 finish.1
  (13 shorter events, 0.1 us)
Async XLA Ops:
  0.6 0.9 slice-start
  0.6 1.0 slice-start.1
  2.3 10.5 %copy-start = (bf16[512,256]{1,0:T(8,128)(2,1)S(1)}, bf16[512,256]{1,0:T(8,128)(2,1)}, u32[]{:S(2)}) copy-start(bf16[512,256]{1,0:T(8,128)(2,1)} %refs_4_.1) | copy-start | bytes 786436
  2.3 22.3 %all-to-all-start = ((bf16[8,32,512]{2,1,0:T(8,128)(2,1)}), bf16[8,32,512]{2,1,0:T(8,128)(2,1)S(1)}, u32[]{:S(2)}, u32[]{:S(2)}) async-start(bf16[8,32,512]{2,1,0:T(8,128)(2,1)} %bitcast.1), calls=%async_computation | async-start | bytes 524288 | tf_op jit(solution)/shard_map/all_to_all | solution.py:122
  12.8 1.0 copy-start.1
  14.6 45.3 %collective-permute-start.2 = (bf16[512,512]{1,0:T(8,128)(2,1)}, bf16[512,512]{1,0:T(8,128)(2,1)S(1)}, u32[]{:S(2)}, u32[]{:S(2)}) collective-permute-start(bf16[512,512]{1,0:T(8,128)(2,1)} %constant_dynamic-update-slice_fusion), channel_id=1, source_target_pairs={{0,256},{64,320},{128,384},{192,448},{256,0},{320,64},{384,128},{4... | collective-permute-start | bytes 1572872 | tf_op jit(solution)/shard_map/ppermute | solution.py:153
  25.4 26.2 %all-to-all-start.1 = ((bf16[8,32,512]{2,1,0:T(8,128)(2,1)}), bf16[8,32,512]{2,1,0:T(8,128)(2,1)S(1)}, u32[]{:S(2)}, u32[]{:S(2)}) async-start(bf16[8,32,512]{2,1,0:T(8,128)(2,1)} %broadcast_in_dim.41), calls=%async_computation.1 | async-start | bytes 524288 | tf_op jit(solution)/shard_map/all_to_all | solution.py:122
  33.5 26.4 %collective-permute-start.1 = (bf16[128,512]{1,0:T(8,128)(2,1)S(1)}, bf16[128,512]{1,0:T(8,128)(2,1)S(1)}, u32[]{:S(2)}, u32[]{:S(2)}) collective-permute-start(bf16[128,512]{1,0:T(8,128)(2,1)S(1)} %get-tuple-element.40), channel_id=1, source_target_pairs={{8,0},{16,8},{24,16},{32,24},{40,32},{48,40},{56,48},{64,56},{72,6... | collective-permute-start | bytes 393224 | tf_op jit(solution)/shard_map/ppermute | solution.py:160
  34.8 25.1 %collective-permute-start = (bf16[128,512]{1,0:T(8,128)(2,1)S(1)}, bf16[128,512]{1,0:T(8,128)(2,1)S(1)}, u32[]{:S(2)}, u32[]{:S(2)}) collective-permute-start(bf16[128,512]{1,0:T(8,128)(2,1)S(1)} %get-tuple-element.41), channel_id=1, source_target_pairs={{0,8},{8,16},{16,24},{24,32},{32,40},{40,48},{48,56},{56,64},{64,7... | collective-permute-start | bytes 393224 | tf_op jit(solution)/shard_map/ppermute | solution.py:159
  39.3 0.7 copy-start.7
  40.1 36.6 %collective-permute-start.4 = (bf16[512,512]{1,0:T(8,128)(2,1)}, bf16[512,512]{1,0:T(8,128)(2,1)S(1)}, u32[]{:S(2)}, u32[]{:S(2)}) collective-permute-start(bf16[512,512]{1,0:T(8,128)(2,1)} %constant_dynamic-update-slice_fusion), channel_id=1, source_target_pairs={{0,64},{64,0},{128,192},{192,128},{256,320},{320,256},{384,448},{4... | collective-permute-start | bytes 1572872 | tf_op jit(solution)/shard_map/ppermute | solution.py:153
  44.0 32.7 %collective-permute-start.3 = (bf16[512,512]{1,0:T(8,128)(2,1)}, bf16[512,512]{1,0:T(8,128)(2,1)S(1)}, u32[]{:S(2)}, u32[]{:S(2)}) collective-permute-start(bf16[512,512]{1,0:T(8,128)(2,1)} %constant_dynamic-update-slice_fusion), channel_id=1, source_target_pairs={{0,128},{64,192},{128,0},{192,64},{256,384},{320,448},{384,256},{4... | collective-permute-start | bytes 1572872 | tf_op jit(solution)/shard_map/ppermute | solution.py:153
  52.3 24.5 %copy-start.3 = (bf16[512,256]{1,0:T(8,128)(2,1)S(1)}, bf16[512,256]{1,0:T(8,128)(2,1)}, u32[]{:S(2)}) copy-start(bf16[512,256]{1,0:T(8,128)(2,1)} %refs_2_.1) | copy-start | bytes 786436
  52.3 24.5 %copy-start.4 = (bf16[512,256]{1,0:T(8,128)(2,1)S(1)}, bf16[512,256]{1,0:T(8,128)(2,1)}, u32[]{:S(2)}) copy-start(bf16[512,256]{1,0:T(8,128)(2,1)} %refs_3_.1) | copy-start | bytes 786436
  52.3 24.4 %all-to-all-start.2 = ((bf16[8,32,512]{2,1,0:T(8,128)(2,1)}), bf16[8,32,512]{2,1,0:T(8,128)(2,1)S(1)}, u32[]{:S(2)}, u32[]{:S(2)}) async-start(bf16[8,32,512]{2,1,0:T(8,128)(2,1)} %broadcast_in_dim.43), calls=%async_computation.2 | async-start | bytes 524288 | tf_op jit(solution)/shard_map/all_to_all | solution.py:122
  83.7 0.8 copy-start.5
  84.5 4.3 %copy-start.6 = (bf16[4,512,128]{2,1,0:T(8,128)(2,1)S(1)}, bf16[4,512,128]{2,1,0:T(8,128)(2,1)}, u32[]{:S(2)}) copy-start(bf16[4,512,128]{2,1,0:T(8,128)(2,1)} %copy-done.5) | copy-start | bytes 1572868
  84.5 15.0 %all-to-all-start.3 = ((bf16[8,128,128]{2,1,0:T(8,128)(2,1)}), bf16[8,128,128]{2,1,0:T(8,128)(2,1)S(1)}, u32[]{:S(2)}, u32[]{:S(2)}) async-start(bf16[8,128,128]{2,1,0:T(8,128)(2,1)} %bitcast.6), calls=%async_computation.3 | async-start | bytes 524288 | tf_op jit(solution)/shard_map/all_to_all | solution.py:122
  88.8 21.9 %collective-permute-start.5 = (bf16[4,512,128]{2,1,0:T(8,128)(2,1)S(1)}, bf16[4,512,128]{2,1,0:T(8,128)(2,1)S(1)}, u32[]{:S(2)}, u32[]{:S(2)}) collective-permute-start(bf16[4,512,128]{2,1,0:T(8,128)(2,1)S(1)} %copy-done.6), channel_id=1, source_target_pairs={{0,256},{64,320},{128,384},{192,448},{256,0},{320,64},{384,128},{4... | collective-permute-start | bytes 1572872 | tf_op jit(solution)/shard_map/ppermute | solution.py:153
  99.5 51.6 %copy-start.2 = (f32[4,512,128]{2,1,0:T(8,128)S(1)}, f32[4,512,128]{2,1,0:T(8,128)}, u32[]{:S(2)}) copy-start(f32[4,512,128]{2,1,0:T(8,128)} %get-tuple-element.26.refs_1_) | copy-start | bytes 3145732
  100.3 26.5 %all-to-all-start.4 = ((bf16[8,128,128]{2,1,0:T(8,128)(2,1)}), bf16[8,128,128]{2,1,0:T(8,128)(2,1)S(1)}, u32[]{:S(2)}, u32[]{:S(2)}) async-start(bf16[8,128,128]{2,1,0:T(8,128)(2,1)} %broadcast_in_dim.44), calls=%async_computation.4 | async-start | bytes 524288 | tf_op jit(solution)/shard_map/all_to_all | solution.py:122
  110.7 36.1 %collective-permute-start.8 = (bf16[4,512,128]{2,1,0:T(8,128)(2,1)}, bf16[4,512,128]{2,1,0:T(8,128)(2,1)S(1)}, u32[]{:S(2)}, u32[]{:S(2)}) collective-permute-start(bf16[4,512,128]{2,1,0:T(8,128)(2,1)} %get-tuple-element.36), channel_id=1, source_target_pairs={{0,128},{64,192},{128,0},{192,64},{256,384},{320,448},{384,256},{4... | collective-permute-start | bytes 1572872 | tf_op jit(solution)/shard_map/ppermute | solution.py:153
  123.0 28.1 %collective-permute-start.9 = (bf16[4,512,128]{2,1,0:T(8,128)(2,1)}, bf16[4,512,128]{2,1,0:T(8,128)(2,1)S(1)}, u32[]{:S(2)}, u32[]{:S(2)}) collective-permute-start(bf16[4,512,128]{2,1,0:T(8,128)(2,1)} %get-tuple-element.37), channel_id=1, source_target_pairs={{0,64},{64,0},{128,192},{192,128},{256,320},{320,256},{384,448},{4... | collective-permute-start | bytes 1572872 | tf_op jit(solution)/shard_map/ppermute | solution.py:153
  127.6 23.5 %all-to-all-start.5 = ((bf16[8,128,128]{2,1,0:T(8,128)(2,1)}), bf16[8,128,128]{2,1,0:T(8,128)(2,1)S(1)}, u32[]{:S(2)}, u32[]{:S(2)}) async-start(bf16[8,128,128]{2,1,0:T(8,128)(2,1)} %broadcast_in_dim.45), calls=%async_computation.5 | async-start | bytes 524288 | tf_op jit(solution)/shard_map/all_to_all | solution.py:122
  135.0 7.6 %collective-permute-start.6 = (bf16[512,128]{1,0:T(8,128)(2,1)S(1)}, bf16[512,128]{1,0:T(8,128)(2,1)S(1)}, u32[]{:S(2)}, u32[]{:S(2)}) collective-permute-start(bf16[512,128]{1,0:T(8,128)(2,1)S(1)} %get-tuple-element.32), channel_id=1, source_target_pairs={{0,8},{8,16},{16,24},{24,32},{32,40},{40,48},{48,56},{56,64},{64,7... | collective-permute-start | bytes 393224 | tf_op jit(solution)/shard_map/ppermute | solution.py:203
  138.9 6.9 %collective-permute-start.7 = (bf16[512,128]{1,0:T(8,128)(2,1)S(1)}, bf16[512,128]{1,0:T(8,128)(2,1)S(1)}, u32[]{:S(2)}, u32[]{:S(2)}) collective-permute-start(bf16[512,128]{1,0:T(8,128)(2,1)S(1)} %get-tuple-element.33), channel_id=1, source_target_pairs={{8,0},{16,8},{24,16},{32,24},{40,32},{48,40},{56,48},{64,56},{72,6... | collective-permute-start | bytes 393224 | tf_op jit(solution)/shard_map/ppermute | solution.py:202

commit v5 on v4

--- a/solution.py
+++ b/solution.py
@@ -160,7 +160,9 @@
     right = lax.ppermute(kv[:BLK], SEQ_AXES, down)
     far = partner(kv, 0)
     kv, piece = tie(kv, piece)
-    fetched = [far] + [partner(kv, r) for r in range(1, RAND)]
+    one = partner(kv, 2)
+    kv, far = tie(kv, far)
+    fetched = [far, partner(kv, 1), one]
     piece = exchange(spread(piece, ny), "y")[0]
     glob = exchange(spread(piece, nz), "z").reshape(grows, 2 * width)
 
@@ -197,8 +199,10 @@
 
     pieces = total(exchange(gglob.reshape(nz, -1, DH), "z"))
     far = partner(gparts[0], 0)
-    far, gleft, gright, *gnear = tie(far, gleft, gright, *gparts[1:])
-    back = [far] + [partner(g, r + 1) for r, g in enumerate(gnear)]
+    pieces, gtwo = tie(pieces, gparts[1])
+    back = [far, partner(gtwo, 1), None]
+    back[0], gleft, gright, gone = tie(far, gleft, gright, gparts[2])
+    back[2] = partner(gone, 2)
     high = lax.ppermute(gleft, SEQ_AXES, down)
     low = lax.ppermute(gright, SEQ_AXES, up)
     pieces = total(exchange(spread(pieces, ny), "y"))

time: 155 us -> 152 us (0.981)
  starting transfers between devices: 92.7 us -> 85.4 us
  waiting for transfers between devices: 41.1 us -> 45.5 us
    ppermute x6, waiting for transfers between devices: 22.1 us -> 30.4 us  [partner(): return lax.ppermute(x, 'y', [(i, i ^ masks[r]) for i in range(ny)])]
    ppermute x6, starting transfers between devices: 34.9 us -> 29.8 us  [partner(): return lax.ppermute(x, 'y', [(i, i ^ masks[r]) for i in range(ny)])]
    all_to_all x6, waiting for transfers between devices: 13.4 us -> 9.51 us  [exchange(): return lax.all_to_all(x, axis, 0, 0, tiled=True)]
    all_to_all x6, starting transfers between devices: 46.7 us -> 44.5 us  [exchange(): return lax.all_to_all(x, axis, 0, 0, tiled=True)]
  transfers between devices with their start and end apart: 16 -> 16, of which waited for: 8 -> 9; matrix products, arithmetic and copies ran while one was open for 4% -> 4% of each run, Pallas kernels for 0% -> 0%
where the time goes in v5:
time: 152 us; the launch traced here: 149 us
  starting transfers between devices  85.4 us (56%)
  waiting for transfers between devices  45.5 us (30%)
  local copies, waits for them, and re-layouts  8.53 us (6%)
  Pallas kernels  8.08 us (5%)
    all_to_all x6, starting transfers between devices, exchange(): return lax.all_to_all(x, axis, 0, 0, tiled=True)  44.5 us
    ppermute x6, waiting for transfers between devices, partner(): return lax.ppermute(x, 'y', [(i, i ^ masks[r]) for i in range(ny)])  30.4 us
    ppermute x6, starting transfers between devices, partner(): return lax.ppermute(x, 'y', [(i, i ^ masks[r]) for i in range(ny)])  29.8 us
    all_to_all x6, waiting for transfers between devices, exchange(): return lax.all_to_all(x, axis, 0, 0, tiled=True)  9.51 us
    pallas_call x1, Pallas kernels, shards(): pl.pallas_call(lambda *refs: attention_kernel(nblk, heads, *refs), out_sh...  6.89 us
    ppermute x1, starting transfers between devices, shards(): left = lax.ppermute(kv[tokens - BLK:], SEQ_AXES, up)  4.55 us
    ppermute x1, waiting for transfers between devices, shards(): high = lax.ppermute(gleft, SEQ_AXES, down)  3.97 us
    ppermute x1, starting transfers between devices, shards(): low = lax.ppermute(gright, SEQ_AXES, up)  3.92 us
  transfers between devices with their start and end apart: 16, of which 9 were waited for; matrix products, arithmetic and copies ran while one was open for 4% of the time, Pallas kernels for 0%

profile of v5, /device:TPU:6, one launch (start us, length us, event | category | flops | bytes accessed | tf_op | source)
XLA Modules:
  0.0 149.4 jit_solution(11709660316819765780)
XLA Ops:
  0.6 0.0 slice-start
  0.6 0.0 slice-start.1
  0.7 0.9 slice-done
  1.5 0.1 slice-done.1
  1.6 0.7 pad_maximum_fusion
  2.3 10.4 %all-to-all-start = ((bf16[8,32,512]{2,1,0:T(8,128)(2,1)}), bf16[8,32,512]{2,1,0:T(8,128)(2,1)S(1)}, u32[]{:S(2)}, u32[]{:S(2)}) async-start(bf16[8,32,512]{2,1,0:T(8,128)(2,1)} %bitcast.1), calls=%async_computation | async-start | bytes 524288 | tf_op jit(solution)/shard_map/all_to_all | solution.py:122
  12.8 0.0 copy-done
  12.8 0.0 copy-start.1
  12.8 0.8 constant_dynamic-update-slice_fusion.1
  13.5 0.3 copy-done.1
  13.8 0.8 constant_dynamic-update-slice_fusion
  14.6 7.7 %collective-permute-start.2 = (bf16[512,512]{1,0:T(8,128)(2,1)}, bf16[512,512]{1,0:T(8,128)(2,1)S(1)}, u32[]{:S(2)}, u32[]{:S(2)}) collective-permute-start(bf16[512,512]{1,0:T(8,128)(2,1)} %constant_dynamic-update-slice_fusion), channel_id=1, source_target_pairs={{0,256},{64,320},{128,384},{192,448},{256,0},{320,64},{384,128},{4... | collective-permute-start | bytes 1572872 | tf_op jit(solution)/shard_map/ppermute | solution.py:153
  22.3 2.3 %all-to-all-done = bf16[8,32,512]{2,1,0:T(8,128)(2,1)S(1)} async-done(((bf16[8,32,512]{2,1,0:T(8,128)(2,1)}), bf16[8,32,512]{2,1,0:T(8,128)(2,1)S(1)}, u32[]{:S(2)}, u32[]{:S(2)}) %all-to-all-start) | async-done | bytes 262176 | tf_op jit(solution)/shard_map/all_to_all | solution.py:122
  24.7 0.7 broadcast_in_dim.41
  25.4 7.1 %all-to-all-start.1 = ((bf16[8,32,512]{2,1,0:T(8,128)(2,1)}), bf16[8,32,512]{2,1,0:T(8,128)(2,1)S(1)}, u32[]{:S(2)}, u32[]{:S(2)}) async-start(bf16[8,32,512]{2,1,0:T(8,128)(2,1)} %broadcast_in_dim.41), calls=%async_computation.1 | async-start | bytes 524288 | tf_op jit(solution)/shard_map/all_to_all | solution.py:122
  32.5 1.0 fusion.2
  33.5 1.3 collective-permute-start.1
  34.8 4.6 %collective-permute-start = (bf16[128,512]{1,0:T(8,128)(2,1)S(1)}, bf16[128,512]{1,0:T(8,128)(2,1)S(1)}, u32[]{:S(2)}, u32[]{:S(2)}) collective-permute-start(bf16[128,512]{1,0:T(8,128)(2,1)S(1)} %get-tuple-element.47), channel_id=1, source_target_pairs={{0,8},{8,16},{16,24},{24,32},{32,40},{40,48},{48,56},{56,64},{64,7... | collective-permute-start | bytes 393224 | tf_op jit(solution)/shard_map/ppermute | solution.py:159
  39.3 0.0 copy-start.7
  39.4 0.7 copy-done.7
  40.0 0.1 add_select_fusion.1
  40.1 3.9 %collective-permute-start.4 = (bf16[512,512]{1,0:T(8,128)(2,1)}, bf16[512,512]{1,0:T(8,128)(2,1)S(1)}, u32[]{:S(2)}, u32[]{:S(2)}) collective-permute-start(bf16[512,512]{1,0:T(8,128)(2,1)} %constant_dynamic-update-slice_fusion), channel_id=1, source_target_pairs={{0,64},{64,0},{128,192},{192,128},{256,320},{320,256},{384,448},{4... | collective-permute-start | bytes 1572872 | tf_op jit(solution)/shard_map/ppermute | solution.py:153
  44.0 1.4 collective-permute-done.2.refs_9_
  45.4 7.2 %collective-permute-start.3 = (bf16[512,512]{1,0:T(8,128)(2,1)}, bf16[512,512]{1,0:T(8,128)(2,1)S(1)}, u32[]{:S(2)}, u32[]{:S(2)}) collective-permute-start(bf16[512,512]{1,0:T(8,128)(2,1)} %constant_dynamic-update-slice_fusion), channel_id=1, source_target_pairs={{0,128},{64,192},{128,0},{192,64},{256,384},{320,448},{384,256},{4... | collective-permute-start | bytes 1572872 | tf_op jit(solution)/shard_map/ppermute | solution.py:153
  52.6 0.0 all-to-all-done.1
  52.6 0.7 broadcast_in_dim.43
  53.4 6.9 %all-to-all-start.2 = ((bf16[8,32,512]{2,1,0:T(8,128)(2,1)}), bf16[8,32,512]{2,1,0:T(8,128)(2,1)S(1)}, u32[]{:S(2)}, u32[]{:S(2)}) async-start(bf16[8,32,512]{2,1,0:T(8,128)(2,1)} %broadcast_in_dim.43), calls=%async_computation.2 | async-start | bytes 524288 | tf_op jit(solution)/shard_map/all_to_all | solution.py:122
  60.3 0.1 copy.11
  60.4 0.1 reshape.39.refs_0_
  60.5 0.1 fusion.1
  60.5 0.1 add_select_fusion
  60.6 0.1 copy.12
  60.7 0.0 collective-permute-done.1.refs_7_
  60.7 0.0 collective-permute-done.refs_6_
  60.7 16.0 %collective-permute-done.4.refs_11_ = bf16[512,512]{1,0:T(8,128)(2,1)S(1)} collective-permute-done((bf16[512,512]{1,0:T(8,128)(2,1)}, bf16[512,512]{1,0:T(8,128)(2,1)S(1)}, u32[]{:S(2)}, u32[]{:S(2)}) %collective-permute-start.4) | collective-permute-done | bytes 524320 | tf_op jit(solution)/shard_map/ppermute | solution.py:153
  76.7 0.0 collective-permute-done.3.refs_10_
  76.7 0.0 all-to-all-done.2
  76.7 0.1 broadcast_in_dim.40
  76.8 0.0 copy-done.3
  76.8 0.0 copy-done.4
  76.8 6.9 %attention.1 = (bf16[512,256]{1,0:T(8,128)(2,1)}, bf16[512,256]{1,0:T(8,128)(2,1)}, f32[4,512,128]{2,1,0:T(8,128)}, bf16[512,128]{1,0:T(8,128)(2,1)S(1)}, bf16[5...) custom-call(s32[12]{0:T(128)S(1)} %reshape.39.refs_0_, ...), custom_call_target="tpu_custom_call" | custom-call | tf_op jit(solution)/shard_map/attention/pallas_call | solution.py:179
  83.7 0.8 copy-done.5
  84.5 6.3 %all-to-all-start.3 = ((bf16[8,128,128]{2,1,0:T(8,128)(2,1)}), bf16[8,128,128]{2,1,0:T(8,128)(2,1)S(1)}, u32[]{:S(2)}, u32[]{:S(2)}) async-start(bf16[8,128,128]{2,1,0:T(8,128)(2,1)} %bitcast.6), calls=%async_computation.3 | async-start | bytes 524288 | tf_op jit(solution)/shard_map/all_to_all | solution.py:122
  90.8 0.0 copy-done.6
  90.8 4.3 %collective-permute-start.5 = (bf16[4,512,128]{2,1,0:T(8,128)(2,1)S(1)}, bf16[4,512,128]{2,1,0:T(8,128)(2,1)S(1)}, u32[]{:S(2)}, u32[]{:S(2)}) collective-permute-start(bf16[4,512,128]{2,1,0:T(8,128)(2,1)S(1)} %copy-done.6), channel_id=1, source_target_pairs={{0,256},{64,320},{128,384},{192,448},{256,0},{320,64},{384,128},{4... | collective-permute-start | bytes 1572872 | tf_op jit(solution)/shard_map/ppermute | solution.py:153
  95.1 6.3 %all-to-all-done.3 = bf16[8,128,128]{2,1,0:T(8,128)(2,1)S(1)} async-done(((bf16[8,128,128]{2,1,0:T(8,128)(2,1)}), bf16[8,128,128]{2,1,0:T(8,128)(2,1)S(1)}, u32[]{:S(2)}, u32[]{:S(2)}) %all-to-all-start.3) | async-done | bytes 262176 | tf_op jit(solution)/shard_map/all_to_all | solution.py:122
  101.4 0.0 copy-start.2
  101.4 0.7 broadcast_in_dim.44
  102.1 6.5 %all-to-all-start.4 = ((bf16[8,128,128]{2,1,0:T(8,128)(2,1)}), bf16[8,128,128]{2,1,0:T(8,128)(2,1)S(1)}, u32[]{:S(2)}, u32[]{:S(2)}) async-start(bf16[8,128,128]{2,1,0:T(8,128)(2,1)} %broadcast_in_dim.44), calls=%async_computation.4 | async-start | bytes 524288 | tf_op jit(solution)/shard_map/all_to_all | solution.py:122
  108.7 4.8 %collective-permute-start.8 = (bf16[4,512,128]{2,1,0:T(8,128)(2,1)}, bf16[4,512,128]{2,1,0:T(8,128)(2,1)S(1)}, u32[]{:S(2)}, u32[]{:S(2)}) collective-permute-start(bf16[4,512,128]{2,1,0:T(8,128)(2,1)} %get-tuple-element.42), channel_id=1, source_target_pairs={{0,128},{64,192},{128,0},{192,64},{256,384},{320,448},{384,256},{4... | collective-permute-start | bytes 1572872 | tf_op jit(solution)/shard_map/ppermute | solution.py:153
  113.5 10.7 %collective-permute-done.5.refs_5_ = bf16[4,512,128]{2,1,0:T(8,128)(2,1)S(1)} collective-permute-done((bf16[4,512,128]{2,1,0:T(8,128)(2,1)S(1)}, bf16[4,512,128]{2,1,0:T(8,128)(2,1)S(1)}, u32[]{:S(2)}, u32[]{:S(2)}) %collective-permute-start.5) | collective-permute-done | bytes 524320 | tf_op jit(solution)/shard_map/ppermute | solution.py:153
  124.2 1.9 %collective-permute-start.9 = (bf16[4,512,128]{2,1,0:T(8,128)(2,1)}, bf16[4,512,128]{2,1,0:T(8,128)(2,1)S(1)}, u32[]{:S(2)}, u32[]{:S(2)}) collective-permute-start(bf16[4,512,128]{2,1,0:T(8,128)(2,1)} %get-tuple-element.43), channel_id=1, source_target_pairs={{0,64},{64,0},{128,192},{192,128},{256,320},{320,256},{384,448},{4... | collective-permute-start | bytes 1572872 | tf_op jit(solution)/shard_map/ppermute | solution.py:153
  126.2 0.9 all-to-all-done.4
  127.1 0.7 broadcast_in_dim.45
  127.8 7.3 %all-to-all-start.5 = ((bf16[8,128,128]{2,1,0:T(8,128)(2,1)}), bf16[8,128,128]{2,1,0:T(8,128)(2,1)S(1)}, u32[]{:S(2)}, u32[]{:S(2)}) async-start(bf16[8,128,128]{2,1,0:T(8,128)(2,1)} %broadcast_in_dim.45), calls=%async_computation.5 | async-start | bytes 524288 | tf_op jit(solution)/shard_map/all_to_all | solution.py:122
  135.1 3.9 %collective-permute-start.6 = (bf16[512,128]{1,0:T(8,128)(2,1)S(1)}, bf16[512,128]{1,0:T(8,128)(2,1)S(1)}, u32[]{:S(2)}, u32[]{:S(2)}) collective-permute-start(bf16[512,128]{1,0:T(8,128)(2,1)S(1)} %get-tuple-element.36), channel_id=1, source_target_pairs={{0,8},{8,16},{16,24},{24,32},{32,40},{40,48},{48,56},{56,64},{64,7... | collective-permute-start | bytes 393224 | tf_op jit(solution)/shard_map/ppermute | solution.py:207
  139.0 1.3 collective-permute-start.7
  140.3 1.6 %collective-permute-done.6.refs_2_ = bf16[512,128]{1,0:T(8,128)(2,1)S(1)} collective-permute-done((bf16[512,128]{1,0:T(8,128)(2,1)S(1)}, bf16[512,128]{1,0:T(8,128)(2,1)S(1)}, u32[]{:S(2)}, u32[]{:S(2)}) %collective-permute-start.6) | collective-permute-done | bytes 131104 | tf_op jit(solution)/shard_map/ppermute | solution.py:207
  141.9 4.0 %collective-permute-done.7.refs_3_ = bf16[512,128]{1,0:T(8,128)(2,1)S(1)} collective-permute-done((bf16[512,128]{1,0:T(8,128)(2,1)S(1)}, bf16[512,128]{1,0:T(8,128)(2,1)S(1)}, u32[]{:S(2)}, u32[]{:S(2)}) %collective-permute-start.7) | collective-permute-done | bytes 131104 | tf_op jit(solution)/shard_map/ppermute | solution.py:206
  145.9 0.0 collective-permute-done.8.refs_6_
  145.9 2.3 %collective-permute-done.9.refs_7_ = bf16[4,512,128]{2,1,0:T(8,128)(2,1)S(1)} collective-permute-done((bf16[4,512,128]{2,1,0:T(8,128)(2,1)}, bf16[4,512,128]{2,1,0:T(8,128)(2,1)S(1)}, u32[]{:S(2)}, u32[]{:S(2)}) %collective-permute-start.9) | collective-permute-done | bytes 524320 | tf_op jit(solution)/shard_map/ppermute | solution.py:153
  148.2 0.0 all-to-all-done.5
  148.2 0.0 copy-done.2
  148.2 1.2 finish.1
  (13 shorter events, 0.1 us)
Async XLA Ops:
  0.6 0.9 slice-start
  0.6 1.0 slice-start.1
  2.3 10.5 %copy-start = (bf16[512,256]{1,0:T(8,128)(2,1)S(1)}, bf16[512,256]{1,0:T(8,128)(2,1)}, u32[]{:S(2)}) copy-start(bf16[512,256]{1,0:T(8,128)(2,1)} %refs_4_.1) | copy-start | bytes 786436
  2.3 22.3 %all-to-all-start = ((bf16[8,32,512]{2,1,0:T(8,128)(2,1)}), bf16[8,32,512]{2,1,0:T(8,128)(2,1)S(1)}, u32[]{:S(2)}, u32[]{:S(2)}) async-start(bf16[8,32,512]{2,1,0:T(8,128)(2,1)} %bitcast.1), calls=%async_computation | async-start | bytes 524288 | tf_op jit(solution)/shard_map/all_to_all | solution.py:122
  12.8 1.0 copy-start.1
  14.6 30.8 %collective-permute-start.2 = (bf16[512,512]{1,0:T(8,128)(2,1)}, bf16[512,512]{1,0:T(8,128)(2,1)S(1)}, u32[]{:S(2)}, u32[]{:S(2)}) collective-permute-start(bf16[512,512]{1,0:T(8,128)(2,1)} %constant_dynamic-update-slice_fusion), channel_id=1, source_target_pairs={{0,256},{64,320},{128,384},{192,448},{256,0},{320,64},{384,128},{4... | collective-permute-start | bytes 1572872 | tf_op jit(solution)/shard_map/ppermute | solution.py:153
  25.4 27.2 %all-to-all-start.1 = ((bf16[8,32,512]{2,1,0:T(8,128)(2,1)}), bf16[8,32,512]{2,1,0:T(8,128)(2,1)S(1)}, u32[]{:S(2)}, u32[]{:S(2)}) async-start(bf16[8,32,512]{2,1,0:T(8,128)(2,1)} %broadcast_in_dim.41), calls=%async_computation.1 | async-start | bytes 524288 | tf_op jit(solution)/shard_map/all_to_all | solution.py:122
  33.5 27.2 %collective-permute-start.1 = (bf16[128,512]{1,0:T(8,128)(2,1)S(1)}, bf16[128,512]{1,0:T(8,128)(2,1)S(1)}, u32[]{:S(2)}, u32[]{:S(2)}) collective-permute-start(bf16[128,512]{1,0:T(8,128)(2,1)S(1)} %get-tuple-element.46), channel_id=1, source_target_pairs={{8,0},{16,8},{24,16},{32,24},{40,32},{48,40},{56,48},{64,56},{72,6... | collective-permute-start | bytes 393224 | tf_op jit(solution)/shard_map/ppermute | solution.py:160
  34.8 25.9 %collective-permute-start = (bf16[128,512]{1,0:T(8,128)(2,1)S(1)}, bf16[128,512]{1,0:T(8,128)(2,1)S(1)}, u32[]{:S(2)}, u32[]{:S(2)}) collective-permute-start(bf16[128,512]{1,0:T(8,128)(2,1)S(1)} %get-tuple-element.47), channel_id=1, source_target_pairs={{0,8},{8,16},{16,24},{24,32},{32,40},{40,48},{48,56},{56,64},{64,7... | collective-permute-start | bytes 393224 | tf_op jit(solution)/shard_map/ppermute | solution.py:159
  39.3 0.7 copy-start.7
  40.1 36.6 %collective-permute-start.4 = (bf16[512,512]{1,0:T(8,128)(2,1)}, bf16[512,512]{1,0:T(8,128)(2,1)S(1)}, u32[]{:S(2)}, u32[]{:S(2)}) collective-permute-start(bf16[512,512]{1,0:T(8,128)(2,1)} %constant_dynamic-update-slice_fusion), channel_id=1, source_target_pairs={{0,64},{64,0},{128,192},{192,128},{256,320},{320,256},{384,448},{4... | collective-permute-start | bytes 1572872 | tf_op jit(solution)/shard_map/ppermute | solution.py:153
  45.4 31.3 %collective-permute-start.3 = (bf16[512,512]{1,0:T(8,128)(2,1)}, bf16[512,512]{1,0:T(8,128)(2,1)S(1)}, u32[]{:S(2)}, u32[]{:S(2)}) collective-permute-start(bf16[512,512]{1,0:T(8,128)(2,1)} %constant_dynamic-update-slice_fusion), channel_id=1, source_target_pairs={{0,128},{64,192},{128,0},{192,64},{256,384},{320,448},{384,256},{4... | collective-permute-start | bytes 1572872 | tf_op jit(solution)/shard_map/ppermute | solution.py:153
  53.4 23.4 %copy-start.3 = (bf16[512,256]{1,0:T(8,128)(2,1)S(1)}, bf16[512,256]{1,0:T(8,128)(2,1)}, u32[]{:S(2)}) copy-start(bf16[512,256]{1,0:T(8,128)(2,1)} %refs_2_.1) | copy-start | bytes 786436
  53.4 23.4 %copy-start.4 = (bf16[512,256]{1,0:T(8,128)(2,1)S(1)}, bf16[512,256]{1,0:T(8,128)(2,1)}, u32[]{:S(2)}) copy-start(bf16[512,256]{1,0:T(8,128)(2,1)} %refs_3_.1) | copy-start | bytes 786436
  53.4 23.4 %all-to-all-start.2 = ((bf16[8,32,512]{2,1,0:T(8,128)(2,1)}), bf16[8,32,512]{2,1,0:T(8,128)(2,1)S(1)}, u32[]{:S(2)}, u32[]{:S(2)}) async-start(bf16[8,32,512]{2,1,0:T(8,128)(2,1)} %broadcast_in_dim.43), calls=%async_computation.2 | async-start | bytes 524288 | tf_op jit(solution)/shard_map/all_to_all | solution.py:122
  83.7 0.8 copy-start.5
  84.5 6.3 %copy-start.6 = (bf16[4,512,128]{2,1,0:T(8,128)(2,1)S(1)}, bf16[4,512,128]{2,1,0:T(8,128)(2,1)}, u32[]{:S(2)}) copy-start(bf16[4,512,128]{2,1,0:T(8,128)(2,1)} %copy-done.5) | copy-start | bytes 1572868
  84.5 16.8 %all-to-all-start.3 = ((bf16[8,128,128]{2,1,0:T(8,128)(2,1)}), bf16[8,128,128]{2,1,0:T(8,128)(2,1)S(1)}, u32[]{:S(2)}, u32[]{:S(2)}) async-start(bf16[8,128,128]{2,1,0:T(8,128)(2,1)} %bitcast.6), calls=%async_computation.3 | async-start | bytes 524288 | tf_op jit(solution)/shard_map/all_to_all | solution.py:122
  90.8 33.5 %collective-permute-start.5 = (bf16[4,512,128]{2,1,0:T(8,128)(2,1)S(1)}, bf16[4,512,128]{2,1,0:T(8,128)(2,1)S(1)}, u32[]{:S(2)}, u32[]{:S(2)}) collective-permute-start(bf16[4,512,128]{2,1,0:T(8,128)(2,1)S(1)} %copy-done.6), channel_id=1, source_target_pairs={{0,256},{64,320},{128,384},{192,448},{256,0},{320,64},{384,128},{4... | collective-permute-start | bytes 1572872 | tf_op jit(solution)/shard_map/ppermute | solution.py:153
  101.4 46.8 %copy-start.2 = (f32[4,512,128]{2,1,0:T(8,128)S(1)}, f32[4,512,128]{2,1,0:T(8,128)}, u32[]{:S(2)}) copy-start(f32[4,512,128]{2,1,0:T(8,128)} %get-tuple-element.31.refs_1_) | copy-start | bytes 3145732
  102.1 24.9 %all-to-all-start.4 = ((bf16[8,128,128]{2,1,0:T(8,128)(2,1)}), bf16[8,128,128]{2,1,0:T(8,128)(2,1)S(1)}, u32[]{:S(2)}, u32[]{:S(2)}) async-start(bf16[8,128,128]{2,1,0:T(8,128)(2,1)} %broadcast_in_dim.44), calls=%async_computation.4 | async-start | bytes 524288 | tf_op jit(solution)/shard_map/all_to_all | solution.py:122
  108.7 37.2 %collective-permute-start.8 = (bf16[4,512,128]{2,1,0:T(8,128)(2,1)}, bf16[4,512,128]{2,1,0:T(8,128)(2,1)S(1)}, u32[]{:S(2)}, u32[]{:S(2)}) collective-permute-start(bf16[4,512,128]{2,1,0:T(8,128)(2,1)} %get-tuple-element.42), channel_id=1, source_target_pairs={{0,128},{64,192},{128,0},{192,64},{256,384},{320,448},{384,256},{4... | collective-permute-start | bytes 1572872 | tf_op jit(solution)/shard_map/ppermute | solution.py:153
  124.2 24.0 %collective-permute-start.9 = (bf16[4,512,128]{2,1,0:T(8,128)(2,1)}, bf16[4,512,128]{2,1,0:T(8,128)(2,1)S(1)}, u32[]{:S(2)}, u32[]{:S(2)}) collective-permute-start(bf16[4,512,128]{2,1,0:T(8,128)(2,1)} %get-tuple-element.43), channel_id=1, source_target_pairs={{0,64},{64,0},{128,192},{192,128},{256,320},{320,256},{384,448},{4... | collective-permute-start | bytes 1572872 | tf_op jit(solution)/shard_map/ppermute | solution.py:153
  127.8 20.4 %all-to-all-start.5 = ((bf16[8,128,128]{2,1,0:T(8,128)(2,1)}), bf16[8,128,128]{2,1,0:T(8,128)(2,1)S(1)}, u32[]{:S(2)}, u32[]{:S(2)}) async-start(bf16[8,128,128]{2,1,0:T(8,128)(2,1)} %broadcast_in_dim.45), calls=%async_computation.5 | async-start | bytes 524288 | tf_op jit(solution)/shard_map/all_to_all | solution.py:122
  135.1 6.8 %collective-permute-start.6 = (bf16[512,128]{1,0:T(8,128)(2,1)S(1)}, bf16[512,128]{1,0:T(8,128)(2,1)S(1)}, u32[]{:S(2)}, u32[]{:S(2)}) collective-permute-start(bf16[512,128]{1,0:T(8,128)(2,1)S(1)} %get-tuple-element.36), channel_id=1, source_target_pairs={{0,8},{8,16},{16,24},{24,32},{32,40},{40,48},{48,56},{56,64},{64,7... | collective-permute-start | bytes 393224 | tf_op jit(solution)/shard_map/ppermute | solution.py:207
  139.0 6.9 %collective-permute-start.7 = (bf16[512,128]{1,0:T(8,128)(2,1)S(1)}, bf16[512,128]{1,0:T(8,128)(2,1)S(1)}, u32[]{:S(2)}, u32[]{:S(2)}) collective-permute-start(bf16[512,128]{1,0:T(8,128)(2,1)S(1)} %get-tuple-element.37), channel_id=1, source_target_pairs={{8,0},{16,8},{24,16},{32,24},{40,32},{48,40},{56,48},{64,56},{72,6... | collective-permute-start | bytes 393224 | tf_op jit(solution)/shard_map/ppermute | solution.py:206

commit v6 on v5

--- a/solution.py
+++ b/solution.py
@@ -37,8 +37,8 @@
     vwin[BLK:BLK + tokens] = v_ref[...]
     kwin[BLK + tokens:] = right_ref[:, :width]
     vwin[BLK + tokens:] = right_ref[:, width:]
-    ksel[:GLOBAL * BLK] = glob_ref[:, :width]
-    vsel[:GLOBAL * BLK] = glob_ref[:, width:]
+    ksel[:GLOBAL * BLK] = glob_ref[:GLOBAL * BLK]
+    vsel[:GLOBAL * BLK] = glob_ref[GLOBAL * BLK:]
     acc_win[...] = jnp.zeros_like(acc_win)
     acc_glob[...] = jnp.zeros_like(acc_glob)
     acc_part[...] = jnp.zeros_like(acc_part)
@@ -153,8 +153,8 @@
         return lax.ppermute(x, "y", [(i, i ^ masks[r]) for i in range(ny)])
 
     grows = GLOBAL * BLK
-    glob = jnp.concatenate([keys[:grows], values[:grows]], axis=1)
-    piece = exchange(glob.reshape(nz, grows // nz, 2 * width), "z")[0]
+    glob = jnp.concatenate([keys[:grows], values[:grows]], axis=0)
+    piece = exchange(glob.reshape(nz, 2 * grows // nz, width), "z")[0]
     kv = jnp.concatenate([keys, values], axis=1)
     left = lax.ppermute(kv[tokens - BLK:], SEQ_AXES, up)
     right = lax.ppermute(kv[:BLK], SEQ_AXES, down)
@@ -164,7 +164,7 @@
     kv, far = tie(kv, far)
     fetched = [far, partner(kv, 1), one]
     piece = exchange(spread(piece, ny), "y")[0]
-    glob = exchange(spread(piece, nz), "z").reshape(grows, 2 * width)
+    glob = exchange(spread(piece, nz), "z").reshape(2 * grows, width)
 
     mine = lax.dynamic_slice_in_dim(rand_blocks, myself * nblk, nblk, 0)
     picks = (mine % nblk).reshape(-1)

time: 152 us -> 152 us (level)
  no operation moved by 1% of the time
where the time goes in v6:
time: 152 us; the launch traced here: 149 us
  starting transfers between devices  85.5 us (56%)
  waiting for transfers between devices  45.3 us (30%)
  local copies, waits for them, and re-layouts  8.52 us (6%)
  Pallas kernels  8.09 us (5%)
    all_to_all x6, starting transfers between devices, exchange(): return lax.all_to_all(x, axis, 0, 0, tiled=True)  44.6 us
    ppermute x6, waiting for transfers between devices, partner(): return lax.ppermute(x, 'y', [(i, i ^ masks[r]) for i in range(ny)])  30.3 us
    ppermute x6, starting transfers between devices, partner(): return lax.ppermute(x, 'y', [(i, i ^ masks[r]) for i in range(ny)])  29.9 us
    all_to_all x6, waiting for transfers between devices, exchange(): return lax.all_to_all(x, axis, 0, 0, tiled=True)  9.45 us
    pallas_call x1, Pallas kernels, shards(): pl.pallas_call(lambda *refs: attention_kernel(nblk, heads, *refs), out_sh...  6.9 us
    ppermute x1, starting transfers between devices, shards(): left = lax.ppermute(kv[tokens - BLK:], SEQ_AXES, up)  4.55 us
    ppermute x1, waiting for transfers between devices, shards(): high = lax.ppermute(gleft, SEQ_AXES, down)  3.97 us
    ppermute x1, starting transfers between devices, shards(): low = lax.ppermute(gright, SEQ_AXES, up)  3.92 us
  transfers between devices with their start and end apart: 16, of which 9 were waited for; matrix products, arithmetic and copies ran while one was open for 4% of the time, Pallas kernels for 0%

profile of v6, /device:TPU:6, one launch (start us, length us, event | category | flops | bytes accessed | tf_op | source)
XLA Modules:
  0.0 149.3 jit_solution(16500790364641922984)
XLA Ops:
  0.6 0.0 slice-start
  0.6 0.0 slice-start.1
  0.7 0.9 slice-done
  1.5 0.1 slice-done.1
  1.6 0.7 pad_maximum_fusion
  2.3 10.4 %all-to-all-start = ((bf16[8,64,256]{2,1,0:T(8,128)(2,1)}), bf16[8,64,256]{2,1,0:T(8,128)(2,1)S(1)}, u32[]{:S(2)}, u32[]{:S(2)}) async-start(bf16[8,64,256]{2,1,0:T(8,128)(2,1)} %bitcast.1), calls=%async_computation | async-start | bytes 524288 | tf_op jit(solution)/shard_map/all_to_all | solution.py:122
  12.8 0.0 copy-done
  12.8 0.0 copy-start.1
  12.8 0.8 constant_dynamic-update-slice_fusion.1
  13.5 0.3 copy-done.1
  13.8 0.8 constant_dynamic-update-slice_fusion
  14.6 7.7 %collective-permute-start.2 = (bf16[512,512]{1,0:T(8,128)(2,1)}, bf16[512,512]{1,0:T(8,128)(2,1)S(1)}, u32[]{:S(2)}, u32[]{:S(2)}) collective-permute-start(bf16[512,512]{1,0:T(8,128)(2,1)} %constant_dynamic-update-slice_fusion), channel_id=1, source_target_pairs={{0,256},{64,320},{128,384},{192,448},{256,0},{320,64},{384,128},{4... | collective-permute-start | bytes 1572872 | tf_op jit(solution)/shard_map/ppermute | solution.py:153
  22.3 2.3 %all-to-all-done = bf16[8,64,256]{2,1,0:T(8,128)(2,1)S(1)} async-done(((bf16[8,64,256]{2,1,0:T(8,128)(2,1)}), bf16[8,64,256]{2,1,0:T(8,128)(2,1)S(1)}, u32[]{:S(2)}, u32[]{:S(2)}) %all-to-all-start) | async-done | bytes 262176 | tf_op jit(solution)/shard_map/all_to_all | solution.py:122
  24.7 0.7 broadcast_in_dim.41
  25.4 7.1 %all-to-all-start.1 = ((bf16[8,64,256]{2,1,0:T(8,128)(2,1)}), bf16[8,64,256]{2,1,0:T(8,128)(2,1)S(1)}, u32[]{:S(2)}, u32[]{:S(2)}) async-start(bf16[8,64,256]{2,1,0:T(8,128)(2,1)} %broadcast_in_dim.41), calls=%async_computation.1 | async-start | bytes 524288 | tf_op jit(solution)/shard_map/all_to_all | solution.py:122
  32.5 1.0 fusion.2
  33.5 1.3 collective-permute-start.1
  34.8 4.6 %collective-permute-start = (bf16[128,512]{1,0:T(8,128)(2,1)S(1)}, bf16[128,512]{1,0:T(8,128)(2,1)S(1)}, u32[]{:S(2)}, u32[]{:S(2)}) collective-permute-start(bf16[128,512]{1,0:T(8,128)(2,1)S(1)} %get-tuple-element.47), channel_id=1, source_target_pairs={{0,8},{8,16},{16,24},{24,32},{32,40},{40,48},{48,56},{56,64},{64,7... | collective-permute-start | bytes 393224 | tf_op jit(solution)/shard_map/ppermute | solution.py:159
  39.3 0.0 copy-start.7
  39.4 0.7 copy-done.7
  40.0 0.1 add_select_fusion.1
  40.1 3.9 %collective-permute-start.4 = (bf16[512,512]{1,0:T(8,128)(2,1)}, bf16[512,512]{1,0:T(8,128)(2,1)S(1)}, u32[]{:S(2)}, u32[]{:S(2)}) collective-permute-start(bf16[512,512]{1,0:T(8,128)(2,1)} %constant_dynamic-update-slice_fusion), channel_id=1, source_target_pairs={{0,64},{64,0},{128,192},{192,128},{256,320},{320,256},{384,448},{4... | collective-permute-start | bytes 1572872 | tf_op jit(solution)/shard_map/ppermute | solution.py:153
  44.0 1.4 collective-permute-done.2.refs_9_
  45.4 7.2 %collective-permute-start.3 = (bf16[512,512]{1,0:T(8,128)(2,1)}, bf16[512,512]{1,0:T(8,128)(2,1)S(1)}, u32[]{:S(2)}, u32[]{:S(2)}) collective-permute-start(bf16[512,512]{1,0:T(8,128)(2,1)} %constant_dynamic-update-slice_fusion), channel_id=1, source_target_pairs={{0,128},{64,192},{128,0},{192,64},{256,384},{320,448},{384,256},{4... | collective-permute-start | bytes 1572872 | tf_op jit(solution)/shard_map/ppermute | solution.py:153
  52.6 0.0 all-to-all-done.1
  52.6 0.7 broadcast_in_dim.43
  53.4 6.9 %all-to-all-start.2 = ((bf16[8,64,256]{2,1,0:T(8,128)(2,1)}), bf16[8,64,256]{2,1,0:T(8,128)(2,1)S(1)}, u32[]{:S(2)}, u32[]{:S(2)}) async-start(bf16[8,64,256]{2,1,0:T(8,128)(2,1)} %broadcast_in_dim.43), calls=%async_computation.2 | async-start | bytes 524288 | tf_op jit(solution)/shard_map/all_to_all | solution.py:122
  60.2 0.1 copy.11
  60.3 0.1 reshape.39.refs_0_
  60.4 0.1 fusion.1
  60.5 0.1 add_select_fusion
  60.6 0.1 copy.12
  60.7 0.0 collective-permute-done.1.refs_7_
  60.7 0.0 collective-permute-done.refs_6_
  60.7 16.0 %collective-permute-done.4.refs_11_ = bf16[512,512]{1,0:T(8,128)(2,1)S(1)} collective-permute-done((bf16[512,512]{1,0:T(8,128)(2,1)}, bf16[512,512]{1,0:T(8,128)(2,1)S(1)}, u32[]{:S(2)}, u32[]{:S(2)}) %collective-permute-start.4) | collective-permute-done | bytes 524320 | tf_op jit(solution)/shard_map/ppermute | solution.py:153
  76.7 0.0 collective-permute-done.3.refs_10_
  76.7 0.0 all-to-all-done.2
  76.7 0.1 broadcast_in_dim.40
  76.8 0.0 copy-done.3
  76.8 0.0 copy-done.4
  76.8 6.9 %attention.1 = (bf16[512,256]{1,0:T(8,128)(2,1)}, bf16[512,256]{1,0:T(8,128)(2,1)}, f32[4,512,128]{2,1,0:T(8,128)}, bf16[512,128]{1,0:T(8,128)(2,1)S(1)}, bf16[5...) custom-call(s32[12]{0:T(128)S(1)} %reshape.39.refs_0_, ...), custom_call_target="tpu_custom_call" | custom-call | tf_op jit(solution)/shard_map/attention/pallas_call | solution.py:179
  83.7 0.8 copy-done.5
  84.5 6.2 %all-to-all-start.3 = ((bf16[8,128,128]{2,1,0:T(8,128)(2,1)}), bf16[8,128,128]{2,1,0:T(8,128)(2,1)S(1)}, u32[]{:S(2)}, u32[]{:S(2)}) async-start(bf16[8,128,128]{2,1,0:T(8,128)(2,1)} %bitcast.6), calls=%async_computation.3 | async-start | bytes 524288 | tf_op jit(solution)/shard_map/all_to_all | solution.py:122
  90.8 0.0 copy-done.6
  90.8 4.3 %collective-permute-start.5 = (bf16[4,512,128]{2,1,0:T(8,128)(2,1)S(1)}, bf16[4,512,128]{2,1,0:T(8,128)(2,1)S(1)}, u32[]{:S(2)}, u32[]{:S(2)}) collective-permute-start(bf16[4,512,128]{2,1,0:T(8,128)(2,1)S(1)} %copy-done.6), channel_id=1, source_target_pairs={{0,256},{64,320},{128,384},{192,448},{256,0},{320,64},{384,128},{4... | collective-permute-start | bytes 1572872 | tf_op jit(solution)/shard_map/ppermute | solution.py:153
  95.1 6.2 %all-to-all-done.3 = bf16[8,128,128]{2,1,0:T(8,128)(2,1)S(1)} async-done(((bf16[8,128,128]{2,1,0:T(8,128)(2,1)}), bf16[8,128,128]{2,1,0:T(8,128)(2,1)S(1)}, u32[]{:S(2)}, u32[]{:S(2)}) %all-to-all-start.3) | async-done | bytes 262176 | tf_op jit(solution)/shard_map/all_to_all | solution.py:122
  101.3 0.0 copy-start.2
  101.4 0.7 broadcast_in_dim.44
  102.1 6.6 %all-to-all-start.4 = ((bf16[8,128,128]{2,1,0:T(8,128)(2,1)}), bf16[8,128,128]{2,1,0:T(8,128)(2,1)S(1)}, u32[]{:S(2)}, u32[]{:S(2)}) async-start(bf16[8,128,128]{2,1,0:T(8,128)(2,1)} %broadcast_in_dim.44), calls=%async_computation.4 | async-start | bytes 524288 | tf_op jit(solution)/shard_map/all_to_all | solution.py:122
  108.7 4.8 %collective-permute-start.8 = (bf16[4,512,128]{2,1,0:T(8,128)(2,1)}, bf16[4,512,128]{2,1,0:T(8,128)(2,1)S(1)}, u32[]{:S(2)}, u32[]{:S(2)}) collective-permute-start(bf16[4,512,128]{2,1,0:T(8,128)(2,1)} %get-tuple-element.42), channel_id=1, source_target_pairs={{0,128},{64,192},{128,0},{192,64},{256,384},{320,448},{384,256},{4... | collective-permute-start | bytes 1572872 | tf_op jit(solution)/shard_map/ppermute | solution.py:153
  113.5 10.7 %collective-permute-done.5.refs_5_ = bf16[4,512,128]{2,1,0:T(8,128)(2,1)S(1)} collective-permute-done((bf16[4,512,128]{2,1,0:T(8,128)(2,1)S(1)}, bf16[4,512,128]{2,1,0:T(8,128)(2,1)S(1)}, u32[]{:S(2)}, u32[]{:S(2)}) %collective-permute-start.5) | collective-permute-done | bytes 524320 | tf_op jit(solution)/shard_map/ppermute | solution.py:153
  124.2 1.9 %collective-permute-start.9 = (bf16[4,512,128]{2,1,0:T(8,128)(2,1)}, bf16[4,512,128]{2,1,0:T(8,128)(2,1)S(1)}, u32[]{:S(2)}, u32[]{:S(2)}) collective-permute-start(bf16[4,512,128]{2,1,0:T(8,128)(2,1)} %get-tuple-element.43), channel_id=1, source_target_pairs={{0,64},{64,0},{128,192},{192,128},{256,320},{320,256},{384,448},{4... | collective-permute-start | bytes 1572872 | tf_op jit(solution)/shard_map/ppermute | solution.py:153
  126.1 0.9 all-to-all-done.4
  127.0 0.7 broadcast_in_dim.45
  127.8 7.3 %all-to-all-start.5 = ((bf16[8,128,128]{2,1,0:T(8,128)(2,1)}), bf16[8,128,128]{2,1,0:T(8,128)(2,1)S(1)}, u32[]{:S(2)}, u32[]{:S(2)}) async-start(bf16[8,128,128]{2,1,0:T(8,128)(2,1)} %broadcast_in_dim.45), calls=%async_computation.5 | async-start | bytes 524288 | tf_op jit(solution)/shard_map/all_to_all | solution.py:122
  135.1 3.9 %collective-permute-start.6 = (bf16[512,128]{1,0:T(8,128)(2,1)S(1)}, bf16[512,128]{1,0:T(8,128)(2,1)S(1)}, u32[]{:S(2)}, u32[]{:S(2)}) collective-permute-start(bf16[512,128]{1,0:T(8,128)(2,1)S(1)} %get-tuple-element.36), channel_id=1, source_target_pairs={{0,8},{8,16},{16,24},{24,32},{32,40},{40,48},{48,56},{56,64},{64,7... | collective-permute-start | bytes 393224 | tf_op jit(solution)/shard_map/ppermute | solution.py:207
  139.0 1.3 collective-permute-start.7
  140.4 1.6 %collective-permute-done.6.refs_2_ = bf16[512,128]{1,0:T(8,128)(2,1)S(1)} collective-permute-done((bf16[512,128]{1,0:T(8,128)(2,1)S(1)}, bf16[512,128]{1,0:T(8,128)(2,1)S(1)}, u32[]{:S(2)}, u32[]{:S(2)}) %collective-permute-start.6) | collective-permute-done | bytes 131104 | tf_op jit(solution)/shard_map/ppermute | solution.py:207
  141.9 4.0 %collective-permute-done.7.refs_3_ = bf16[512,128]{1,0:T(8,128)(2,1)S(1)} collective-permute-done((bf16[512,128]{1,0:T(8,128)(2,1)S(1)}, bf16[512,128]{1,0:T(8,128)(2,1)S(1)}, u32[]{:S(2)}, u32[]{:S(2)}) %collective-permute-start.7) | collective-permute-done | bytes 131104 | tf_op jit(solution)/shard_map/ppermute | solution.py:206
  145.9 0.0 collective-permute-done.8.refs_6_
  145.9 2.2 %collective-permute-done.9.refs_7_ = bf16[4,512,128]{2,1,0:T(8,128)(2,1)S(1)} collective-permute-done((bf16[4,512,128]{2,1,0:T(8,128)(2,1)}, bf16[4,512,128]{2,1,0:T(8,128)(2,1)S(1)}, u32[]{:S(2)}, u32[]{:S(2)}) %collective-permute-start.9) | collective-permute-done | bytes 524320 | tf_op jit(solution)/shard_map/ppermute | solution.py:153
  148.1 0.0 all-to-all-done.5
  148.1 0.0 copy-done.2
  148.1 1.2 finish.1
  (13 shorter events, 0.1 us)
Async XLA Ops:
  0.6 0.9 slice-start
  0.6 1.0 slice-start.1
  2.3 10.5 %copy-start = (bf16[512,256]{1,0:T(8,128)(2,1)S(1)}, bf16[512,256]{1,0:T(8,128)(2,1)}, u32[]{:S(2)}) copy-start(bf16[512,256]{1,0:T(8,128)(2,1)} %refs_4_.1) | copy-start | bytes 786436
  2.3 22.3 %all-to-all-start = ((bf16[8,64,256]{2,1,0:T(8,128)(2,1)}), bf16[8,64,256]{2,1,0:T(8,128)(2,1)S(1)}, u32[]{:S(2)}, u32[]{:S(2)}) async-start(bf16[8,64,256]{2,1,0:T(8,128)(2,1)} %bitcast.1), calls=%async_computation | async-start | bytes 524288 | tf_op jit(solution)/shard_map/all_to_all | solution.py:122
  12.8 1.0 copy-start.1
  14.6 30.8 %collective-permute-start.2 = (bf16[512,512]{1,0:T(8,128)(2,1)}, bf16[512,512]{1,0:T(8,128)(2,1)S(1)}, u32[]{:S(2)}, u32[]{:S(2)}) collective-permute-start(bf16[512,512]{1,0:T(8,128)(2,1)} %constant_dynamic-update-slice_fusion), channel_id=1, source_target_pairs={{0,256},{64,320},{128,384},{192,448},{256,0},{320,64},{384,128},{4... | collective-permute-start | bytes 1572872 | tf_op jit(solution)/shard_map/ppermute | solution.py:153
  25.4 27.2 %all-to-all-start.1 = ((bf16[8,64,256]{2,1,0:T(8,128)(2,1)}), bf16[8,64,256]{2,1,0:T(8,128)(2,1)S(1)}, u32[]{:S(2)}, u32[]{:S(2)}) async-start(bf16[8,64,256]{2,1,0:T(8,128)(2,1)} %broadcast_in_dim.41), calls=%async_computation.1 | async-start | bytes 524288 | tf_op jit(solution)/shard_map/all_to_all | solution.py:122
  33.5 27.2 %collective-permute-start.1 = (bf16[128,512]{1,0:T(8,128)(2,1)S(1)}, bf16[128,512]{1,0:T(8,128)(2,1)S(1)}, u32[]{:S(2)}, u32[]{:S(2)}) collective-permute-start(bf16[128,512]{1,0:T(8,128)(2,1)S(1)} %get-tuple-element.46), channel_id=1, source_target_pairs={{8,0},{16,8},{24,16},{32,24},{40,32},{48,40},{56,48},{64,56},{72,6... | collective-permute-start | bytes 393224 | tf_op jit(solution)/shard_map/ppermute | solution.py:160
  34.8 25.9 %collective-permute-start = (bf16[128,512]{1,0:T(8,128)(2,1)S(1)}, bf16[128,512]{1,0:T(8,128)(2,1)S(1)}, u32[]{:S(2)}, u32[]{:S(2)}) collective-permute-start(bf16[128,512]{1,0:T(8,128)(2,1)S(1)} %get-tuple-element.47), channel_id=1, source_target_pairs={{0,8},{8,16},{16,24},{24,32},{32,40},{40,48},{48,56},{56,64},{64,7... | collective-permute-start | bytes 393224 | tf_op jit(solution)/shard_map/ppermute | solution.py:159
  39.3 0.7 copy-start.7
  40.1 36.6 %collective-permute-start.4 = (bf16[512,512]{1,0:T(8,128)(2,1)}, bf16[512,512]{1,0:T(8,128)(2,1)S(1)}, u32[]{:S(2)}, u32[]{:S(2)}) collective-permute-start(bf16[512,512]{1,0:T(8,128)(2,1)} %constant_dynamic-update-slice_fusion), channel_id=1, source_target_pairs={{0,64},{64,0},{128,192},{192,128},{256,320},{320,256},{384,448},{4... | collective-permute-start | bytes 1572872 | tf_op jit(solution)/shard_map/ppermute | solution.py:153
  45.4 31.3 %collective-permute-start.3 = (bf16[512,512]{1,0:T(8,128)(2,1)}, bf16[512,512]{1,0:T(8,128)(2,1)S(1)}, u32[]{:S(2)}, u32[]{:S(2)}) collective-permute-start(bf16[512,512]{1,0:T(8,128)(2,1)} %constant_dynamic-update-slice_fusion), channel_id=1, source_target_pairs={{0,128},{64,192},{128,0},{192,64},{256,384},{320,448},{384,256},{4... | collective-permute-start | bytes 1572872 | tf_op jit(solution)/shard_map/ppermute | solution.py:153
  53.4 23.4 %copy-start.3 = (bf16[512,256]{1,0:T(8,128)(2,1)S(1)}, bf16[512,256]{1,0:T(8,128)(2,1)}, u32[]{:S(2)}) copy-start(bf16[512,256]{1,0:T(8,128)(2,1)} %refs_2_.1) | copy-start | bytes 786436
  53.4 23.4 %copy-start.4 = (bf16[512,256]{1,0:T(8,128)(2,1)S(1)}, bf16[512,256]{1,0:T(8,128)(2,1)}, u32[]{:S(2)}) copy-start(bf16[512,256]{1,0:T(8,128)(2,1)} %refs_3_.1) | copy-start | bytes 786436
  53.4 23.4 %all-to-all-start.2 = ((bf16[8,64,256]{2,1,0:T(8,128)(2,1)}), bf16[8,64,256]{2,1,0:T(8,128)(2,1)S(1)}, u32[]{:S(2)}, u32[]{:S(2)}) async-start(bf16[8,64,256]{2,1,0:T(8,128)(2,1)} %broadcast_in_dim.43), calls=%async_computation.2 | async-start | bytes 524288 | tf_op jit(solution)/shard_map/all_to_all | solution.py:122
  83.7 0.8 copy-start.5
  84.5 6.2 %copy-start.6 = (bf16[4,512,128]{2,1,0:T(8,128)(2,1)S(1)}, bf16[4,512,128]{2,1,0:T(8,128)(2,1)}, u32[]{:S(2)}) copy-start(bf16[4,512,128]{2,1,0:T(8,128)(2,1)} %copy-done.5) | copy-start | bytes 1572868
  84.5 16.8 %all-to-all-start.3 = ((bf16[8,128,128]{2,1,0:T(8,128)(2,1)}), bf16[8,128,128]{2,1,0:T(8,128)(2,1)S(1)}, u32[]{:S(2)}, u32[]{:S(2)}) async-start(bf16[8,128,128]{2,1,0:T(8,128)(2,1)} %bitcast.6), calls=%async_computation.3 | async-start | bytes 524288 | tf_op jit(solution)/shard_map/all_to_all | solution.py:122
  90.8 33.4 %collective-permute-start.5 = (bf16[4,512,128]{2,1,0:T(8,128)(2,1)S(1)}, bf16[4,512,128]{2,1,0:T(8,128)(2,1)S(1)}, u32[]{:S(2)}, u32[]{:S(2)}) collective-permute-start(bf16[4,512,128]{2,1,0:T(8,128)(2,1)S(1)} %copy-done.6), channel_id=1, source_target_pairs={{0,256},{64,320},{128,384},{192,448},{256,0},{320,64},{384,128},{4... | collective-permute-start | bytes 1572872 | tf_op jit(solution)/shard_map/ppermute | solution.py:153
  101.3 46.8 %copy-start.2 = (f32[4,512,128]{2,1,0:T(8,128)S(1)}, f32[4,512,128]{2,1,0:T(8,128)}, u32[]{:S(2)}) copy-start(f32[4,512,128]{2,1,0:T(8,128)} %get-tuple-element.31.refs_1_) | copy-start | bytes 3145732
  102.1 24.9 %all-to-all-start.4 = ((bf16[8,128,128]{2,1,0:T(8,128)(2,1)}), bf16[8,128,128]{2,1,0:T(8,128)(2,1)S(1)}, u32[]{:S(2)}, u32[]{:S(2)}) async-start(bf16[8,128,128]{2,1,0:T(8,128)(2,1)} %broadcast_in_dim.44), calls=%async_computation.4 | async-start | bytes 524288 | tf_op jit(solution)/shard_map/all_to_all | solution.py:122
  108.7 37.2 %collective-permute-start.8 = (bf16[4,512,128]{2,1,0:T(8,128)(2,1)}, bf16[4,512,128]{2,1,0:T(8,128)(2,1)S(1)}, u32[]{:S(2)}, u32[]{:S(2)}) collective-permute-start(bf16[4,512,128]{2,1,0:T(8,128)(2,1)} %get-tuple-element.42), channel_id=1, source_target_pairs={{0,128},{64,192},{128,0},{192,64},{256,384},{320,448},{384,256},{4... | collective-permute-start | bytes 1572872 | tf_op jit(solution)/shard_map/ppermute | solution.py:153
  124.2 23.9 %collective-permute-start.9 = (bf16[4,512,128]{2,1,0:T(8,128)(2,1)}, bf16[4,512,128]{2,1,0:T(8,128)(2,1)S(1)}, u32[]{:S(2)}, u32[]{:S(2)}) collective-permute-start(bf16[4,512,128]{2,1,0:T(8,128)(2,1)} %get-tuple-element.43), channel_id=1, source_target_pairs={{0,64},{64,0},{128,192},{192,128},{256,320},{320,256},{384,448},{4... | collective-permute-start | bytes 1572872 | tf_op jit(solution)/shard_map/ppermute | solution.py:153
  127.8 20.3 %all-to-all-start.5 = ((bf16[8,128,128]{2,1,0:T(8,128)(2,1)}), bf16[8,128,128]{2,1,0:T(8,128)(2,1)S(1)}, u32[]{:S(2)}, u32[]{:S(2)}) async-start(bf16[8,128,128]{2,1,0:T(8,128)(2,1)} %broadcast_in_dim.45), calls=%async_computation.5 | async-start | bytes 524288 | tf_op jit(solution)/shard_map/all_to_all | solution.py:122
  135.1 6.8 %collective-permute-start.6 = (bf16[512,128]{1,0:T(8,128)(2,1)S(1)}, bf16[512,128]{1,0:T(8,128)(2,1)S(1)}, u32[]{:S(2)}, u32[]{:S(2)}) collective-permute-start(bf16[512,128]{1,0:T(8,128)(2,1)S(1)} %get-tuple-element.36), channel_id=1, source_target_pairs={{0,8},{8,16},{16,24},{24,32},{32,40},{40,48},{48,56},{56,64},{64,7... | collective-permute-start | bytes 393224 | tf_op jit(solution)/shard_map/ppermute | solution.py:207
  139.0 6.9 %collective-permute-start.7 = (bf16[512,128]{1,0:T(8,128)(2,1)S(1)}, bf16[512,128]{1,0:T(8,128)(2,1)S(1)}, u32[]{:S(2)}, u32[]{:S(2)}) collective-permute-start(bf16[512,128]{1,0:T(8,128)(2,1)S(1)} %get-tuple-element.37), channel_id=1, source_target_pairs={{8,0},{16,8},{24,16},{32,24},{40,32},{48,40},{56,48},{64,56},{72,6... | collective-permute-start | bytes 393224 | tf_op jit(solution)/shard_map/ppermute | solution.py:206
